TPU v7x, 32 devices: a whole 2x2x4 slice. The times are simulated.
32 devices in a mesh: row: 2 (over y), col: 16 (over z, x, core).
Axes of the slice: x: 2, y: 2, z: 4, core: 2. Of those that a mesh axis runs over, the one named last changes fastest.
Arguments:
- blocks: bfloat16 [64, 27, 128, 128], P(('row', 'col')), as said below
- columns: int32 [64, 27], P(('row', 'col')), may hold values from 0 to 63, as said below
- counts: int32 [64], P(('row', 'col')), may hold values from 1 to 27
Outputs:
- square: bfloat16 [64, 27, 128, 128], P(('row', 'col'))
- traces: float32 [2], replicated
Inputs may be any that keep to these rules, and one draw needn't show every extreme that they name: `blocks`: exactly symmetric: slot w of block row i is the transpose of slot 26 - w of block row i + w - 13 whenever both rows lie in the window. The first counts[i] entries of row i are the block columns of row i's nonzero blocks in increasing order, each within 13 of i and inside the window; the diagonal block is always among them and the pattern is symmetric; later entries repeat the last one.
All inputs are finite; a program needn't handle non-finite values.
Results may differ from a plain program's by a relative error of at most 0.0012.
Values may be sent and summed in bfloat16 or wider, within the bound.
No kernel may reach another device: no remote copies, remote signals or barrier semaphores. Data moves between devices by JAX's collectives and lax.ppermute only.
A program may use at most 64 MiB of HBM per device.

v0:
```python
import jax
import jax.numpy as jnp
from jax import lax
from jax.sharding import PartitionSpec as P


def passed_along(value, axis, by):
    devices = lax.axis_size(axis)
    pairs = [(i, i + by) for i in range(devices) if 0 <= i + by < devices]
    return lax.ppermute(value, axis, pairs)


def pattern_mask(columns, counts, first_row, half_band, band_width):
    slot_count = columns.shape[1]
    row_count = columns.shape[0]
    row_ids = first_row + jnp.arange(row_count, dtype=jnp.int32)
    offsets = columns - row_ids[:, None] + half_band
    in_list = jnp.arange(slot_count, dtype=jnp.int32)[None, :] < counts[:, None]
    targets = jnp.arange(band_width, dtype=jnp.int32)
    matches = (offsets[:, :, None] == targets[None, None, :]) & in_list[:, :, None]
    return jnp.sum(matches.astype(jnp.float32), axis=1)


def neighbour_rows(source, upward, reach_rows):
    row_count = source.shape[0]
    sections = (reach_rows + row_count - 1) // row_count
    segments = []
    for section_index in range(1, sections + 1):
        wanted = min(row_count, reach_rows - (section_index - 1) * row_count)
        outgoing = source[:wanted] if upward else source[row_count - wanted :]
        received = passed_along(
            outgoing, ("row", "col"), -section_index if upward else section_index
        )
        if upward:
            segments.append((section_index * row_count, received))
        else:
            segments.append((row_count - wanted - section_index * row_count, received))
    if not upward:
        segments = segments[::-1]
    return segments


def take_rows(segments, row_begin, row_end, slot_low, slot_high):
    selected = []
    for seg_begin, seg_rows in segments:
        seg_end = seg_begin + seg_rows.shape[0]
        keep_begin = max(row_begin, seg_begin)
        keep_end = min(row_end, seg_end)
        if keep_begin < keep_end:
            selected.append(
                seg_rows[keep_begin - seg_begin : keep_end - seg_begin, slot_low:slot_high]
            )
    if len(selected) == 1:
        return selected[0]
    return jnp.concatenate(selected, axis=0)


def body(blocks, columns, counts):
    row_count = blocks.shape[0]
    band_width = blocks.shape[1]
    half_band = (band_width - 1) // 2
    block_size = blocks.shape[2]
    first_row = lax.axis_index(("row", "col")) * row_count
    band_mask = pattern_mask(columns, counts, first_row, half_band, band_width)
    density = blocks * band_mask.astype(jnp.bfloat16)[:, :, None, None]
    segments = (
        neighbour_rows(density, False, half_band)
        + [(0, density)]
        + neighbour_rows(density, True, half_band)
    )
    results = []
    for offset in range(-half_band, half_band + 1):
        lower_slot = max(0, offset)
        upper_slot = min(band_width, band_width + offset)
        right_side = take_rows(
            segments, offset, offset + row_count, lower_slot - offset, upper_slot - offset
        )
        results.append(
            jnp.einsum(
                "lsxz,lsyz->lxy",
                density[:, lower_slot:upper_slot],
                right_side,
                preferred_element_type=jnp.float32,
            )
        )
    product = jnp.stack(results, axis=1) * band_mask[:, :, None, None]
    second = jnp.sum(jnp.trace(product[:, half_band], axis1=1, axis2=2))
    third = jnp.sum(density * product)
    square = product.astype(jnp.bfloat16)
    trace_terms = lax.psum((second, third), ("row", "col"))
    traces = jnp.stack([trace_terms[0], trace_terms[1]]) / (
        row_count * lax.axis_size(("row", "col")) * block_size
    )
    return (square, traces)


def solution(mesh):
    return jax.shard_map(
        body,
        mesh=mesh,
        in_specs=(P(("row", "col"), None, None, None), P(("row", "col"), None), P(("row", "col"))),
        out_specs=(P(("row", "col"), None, None, None), P()),
        check_vma=False,
    )
```

profile of v0, /device:TPU:0, one launch (start us, length us, event | category | flops | bytes accessed | tf_op | source)
XLA Modules:
  0.0 691.9 jit_solution(17984066114294293658)
XLA Ops:
  0.6 0.8 subtract_add_fusion
  1.5 0.7 iota_compare_fusion.1
  2.3 1.7 broadcast_multiply_fusion.1
  4.0 6.0 collective-permute-start.1
  10.0 2.8 collective-permute-start.2
  12.7 3.5 collective-permute-start.3
  16.4 4.2 collective-permute-start
  20.6 1.3 collective-permute-start.13
  22.0 120.4 %collective-permute-done = bf16[1,27,128,128]{3,2,1,0:T(8,128)(2,1)S(1)} collective-permute-done((bf16[1,27,128,128]{3,2,1,0:T(8,128)(2,1)S(1)}, bf16[1,27,128,128]{3,2,1,0:T(8,128)(2,1)S(1)}, u32[]{:S(2)}, u32[]{:S(2)}) %collective-permute-start) | collective-permute-done | bytes 884768 | tf_op jit(solution)/shard_map/ppermute | solution.py:10
  142.5 2.2 collective-permute-start.4
  144.7 54.9 %collective-permute-start.5 = (bf16[2,27,128,128]{3,2,1,0:T(8,128)(2,1)S(1)}, bf16[2,27,128,128]{3,2,1,0:T(8,128)(2,1)S(1)}, u32[]{:S(2)}, u32[]{:S(2)}) collective-permute-start(bf16[2,27,128,128]{3,2,1,0:T(8,128)(2,1)S(1)} %broadcast_multiply_fusion.1), channel_id=1, source_target_pairs={{0,2},{1,3},{2,4},{3,5},{4,6},{5,7},{6,8},{7,9},{8,10},{9,11},{10,... | collective-permute-start | bytes 5308424 | tf_op jit(solution)/shard_map/ppermute | solution.py:10
  199.6 100.1 %collective-permute-start.6 = (bf16[2,27,128,128]{3,2,1,0:T(8,128)(2,1)S(1)}, bf16[2,27,128,128]{3,2,1,0:T(8,128)(2,1)S(1)}, u32[]{:S(2)}, u32[]{:S(2)}) collective-permute-start(bf16[2,27,128,128]{3,2,1,0:T(8,128)(2,1)S(1)} %broadcast_multiply_fusion.1), channel_id=1, source_target_pairs={{0,1},{1,2},{2,3},{3,4},{4,5},{5,6},{6,7},{7,8},{8,9},{9,10},{10,1... | collective-permute-start | bytes 5308424 | tf_op jit(solution)/shard_map/ppermute | solution.py:10
  299.7 1.3 collective-permute-start.7
  301.3 1.4 collective-permute-start.8
  305.6 1.3 collective-permute-start.9
  307.0 1.3 collective-permute-start.10
  308.4 1.3 collective-permute-start.11
  309.9 74.7 %collective-permute-done.7 = bf16[2,27,128,128]{3,2,1,0:T(8,128)(2,1)S(1)} collective-permute-done((bf16[2,27,128,128]{3,2,1,0:T(8,128)(2,1)S(1)}, bf16[2,27,128,128]{3,2,1,0:T(8,128)(2,1)S(1)}, u32[]{:S(2)}, u32[]{:S(2)}) %collective-permute-start.7) | collective-permute-done | bytes 1769504 | tf_op jit(solution)/shard_map/ppermute | solution.py:10
  384.6 1.5 collective-permute-start.12
  388.9 0.6 fusion.151
  389.6 69.0 %collective-permute-done.8 = bf16[2,27,128,128]{3,2,1,0:T(8,128)(2,1)S(1)} collective-permute-done((bf16[2,27,128,128]{3,2,1,0:T(8,128)(2,1)S(1)}, bf16[2,27,128,128]{3,2,1,0:T(8,128)(2,1)S(1)}, u32[]{:S(2)}, u32[]{:S(2)}) %collective-permute-start.8) | collective-permute-done | bytes 1769504 | tf_op jit(solution)/shard_map/ppermute | solution.py:10
  459.3 0.6 fusion.172
  460.5 0.6 fusion.157
  462.5 77.2 %collective-permute-done.10 = bf16[2,27,128,128]{3,2,1,0:T(8,128)(2,1)S(1)} collective-permute-done((bf16[2,27,128,128]{3,2,1,0:T(8,128)(2,1)S(1)}, bf16[2,27,128,128]{3,2,1,0:T(8,128)(2,1)S(1)}, u32[]{:S(2)}, u32[]{:S(2)}) %collective-permute-start.10) | collective-permute-done | bytes 1769504 | tf_op jit(solution)/shard_map/ppermute | solution.py:10
  539.8 2.7 collective-permute-done.11
  545.7 26.3 %collective-permute-done.12 = bf16[2,27,128,128]{3,2,1,0:T(8,128)(2,1)S(1)} collective-permute-done((bf16[2,27,128,128]{3,2,1,0:T(8,128)(2,1)S(1)}, bf16[2,27,128,128]{3,2,1,0:T(8,128)(2,1)S(1)}, u32[]{:S(2)}, u32[]{:S(2)}) %collective-permute-start.12) | collective-permute-done | bytes 1769504 | tf_op jit(solution)/shard_map/ppermute | solution.py:10
  573.9 1.1 copy-done
  575.0 2.0 multiply_reduce_fusion
  577.0 1.5 convert_element_type.18
  578.5 0.6 fusion.190
  579.2 110.9 %all-reduce = (f32[1]{0:T(128)}, f32[1]{0:T(128)}) all-reduce(f32[1]{0:T(128)} %bitcast.83, f32[1]{0:T(128)} %bitcast.82), channel_id=1, replica_groups=mesh['row'=2,'col'=16] {'row','col'}, use_global_device_ids=true, to_apply=%region_4.5 | all-reduce | flops 2 | bytes 16 | tf_op jit(solution)/shard_map/psum | solution.py:90
  690.1 1.8 maximum_multiply_fusion
  (72 shorter events, 14.4 us)
Async XLA Ops:
  4.0 195.6 %collective-permute-start.1 = (bf16[2,27,128,128]{3,2,1,0:T(8,128)(2,1)S(1)}, bf16[2,27,128,128]{3,2,1,0:T(8,128)(2,1)S(1)}, u32[]{:S(2)}, u32[]{:S(2)}) collective-permute-start(bf16[2,27,128,128]{3,2,1,0:T(8,128)(2,1)S(1)} %broadcast_multiply_fusion.1), channel_id=1, source_target_pairs={{0,6},{1,7},{2,8},{3,9},{4,10},{5,11},{6,12},{7,13},{8,14},{9,15},... | collective-permute-start | bytes 5308424 | tf_op jit(solution)/shard_map/ppermute | solution.py:10
  10.0 289.8 %collective-permute-start.2 = (bf16[2,27,128,128]{3,2,1,0:T(8,128)(2,1)S(1)}, bf16[2,27,128,128]{3,2,1,0:T(8,128)(2,1)S(1)}, u32[]{:S(2)}, u32[]{:S(2)}) collective-permute-start(bf16[2,27,128,128]{3,2,1,0:T(8,128)(2,1)S(1)} %broadcast_multiply_fusion.1), channel_id=1, source_target_pairs={{0,5},{1,6},{2,7},{3,8},{4,9},{5,10},{6,11},{7,12},{8,13},{9,14},{... | collective-permute-start | bytes 5308424 | tf_op jit(solution)/shard_map/ppermute | solution.py:10
  12.7 288.5 %collective-permute-start.3 = (bf16[2,27,128,128]{3,2,1,0:T(8,128)(2,1)S(1)}, bf16[2,27,128,128]{3,2,1,0:T(8,128)(2,1)S(1)}, u32[]{:S(2)}, u32[]{:S(2)}) collective-permute-start(bf16[2,27,128,128]{3,2,1,0:T(8,128)(2,1)S(1)} %broadcast_multiply_fusion.1), channel_id=1, source_target_pairs={{0,4},{1,5},{2,6},{3,7},{4,8},{5,9},{6,10},{7,11},{8,12},{9,13},{1... | collective-permute-start | bytes 5308424 | tf_op jit(solution)/shard_map/ppermute | solution.py:10
  16.4 126.1 %collective-permute-start = (bf16[1,27,128,128]{3,2,1,0:T(8,128)(2,1)S(1)}, bf16[1,27,128,128]{3,2,1,0:T(8,128)(2,1)S(1)}, u32[]{:S(2)}, u32[]{:S(2)}) collective-permute-start(bf16[1,27,128,128]{3,2,1,0:T(8,128)(2,1)S(1)} %get-tuple-element.7), channel_id=1, source_target_pairs={{0,7},{1,8},{2,9},{3,10},{4,11},{5,12},{6,13},{7,14},{8,15},{9,16}... | collective-permute-start | bytes 2654216 | tf_op jit(solution)/shard_map/ppermute | solution.py:10
  20.6 124.1 %collective-permute-start.13 = (bf16[1,27,128,128]{3,2,1,0:T(8,128)(2,1)S(1)}, bf16[1,27,128,128]{3,2,1,0:T(8,128)(2,1)S(1)}, u32[]{:S(2)}, u32[]{:S(2)}) collective-permute-start(bf16[1,27,128,128]{3,2,1,0:T(8,128)(2,1)S(1)} %get-tuple-element.6), channel_id=1, source_target_pairs={{7,0},{8,1},{9,2},{10,3},{11,4},{12,5},{13,6},{14,7},{15,8},{16,9}... | collective-permute-start | bytes 2654216 | tf_op jit(solution)/shard_map/ppermute | solution.py:10
  142.5 158.6 %copy-start.2 = (bf16[1,27,128,128]{3,2,1,0:T(8,128)(2,1)}, bf16[1,27,128,128]{3,2,1,0:T(8,128)(2,1)S(1)}, u32[]{:S(2)}) copy-start(bf16[1,27,128,128]{3,2,1,0:T(8,128)(2,1)S(1)} %collective-permute-done) | copy-start | bytes 2654212
  142.5 163.1 %collective-permute-start.4 = (bf16[2,27,128,128]{3,2,1,0:T(8,128)(2,1)S(1)}, bf16[2,27,128,128]{3,2,1,0:T(8,128)(2,1)S(1)}, u32[]{:S(2)}, u32[]{:S(2)}) collective-permute-start(bf16[2,27,128,128]{3,2,1,0:T(8,128)(2,1)S(1)} %broadcast_multiply_fusion.1), channel_id=1, source_target_pairs={{0,3},{1,4},{2,5},{3,6},{4,7},{5,8},{6,9},{7,10},{8,11},{9,12},{10... | collective-permute-start | bytes 5308424 | tf_op jit(solution)/shard_map/ppermute | solution.py:10
  144.7 156.4 %copy-start.1 = (bf16[1,27,128,128]{3,2,1,0:T(8,128)(2,1)}, bf16[1,27,128,128]{3,2,1,0:T(8,128)(2,1)S(1)}, u32[]{:S(2)}) copy-start(bf16[1,27,128,128]{3,2,1,0:T(8,128)(2,1)S(1)} %collective-permute-done.13) | copy-start | bytes 2654212
  144.7 162.3 %collective-permute-start.5 = (bf16[2,27,128,128]{3,2,1,0:T(8,128)(2,1)S(1)}, bf16[2,27,128,128]{3,2,1,0:T(8,128)(2,1)S(1)}, u32[]{:S(2)}, u32[]{:S(2)}) collective-permute-start(bf16[2,27,128,128]{3,2,1,0:T(8,128)(2,1)S(1)} %broadcast_multiply_fusion.1), channel_id=1, source_target_pairs={{0,2},{1,3},{2,4},{3,5},{4,6},{5,7},{6,8},{7,9},{8,10},{9,11},{10,... | collective-permute-start | bytes 5308424 | tf_op jit(solution)/shard_map/ppermute | solution.py:10
  199.6 108.8 %collective-permute-start.6 = (bf16[2,27,128,128]{3,2,1,0:T(8,128)(2,1)S(1)}, bf16[2,27,128,128]{3,2,1,0:T(8,128)(2,1)S(1)}, u32[]{:S(2)}, u32[]{:S(2)}) collective-permute-start(bf16[2,27,128,128]{3,2,1,0:T(8,128)(2,1)S(1)} %broadcast_multiply_fusion.1), channel_id=1, source_target_pairs={{0,1},{1,2},{2,3},{3,4},{4,5},{5,6},{6,7},{7,8},{8,9},{9,10},{10,1... | collective-permute-start | bytes 5308424 | tf_op jit(solution)/shard_map/ppermute | solution.py:10
  299.7 84.9 %collective-permute-start.7 = (bf16[2,27,128,128]{3,2,1,0:T(8,128)(2,1)S(1)}, bf16[2,27,128,128]{3,2,1,0:T(8,128)(2,1)S(1)}, u32[]{:S(2)}, u32[]{:S(2)}) collective-permute-start(bf16[2,27,128,128]{3,2,1,0:T(8,128)(2,1)S(1)} %broadcast_multiply_fusion.1), channel_id=1, source_target_pairs={{1,0},{2,1},{3,2},{4,3},{5,4},{6,5},{7,6},{8,7},{9,8},{10,9},{11,1... | collective-permute-start | bytes 5308424 | tf_op jit(solution)/shard_map/ppermute | solution.py:10
  301.2 1.6 slice-start.1
  301.3 157.3 %collective-permute-start.8 = (bf16[2,27,128,128]{3,2,1,0:T(8,128)(2,1)S(1)}, bf16[2,27,128,128]{3,2,1,0:T(8,128)(2,1)S(1)}, u32[]{:S(2)}, u32[]{:S(2)}) collective-permute-start(bf16[2,27,128,128]{3,2,1,0:T(8,128)(2,1)S(1)} %broadcast_multiply_fusion.1), channel_id=1, source_target_pairs={{2,0},{3,1},{4,2},{5,3},{6,4},{7,5},{8,6},{9,7},{10,8},{11,9},{12,... | collective-permute-start | bytes 5308424 | tf_op jit(solution)/shard_map/ppermute | solution.py:10
  305.6 156.8 %collective-permute-start.9 = (bf16[2,27,128,128]{3,2,1,0:T(8,128)(2,1)S(1)}, bf16[2,27,128,128]{3,2,1,0:T(8,128)(2,1)S(1)}, u32[]{:S(2)}, u32[]{:S(2)}) collective-permute-start(bf16[2,27,128,128]{3,2,1,0:T(8,128)(2,1)S(1)} %broadcast_multiply_fusion.1), channel_id=1, source_target_pairs={{3,0},{4,1},{5,2},{6,3},{7,4},{8,5},{9,6},{10,7},{11,8},{12,9},{13... | collective-permute-start | bytes 5308424 | tf_op jit(solution)/shard_map/ppermute | solution.py:10
  307.0 232.7 %collective-permute-start.10 = (bf16[2,27,128,128]{3,2,1,0:T(8,128)(2,1)S(1)}, bf16[2,27,128,128]{3,2,1,0:T(8,128)(2,1)S(1)}, u32[]{:S(2)}, u32[]{:S(2)}) collective-permute-start(bf16[2,27,128,128]{3,2,1,0:T(8,128)(2,1)S(1)} %broadcast_multiply_fusion.1), channel_id=1, source_target_pairs={{4,0},{5,1},{6,2},{7,3},{8,4},{9,5},{10,6},{11,7},{12,8},{13,9},{1... | collective-permute-start | bytes 5308424 | tf_op jit(solution)/shard_map/ppermute | solution.py:10
  308.4 234.1 %collective-permute-start.11 = (bf16[2,27,128,128]{3,2,1,0:T(8,128)(2,1)S(1)}, bf16[2,27,128,128]{3,2,1,0:T(8,128)(2,1)S(1)}, u32[]{:S(2)}, u32[]{:S(2)}) collective-permute-start(bf16[2,27,128,128]{3,2,1,0:T(8,128)(2,1)S(1)} %broadcast_multiply_fusion.1), channel_id=1, source_target_pairs={{5,0},{6,1},{7,2},{8,3},{9,4},{10,5},{11,6},{12,7},{13,8},{14,9},{... | collective-permute-start | bytes 5308424 | tf_op jit(solution)/shard_map/ppermute | solution.py:10
  384.6 187.4 %collective-permute-start.12 = (bf16[2,27,128,128]{3,2,1,0:T(8,128)(2,1)S(1)}, bf16[2,27,128,128]{3,2,1,0:T(8,128)(2,1)S(1)}, u32[]{:S(2)}, u32[]{:S(2)}) collective-permute-start(bf16[2,27,128,128]{3,2,1,0:T(8,128)(2,1)S(1)} %broadcast_multiply_fusion.1), channel_id=1, source_target_pairs={{6,0},{7,1},{8,2},{9,3},{10,4},{11,5},{12,6},{13,7},{14,8},{15,9},... | collective-permute-start | bytes 5308424 | tf_op jit(solution)/shard_map/ppermute | solution.py:10
  572.5 1.0 slice-start
  573.5 1.5 copy-start
where the time goes:
time: 694 us; the launch traced here: 692 us
  waiting for transfers between devices  370 us (53%)
  starting transfers between devices  183 us (26%)
  blocking collectives  111 us (16%)
  matrix products  13.9 us (2%)
  other arithmetic  9.24 us (1%)
    ppermute x14, waiting for transfers between devices, passed_along(): return lax.ppermute(value, axis, pairs)  370 us
    ppermute x14, starting transfers between devices, passed_along(): return lax.ppermute(value, axis, pairs)  183 us
    psum x1, blocking collectives, body(): trace_terms = lax.psum((second, third), ('row', 'col'))  111 us
  transfers between devices with their start and end apart: 14, of which 6 were waited for; matrix products, arithmetic and copies ran while one was open for 2% of the time, Pallas kernels for 0%

commit v1 on v0

v1 whole, which is shorter than its diff:
```python
import jax
import jax.numpy as jnp
from jax import lax
from jax.experimental import pallas as pl
from jax.experimental.pallas import tpu as pltpu
from jax.sharding import PartitionSpec as P

AXES = ("row", "col")
HALF = 13
BAND = 2 * HALF + 1
BS = 128
NEAR = HALF
FAR = 12
NCOL = NEAR + 1
NEAR_W, OWN_W, FAR_W = NCOL * BS, 4 * BS, FAR * BS
OWN_AT, FAR_AT = NEAR_W, NEAR_W + OWN_W
VMEM_LIMIT = 48 * 1024 * 1024

VM = pl.BlockSpec(memory_space=pltpu.VMEM)
SM = pl.BlockSpec(memory_space=pltpu.SMEM)


def params():
    return pltpu.CompilerParams(vmem_limit_bytes=VMEM_LIMIT)


def permute(value, target):
    devices = lax.axis_size(AXES)
    pairs = [(i, target(i)) for i in range(devices)]
    return lax.ppermute(value, AXES, [(i, j) for i, j in pairs if 0 <= j < devices])


def to_partner(value):
    return permute(value, lambda i: i ^ 1)


def to_side(value, distance):
    def target(i):
        chip, core = divmod(i, 2)
        return 2 * (chip + distance) if core else 2 * (chip - distance) + 1

    return permute(value, target)


def total(value):
    devices = lax.axis_size(AXES)
    if devices & (devices - 1):
        return lax.psum(value, AXES)
    step = 1
    while step < devices:
        value = value + permute(value, lambda i: i ^ step)
        step *= 2
    return value


def nn(a, b):
    return lax.dot_general(a, b, (((1,), (0,)), ((), ())), preferred_element_type=jnp.float32)


def nt(a, b):
    return lax.dot_general(a, b, (((1,), (1,)), ((), ())), preferred_element_type=jnp.float32)


def cut(i, n=1):
    return slice(i * BS, (i + n) * BS)


def own_kernel(meta, columns, counts, blocks, mine, other, mask, flags):
    core = meta[0]
    first_row = meta[1]
    for r in range(2):

        @pl.loop(0, BAND)
        def _(w):
            flags[r, w] = 0

        @pl.loop(0, counts[r])
        def _(n):
            flags[r, columns[r, n] - first_row - r + HALF] = 1

    for r in range(2):

        @pl.loop(0, BAND)
        def _(a):
            keep = flags[r, a]
            mask[r, a] = keep
            block = jnp.where(keep > 0, blocks[r, a], jnp.zeros((BS, BS), blocks.dtype))
            e = jnp.where(core > 0, 1 - r, r)
            w = jnp.where(core > 0, BAND - 1 - a, a)
            mine[e, w] = block
            other[1 - e, BAND - 1 - w] = block


def own_rows(meta, columns, counts, blocks):
    shape = jax.ShapeDtypeStruct(blocks.shape, blocks.dtype)
    return pl.pallas_call(
        own_kernel,
        out_shape=(shape, shape, jax.ShapeDtypeStruct((2, BAND), jnp.int32)),
        in_specs=[SM, SM, SM, VM],
        out_specs=(VM, VM, SM),
        scratch_shapes=[pltpu.SMEM((2, BAND), jnp.int32)],
        compiler_params=params(),
        name="own_rows",
    )(meta, columns, counts, blocks)


def fill_rows(mine, part, rows):
    zero = jnp.zeros((BS, BS), rows.dtype)

    def block(e, k):
        w = k - e + HALF
        if not 0 <= w < BAND:
            return zero
        return mine[e, w] if e < 2 else part[e - 2, w]

    for e in range(4):
        for t in range(1, NCOL + 1):
            rows[cut(e), cut(t - 1)] = block(e, -t)
        if rows.shape[1] > NEAR_W:
            for k in range(4):
                rows[cut(e), OWN_AT + k * BS : OWN_AT + (k + 1) * BS] = block(e, k)
            for u in range(1, FAR + 1):
                rows[cut(e), FAR_AT + (u - 1) * BS : FAR_AT + u * BS] = block(e, 3 + u)


def cross_start(t):
    return sum(11 - 2 * s for s in range(1, t))


def far_kernel(mine, part, cross, swapped, corner, partial, inner, sums, rows, upper, lower):
    fill_rows(mine, part, rows)
    zero = jnp.zeros((BS, BS), rows.dtype)

    def from_near(t, u):
        if t + u > 10:
            return zero
        if t == 5:
            return corner[0]
        return cross[cross_start(t) + 10 - t - u]

    def from_far(u, t):
        if t + u > 10:
            return zero
        return swapped[cross_start(u) + 10 - t - u]

    def tr(x):
        return jnp.transpose(x.astype(jnp.float32)).astype(x.dtype)

    for c in range(5):
        for g in range(c, 5 - c):
            for t in (2 * c + 1, 2 * c + 2):
                for u in (2 * g + 1, 2 * g + 2):
                    if t <= u or t + u > 10:
                        upper[cut(t - 1), cut(u - 1)] = from_near(t, u)
                    else:
                        upper[cut(t - 1), cut(u - 1)] = tr(from_far(u, t))
        for g in range(min(c, 5 - c)):
            for t in (2 * c + 1, 2 * c + 2):
                for u in (2 * g + 1, 2 * g + 2):
                    lower[cut(u - 1), cut(t - 1)] = from_far(u, t)

    third = jnp.zeros((1, 1), jnp.float32)
    own = rows[:, OWN_AT:FAR_AT]
    for c in range(NCOL // 2):
        near = rows[:, cut(2 * c, 2)]
        value = nn(own, near)
        if c < 3:
            value += nt(
                rows[:, FAR_AT + 2 * c * BS : FAR_AT + (10 - 2 * c) * BS],
                upper[cut(2 * c, 2), 2 * c * BS : (10 - 2 * c) * BS],
            )
        before = min(c, 5 - c)
        if before > 0:
            value += nn(
                rows[:, FAR_AT : FAR_AT + 2 * before * BS],
                lower[: 2 * before * BS, cut(2 * c, 2)],
            )
        partial[:, cut(2 * c, 2)] = value
        third += jnp.sum(near.astype(jnp.float32) * value, keepdims=True)
    third = 3.0 * third
    top = rows[: 2 * BS, OWN_AT:FAR_AT]
    third += jnp.sum(top.astype(jnp.float32) * nn(top, own), keepdims=True)
    inner[...] = nt(rows[: 2 * BS, :], rows[...])
    second = jnp.zeros((1, 1), jnp.float32)
    for e in range(2):
        for w in range(BAND):
            x = mine[e, w].astype(jnp.float32)
            second += jnp.sum(x * x, keepdims=True)
    sums[0:1, :] = jnp.broadcast_to(second, (1, BS))
    sums[1:2, :] = jnp.broadcast_to(third, (1, BS))


def far_part(mine, part, cross, swapped, corner):
    return pl.pallas_call(
        far_kernel,
        out_shape=(
            jax.ShapeDtypeStruct((4 * BS, NEAR_W), jnp.float32),
            jax.ShapeDtypeStruct((2 * BS, OWN_W), jnp.float32),
            jax.ShapeDtypeStruct((2, BS), jnp.float32),
        ),
        in_specs=[VM] * 5,
        out_specs=(VM,) * 3,
        scratch_shapes=[
            pltpu.VMEM((4 * BS, FAR_AT + FAR_W), jnp.bfloat16),
            pltpu.VMEM((10 * BS, 10 * BS), jnp.bfloat16),
            pltpu.VMEM((10 * BS, 10 * BS), jnp.bfloat16),
        ],
        compiler_params=params(),
        cost_estimate=pl.CostEstimate(flops=3 * 10**9, bytes_accessed=10**7, transcendentals=0),
        name="far_part",
    )(mine, part, cross, swapped, corner)


def near_start(t):
    first = 4 * ((t - 1) // 4) + 1
    return sum(14 - s for s in range(first, t))


def near_kernel(meta, mask, mine, part, d1, d2, d3, d4, partial, inner, out, away, rows, pairs):
    core = meta[0]
    fill_rows(mine, part, rows)
    zero = jnp.zeros((BS, BS), rows.dtype)
    packed = (d1, d2, d3, d4)

    def block(t, s):
        if s > NEAR:
            return zero
        return packed[(t - 1) // 4][near_start(t) + s - t]

    for t in range(1, NCOL + 1):
        for s in range(t, NCOL + 1):
            pairs[cut(t - 1), cut(s - 1)] = block(t, s)
        if t % 2 == 0:
            x = block(t - 1, t)
            x = jnp.transpose(x.astype(jnp.float32)).astype(x.dtype)
            pairs[cut(t - 1), cut(t - 2)] = x

    def put(e, w, value):
        r = jnp.where(core > 0, 1 - e, e)
        a = jnp.where(core > 0, BAND - 1 - w, w)
        keep = mask[r, a]
        out[r, a] = jnp.where(keep > 0, value, 0.0).astype(out.dtype)

    for e in range(2):
        for k in range(4):
            put(e, k - e + HALF, inner[cut(e), cut(k)])
    for c in range(NCOL // 2):
        value = partial[:, cut(2 * c, 2)]
        value += nt(rows[:, 2 * c * BS :], pairs[cut(2 * c, 2), 2 * c * BS :])
        if c > 0:
            value += nn(rows[:, : 2 * c * BS], pairs[: 2 * c * BS, cut(2 * c, 2)])
        for n in range(2):
            t = 2 * c + 1 + n
            for e in range(4):
                if e + t > HALF:
                    continue
                x = value[cut(e), cut(n)]
                if e < 2:
                    put(e, HALF - e - t, x)
                else:
                    away[(e - 2) * 11 + t - 1] = x.astype(away.dtype)


def near_part(meta, mask, mine, part, near, partial, inner):
    return pl.pallas_call(
        near_kernel,
        out_shape=(
            jax.ShapeDtypeStruct(mine.shape, mine.dtype),
            jax.ShapeDtypeStruct((21, BS, BS), mine.dtype),
        ),
        in_specs=[SM, SM] + [VM] * 8,
        out_specs=(VM, VM),
        scratch_shapes=[
            pltpu.VMEM((4 * BS, NEAR_W), jnp.bfloat16),
            pltpu.VMEM((NEAR_W, NEAR_W), jnp.bfloat16),
        ],
        compiler_params=params(),
        cost_estimate=pl.CostEstimate(flops=3 * 10**9, bytes_accessed=10**7, transcendentals=0),
        name="near_part",
    )(meta, mask, mine, part, *near, partial, inner)


def join_kernel(meta, mask, came, _, out, held, sems):
    core = meta[0]
    copies = []
    for e, count, base in ((0, 10, 11), (1, 11, 0)):
        r = jnp.where(core > 0, 1 - e, e)

        @pl.loop(0, count)
        def _(n):
            w = BAND - count + n
            a = jnp.where(core > 0, BAND - 1 - w, w)
            spot = jnp.where(core > 0, count - 1 - n, n)
            keep = mask[r, a]
            x = came[base + n]
            held[base + spot] = jnp.where(keep > 0, x, jnp.zeros_like(x))

        start = jnp.where(core > 0, 0, BAND - count)
        copy = pltpu.make_async_copy(
            held.at[pl.ds(base, count)], out.at[r, pl.ds(start, count)], sems.at[e]
        )
        copy.start()
        copies.append(copy)
    for copy in copies:
        copy.wait()


def join(meta, mask, came, out):
    anywhere = pl.BlockSpec(memory_space=pl.ANY)
    return pl.pallas_call(
        join_kernel,
        out_shape=jax.ShapeDtypeStruct(out.shape, out.dtype),
        in_specs=[SM, SM, VM, anywhere],
        out_specs=anywhere,
        scratch_shapes=[
            pltpu.VMEM(came.shape, came.dtype),
            pltpu.SemaphoreType.DMA((2,)),
        ],
        input_output_aliases={3: 0},
        compiler_params=params(),
        name="join",
    )(meta, mask, came, out)


def body(blocks, columns, counts):
    index = lax.axis_index(AXES)
    meta = jnp.stack([index % 2, index * 2]).astype(jnp.int32)
    mine, other, mask = own_rows(meta, columns, counts, blocks)
    part = to_partner(other)

    def row(e):
        return mine[e] if e < 2 else part[e - 2]

    cross = jnp.concatenate([row(e)[: 9 - 2 * e] for e in range(4)], axis=0)
    cross = to_side(cross, 1)
    corner = to_side(mine[0, :1], 2)
    near = []
    for distance in range(1, 5):
        runs = [(e, 4 * (distance - 1) + 1 + e) for e in range(4)]
        runs = [row(e)[HALF : BAND - t] for e, t in runs if t <= HALF]
        near.append(to_side(jnp.concatenate(runs, axis=0), distance))
    swapped = to_partner(cross)
    partial, inner, sums = far_part(mine, part, cross, swapped, corner)
    traces = total(sums[:, 0]) / (2 * BS * lax.axis_size(AXES))
    out, away = near_part(meta, mask, mine, part, near, partial, inner)
    square = join(meta, mask, to_partner(away), out)
    return square, traces


def solution(mesh):
    return jax.shard_map(
        body,
        mesh=mesh,
        in_specs=(P(AXES, None, None, None), P(AXES, None), P(AXES)),
        out_specs=(P(AXES, None, None, None), P()),
        check_vma=False,
    )
```

time: 694 us -> 121 us (0.17)
  waiting for transfers between devices: 370 us -> 13.4 us
  blocking collectives: 111 us -> 0 us
  starting transfers between devices: 183 us -> 84.3 us
  Pallas kernels: 0 us -> 17.8 us
  matrix products: 13.9 us -> 0 us
  other arithmetic: 9.24 us -> 1.12 us
    ppermute x14, waiting for transfers between devices: 370 us -> 13.4 us  [permute(): lax.ppermute(value, AXES, [(i, j) for i, j in pairs if 0 <= j < devices])]
    psum x1 -> x0, blocking collectives: 111 us -> none  [body(): trace_terms = lax.psum((second, third), ('row', 'col'))]
    ppermute x14, starting transfers between devices: 183 us -> 84.3 us  [permute(): lax.ppermute(value, AXES, [(i, j) for i, j in pairs if 0 <= j < devices])]
    pallas_call x0 -> x4, Pallas kernels: none -> 17.8 us  [the longest x1 7.72 us: near_part(): pl.pallas_call(near_kernel, out_shape=(jax.ShapeDtypeStruct(mine.shape, m...]
    dot_general x27 -> x0, matrix products: 13.9 us -> none  [body(): jnp.einsum('lsxz,lsyz->lxy', density[:, lower_slot:upper_slot], right_sid...]
  transfers between devices with their start and end apart: 14 -> 14, of which waited for: 6 -> 6; matrix products, arithmetic and copies ran while one was open for 2% -> 1% of each run, Pallas kernels for 0% -> 5%
where the time goes in v1:
time: 121 us
  starting transfers between devices  84.3 us (70%)
  Pallas kernels  17.8 us (15%)
  waiting for transfers between devices  13.4 us (11%)
  local copies, waits for them, and re-layouts  3.21 us (3%)
    ppermute x14, starting transfers between devices, permute(): lax.ppermute(value, AXES, [(i, j) for i, j in pairs if 0 <= j < devices])  84.3 us
    ppermute x14, waiting for transfers between devices, permute(): lax.ppermute(value, AXES, [(i, j) for i, j in pairs if 0 <= j < devices])  13.4 us
    pallas_call x1, Pallas kernels, near_part(): pl.pallas_call(near_kernel, out_shape=(jax.ShapeDtypeStruct(mine.shape, m...  7.72 us
    pallas_call x1, Pallas kernels, far_part(): pl.pallas_call(far_kernel, out_shape=(jax.ShapeDtypeStruct((4 * BS, NEAR_...  5.81 us
    unnamed x8, local copies, waits for them, and re-layouts  2.81 us
    pallas_call x1, Pallas kernels, own_rows(): pl.pallas_call(own_kernel, out_shape=(shape, shape, jax.ShapeDtypeStruct(...  2.54 us
  transfers between devices with their start and end apart: 14, of which 6 were waited for; matrix products, arithmetic and copies ran while one was open for 1% of the time, Pallas kernels for 5%

profile of v1, /device:TPU:0, one launch (start us, length us, event | category | flops | bytes accessed | tf_op | source)
XLA Modules:
  0.0 120.6 jit_solution(6445766852317186233)
XLA Ops:
  0.6 0.1 pad_add_fusion.meta
  0.7 1.5 %copy-done = bf16[2,27,128,128]{3,2,1,0:T(8,128)(2,1)S(1)} copy-done((bf16[2,27,128,128]{3,2,1,0:T(8,128)(2,1)S(1)}, bf16[2,27,128,128]{3,2,1,0:T(8,128)(2,1)}, u32[]{:S(2)}) %copy-start) | copy-done | bytes 1769496
  2.2 0.7 copy-done.2
  2.9 0.7 copy-done.3
  3.5 2.5 %own_rows.1 = (bf16[2,27,128,128]{3,2,1,0:T(8,128)(2,1)S(1)}, bf16[2,27,128,128]{3,2,1,0:T(8,128)(2,1)S(1)}, s32[2,27]{1,0:T(2,128)S(1)}) custom-call(s32[2]{0:T(128)S(1)} %pad_add_fusion.meta, s32[2,27]{1,0:T(2,128)S(1)} %copy-done.2, s32[2]{0:T(128)S(1)} %copy-done.3, bf16[2,27,128,128]{3,2,1,0:T(8,128)(2,1)S(1)} %copy-done), custom_call_target="tpu_custom_call" | custom-call | tf_op jit(solution)/shard_map/own_rows/pallas_call | solution.py:96
  6.1 0.6 collective-permute-start
  6.8 3.1 %collective-permute-done.part = bf16[2,27,128,128]{3,2,1,0:T(8,128)(2,1)S(1)} collective-permute-done((bf16[2,27,128,128]{3,2,1,0:T(8,128)(2,1)S(1)}, bf16[2,27,128,128]{3,2,1,0:T(8,128)(2,1)S(1)}, u32[]{:S(2)}, u32[]{:S(2)}) %collective-permute-start) | collective-permute-done | bytes 1769504 | tf_op jit(solution)/shard_map/ppermute | solution.py:30
  10.0 0.1 pad_maximum_fusion.2
  10.1 0.7 collective-permute-start.5
  10.9 0.2 pad_maximum_fusion
  11.1 0.8 collective-permute-start.1
  11.9 0.1 pad_maximum_fusion.1
  12.1 0.7 collective-permute-start.2
  12.8 29.5 %collective-permute-start.6 = (bf16[24,128,128]{2,1,0:T(8,128)(2,1)S(1)}, bf16[24,128,128]{2,1,0:T(8,128)(2,1)S(1)}, u32[]{:S(2)}, u32[]{:S(2)}) collective-permute-start(bf16[24,128,128]{2,1,0:T(8,128)(2,1)S(1)} %collective-permute-done.5.cross), channel_id=1, source_target_pairs={{0,1},{1,0},{2,3},{3,2},{4,5},{5,4},{6,7},{7,6},{8,9},{9,8},{10,11... | collective-permute-start | bytes 2359304 | tf_op jit(solution)/shard_map/ppermute | solution.py:30
  42.4 0.7 collective-permute-start.3
  43.1 0.7 collective-permute-start.7
  43.8 0.7 collective-permute-start.4
  44.5 5.8 %far_part.1 = (f32[512,1792]{1,0:T(8,128)}, f32[256,512]{1,0:T(8,128)S(1)}, f32[2,128]{1,0:T(2,128)S(1)}) custom-call(bf16[2,27,128,128]{3,2,1,0:T(8,128)(2,1)S(1)} %get-tuple-element.11.mine, bf16[2,27,128,128]{3,2,1,0:T(8,128)(2,1)S(1)} %collective-permute-done.part, bf16[24,128,128]{2,1,0:T(8,128)(2,1)S(1)} %collective-permute-done.5.cross, ...), custom_call_target="tpu_custom_call" | custom-call | flops 3000000000 | bytes 10000000 | tf_op jit(solution)/shard_map/far_part/pallas_call | solution.py:194
  50.3 7.7 %near_part.1 = (bf16[2,27,128,128]{3,2,1,0:T(8,128)(2,1)}, bf16[21,128,128]{2,1,0:T(8,128)(2,1)S(1)}) custom-call(s32[2]{0:T(128)S(1)} %pad_add_fusion.meta, s32[2,27]{1,0:T(2,128)S(1)} %get-tuple-element.10.mask, bf16[2,27,128,128]{3,2,1,0:T(8,128)(2,1)S(1)} %get-tuple-element.11.mine, bf16[2,27,128,128]{3,2,1,0:T(8,128)(2,1)} %copy-done.1, ...), custom_call_target="tpu_custom_call" | custom-call | flops 3000000000 | bytes 10000000 | tf_op jit(solution)/shard_map/near_part/pallas_call | solution.py:265
  58.1 37.0 %collective-permute-start.8 = (bf16[21,128,128]{2,1,0:T(8,128)(2,1)S(1)}, bf16[21,128,128]{2,1,0:T(8,128)(2,1)S(1)}, u32[]{:S(2)}, u32[]{:S(2)}) collective-permute-start(bf16[21,128,128]{2,1,0:T(8,128)(2,1)S(1)} %get-tuple-element.15), channel_id=1, source_target_pairs={{0,1},{1,0},{2,3},{3,2},{4,5},{5,4},{6,7},{7,6},{8,9},{9,8},{10,11... | collective-permute-start | bytes 2064392 | tf_op jit(solution)/shard_map/ppermute | solution.py:30
  95.1 0.1 slice_reduce_fusion
  95.3 1.6 %collective-permute-done.9 = f32[2]{0:T(128)S(1)} collective-permute-done((f32[2]{0:T(128)S(1)}, f32[2]{0:T(128)S(1)}, u32[]{:S(2)}, u32[]{:S(2)}) %collective-permute-start.9) | collective-permute-done | bytes 40 | tf_op jit(solution)/shard_map/ppermute | solution.py:30
  96.9 3.3 %collective-permute-start.10 = (f32[2]{0:T(128)S(1)}, f32[2]{0:T(128)S(1)}, u32[]{:S(2)}, u32[]{:S(2)}) collective-permute-start(f32[2]{0:T(128)S(1)} %add.24), channel_id=1, source_target_pairs={{0,2},{1,3},{2,0},{3,1},{4,6},{5,7},{6,4},{7,5},{8,10},{9,11},{10,... | collective-permute-start | bytes 32 | tf_op jit(solution)/shard_map/ppermute | solution.py:30
  100.2 1.5 %collective-permute-done.10 = f32[2]{0:T(128)S(1)} collective-permute-done((f32[2]{0:T(128)S(1)}, f32[2]{0:T(128)S(1)}, u32[]{:S(2)}, u32[]{:S(2)}) %collective-permute-start.10) | collective-permute-done | bytes 40 | tf_op jit(solution)/shard_map/ppermute | solution.py:30
  101.7 0.7 collective-permute-start.11
  102.4 2.8 %collective-permute-done.11 = f32[2]{0:T(128)S(1)} collective-permute-done((f32[2]{0:T(128)S(1)}, f32[2]{0:T(128)S(1)}, u32[]{:S(2)}, u32[]{:S(2)}) %collective-permute-start.11) | collective-permute-done | bytes 40 | tf_op jit(solution)/shard_map/ppermute | solution.py:30
  105.2 1.6 %collective-permute-start.12 = (f32[2]{0:T(128)S(1)}, f32[2]{0:T(128)S(1)}, u32[]{:S(2)}, u32[]{:S(2)}) collective-permute-start(f32[2]{0:T(128)S(1)} %add.26), channel_id=1, source_target_pairs={{0,8},{1,9},{2,10},{3,11},{4,12},{5,13},{6,14},{7,15},{8,0},{9,1},... | collective-permute-start | bytes 32 | tf_op jit(solution)/shard_map/ppermute | solution.py:30
  106.8 2.8 %collective-permute-done.12 = f32[2]{0:T(128)S(1)} collective-permute-done((f32[2]{0:T(128)S(1)}, f32[2]{0:T(128)S(1)}, u32[]{:S(2)}, u32[]{:S(2)}) %collective-permute-start.12) | collective-permute-done | bytes 40 | tf_op jit(solution)/shard_map/ppermute | solution.py:30
  109.7 7.2 %collective-permute-start.13 = (f32[2]{0:T(128)S(1)}, f32[2]{0:T(128)S(1)}, u32[]{:S(2)}, u32[]{:S(2)}) collective-permute-start(f32[2]{0:T(128)S(1)} %add.27), channel_id=1, source_target_pairs={{0,16},{1,17},{2,18},{3,19},{4,20},{5,21},{6,22},{7,23},{8,24},{9,... | collective-permute-start | bytes 32 | tf_op jit(solution)/shard_map/ppermute | solution.py:30
  116.9 1.5 %collective-permute-done.13 = f32[2]{0:T(128)S(1)} collective-permute-done((f32[2]{0:T(128)S(1)}, f32[2]{0:T(128)S(1)}, u32[]{:S(2)}, u32[]{:S(2)}) %collective-permute-start.13) | collective-permute-done | bytes 40 | tf_op jit(solution)/shard_map/ppermute | solution.py:30
  118.4 0.5 add_multiply_fusion
  119.0 1.7 %join.1 = bf16[2,27,128,128]{3,2,1,0:T(8,128)(2,1)} custom-call(s32[2]{0:T(128)S(1)} %pad_add_fusion.meta, s32[2,27]{1,0:T(2,128)S(1)} %get-tuple-element.10.mask, bf16[21,128,128]{2,1,0:T(8,128)(2,1)S(1)} %collective-permute-done.8.came, bf16[2,27,128,128]{3,2,1,0:T(8,128)(2,1)} %get-tuple-element.16._), custom_call_target="tpu_custom_call", output_to_operand_aliasing={{}: (3, {})} | custom-call | tf_op jit(solution)/shard_map/join/pallas_call | solution.py:310
  (34 shorter events, 0.5 us)
Async XLA Ops:
  0.7 1.5 %copy-start = (bf16[2,27,128,128]{3,2,1,0:T(8,128)(2,1)S(1)}, bf16[2,27,128,128]{3,2,1,0:T(8,128)(2,1)}, u32[]{:S(2)}) copy-start(bf16[2,27,128,128]{3,2,1,0:T(8,128)(2,1)} %blocks.1) | copy-start | bytes 5308420
  2.2 0.7 copy-start.2
  2.9 0.7 copy-start.3
  6.1 3.9 %collective-permute-start = (bf16[2,27,128,128]{3,2,1,0:T(8,128)(2,1)S(1)}, bf16[2,27,128,128]{3,2,1,0:T(8,128)(2,1)S(1)}, u32[]{:S(2)}, u32[]{:S(2)}) collective-permute-start(bf16[2,27,128,128]{3,2,1,0:T(8,128)(2,1)S(1)} %get-tuple-element.12), channel_id=1, source_target_pairs={{0,1},{1,0},{2,3},{3,2},{4,5},{5,4},{6,7},{7,6},{8,9},{9,8},{10,11... | collective-permute-start | bytes 5308424 | tf_op jit(solution)/shard_map/ppermute | solution.py:30
  10.0 34.5 %copy-start.1 = (bf16[2,27,128,128]{3,2,1,0:T(8,128)(2,1)}, bf16[2,27,128,128]{3,2,1,0:T(8,128)(2,1)S(1)}, u32[]{:S(2)}) copy-start(bf16[2,27,128,128]{3,2,1,0:T(8,128)(2,1)S(1)} %collective-permute-done.part) | copy-start | bytes 5308420
  10.1 2.7 %collective-permute-start.5 = (bf16[24,128,128]{2,1,0:T(8,128)(2,1)S(1)}, bf16[24,128,128]{2,1,0:T(8,128)(2,1)S(1)}, u32[]{:S(2)}, u32[]{:S(2)}) collective-permute-start(bf16[24,128,128]{2,1,0:T(8,128)(2,1)S(1)} %pad_maximum_fusion.2), channel_id=1, source_target_pairs={{1,2},{2,1},{3,4},{4,3},{5,6},{6,5},{7,8},{8,7},{9,10},{10,9},{11,... | collective-permute-start | bytes 2359304 | tf_op jit(solution)/shard_map/ppermute | solution.py:30
  11.1 39.2 %collective-permute-start.1 = (bf16[46,128,128]{2,1,0:T(8,128)(2,1)S(1)}, bf16[46,128,128]{2,1,0:T(8,128)(2,1)S(1)}, u32[]{:S(2)}, u32[]{:S(2)}) collective-permute-start(bf16[46,128,128]{2,1,0:T(8,128)(2,1)S(1)} %pad_maximum_fusion), channel_id=1, source_target_pairs={{1,2},{2,1},{3,4},{4,3},{5,6},{6,5},{7,8},{8,7},{9,10},{10,9},{11,... | collective-permute-start | bytes 4521992 | tf_op jit(solution)/shard_map/ppermute | solution.py:30
  12.1 38.3 %collective-permute-start.2 = (bf16[30,128,128]{2,1,0:T(8,128)(2,1)S(1)}, bf16[30,128,128]{2,1,0:T(8,128)(2,1)S(1)}, u32[]{:S(2)}, u32[]{:S(2)}) collective-permute-start(bf16[30,128,128]{2,1,0:T(8,128)(2,1)S(1)} %pad_maximum_fusion.1), channel_id=1, source_target_pairs={{1,4},{3,6},{4,1},{5,8},{6,3},{7,10},{8,5},{9,12},{10,7},{11,14},{... | collective-permute-start | bytes 2949128 | tf_op jit(solution)/shard_map/ppermute | solution.py:30
  12.8 31.7 %collective-permute-start.6 = (bf16[24,128,128]{2,1,0:T(8,128)(2,1)S(1)}, bf16[24,128,128]{2,1,0:T(8,128)(2,1)S(1)}, u32[]{:S(2)}, u32[]{:S(2)}) collective-permute-start(bf16[24,128,128]{2,1,0:T(8,128)(2,1)S(1)} %collective-permute-done.5.cross), channel_id=1, source_target_pairs={{0,1},{1,0},{2,3},{3,2},{4,5},{5,4},{6,7},{7,6},{8,9},{9,8},{10,11... | collective-permute-start | bytes 2359304 | tf_op jit(solution)/shard_map/ppermute | solution.py:30
  42.4 7.9 %collective-permute-start.3 = (bf16[14,128,128]{2,1,0:T(8,128)(2,1)S(1)}, bf16[14,128,128]{2,1,0:T(8,128)(2,1)S(1)}, u32[]{:S(2)}, u32[]{:S(2)}) collective-permute-start(bf16[14,128,128]{2,1,0:T(8,128)(2,1)S(1)} %pad_maximum_fusion.3), channel_id=1, source_target_pairs={{1,6},{3,8},{5,10},{6,1},{7,12},{8,3},{9,14},{10,5},{11,16},{12,7}... | collective-permute-start | bytes 1376264 | tf_op jit(solution)/shard_map/ppermute | solution.py:30
  43.1 0.7 collective-permute-start.7
  43.8 6.5 %collective-permute-start.4 = (bf16[1,128,128]{2,1,0:T(8,128)(2,1)S(1)}, bf16[1,128,128]{2,1,0:T(8,128)(2,1)S(1)}, u32[]{:S(2)}, u32[]{:S(2)}) collective-permute-start(bf16[1,128,128]{2,1,0:T(8,128)(2,1)S(1)} %get-tuple-element.19), channel_id=1, source_target_pairs={{1,8},{3,10},{5,12},{7,14},{8,1},{9,16},{10,3},{11,18},{12,5},{13,... | collective-permute-start | bytes 98312 | tf_op jit(solution)/shard_map/ppermute | solution.py:30
  58.1 60.9 %collective-permute-start.8 = (bf16[21,128,128]{2,1,0:T(8,128)(2,1)S(1)}, bf16[21,128,128]{2,1,0:T(8,128)(2,1)S(1)}, u32[]{:S(2)}, u32[]{:S(2)}) collective-permute-start(bf16[21,128,128]{2,1,0:T(8,128)(2,1)S(1)} %get-tuple-element.15), channel_id=1, source_target_pairs={{0,1},{1,0},{2,3},{3,2},{4,5},{5,4},{6,7},{7,6},{8,9},{9,8},{10,11... | collective-permute-start | bytes 2064392 | tf_op jit(solution)/shard_map/ppermute | solution.py:30
  95.2 1.7 %collective-permute-start.9 = (f32[2]{0:T(128)S(1)}, f32[2]{0:T(128)S(1)}, u32[]{:S(2)}, u32[]{:S(2)}) collective-permute-start(f32[2]{0:T(128)S(1)} %slice_reduce_fusion), channel_id=1, source_target_pairs={{0,1},{1,0},{2,3},{3,2},{4,5},{5,4},{6,7},{7,6},{8,9},{9,8},{10,11... | collective-permute-start | bytes 32 | tf_op jit(solution)/shard_map/ppermute | solution.py:30
  96.9 4.8 %collective-permute-start.10 = (f32[2]{0:T(128)S(1)}, f32[2]{0:T(128)S(1)}, u32[]{:S(2)}, u32[]{:S(2)}) collective-permute-start(f32[2]{0:T(128)S(1)} %add.24), channel_id=1, source_target_pairs={{0,2},{1,3},{2,0},{3,1},{4,6},{5,7},{6,4},{7,5},{8,10},{9,11},{10,... | collective-permute-start | bytes 32 | tf_op jit(solution)/shard_map/ppermute | solution.py:30
  101.7 3.5 %collective-permute-start.11 = (f32[2]{0:T(128)S(1)}, f32[2]{0:T(128)S(1)}, u32[]{:S(2)}, u32[]{:S(2)}) collective-permute-start(f32[2]{0:T(128)S(1)} %add.25), channel_id=1, source_target_pairs={{0,4},{1,5},{2,6},{3,7},{4,0},{5,1},{6,2},{7,3},{8,12},{9,13},{10,... | collective-permute-start | bytes 32 | tf_op jit(solution)/shard_map/ppermute | solution.py:30
  105.2 4.4 %collective-permute-start.12 = (f32[2]{0:T(128)S(1)}, f32[2]{0:T(128)S(1)}, u32[]{:S(2)}, u32[]{:S(2)}) collective-permute-start(f32[2]{0:T(128)S(1)} %add.26), channel_id=1, source_target_pairs={{0,8},{1,9},{2,10},{3,11},{4,12},{5,13},{6,14},{7,15},{8,0},{9,1},... | collective-permute-start | bytes 32 | tf_op jit(solution)/shard_map/ppermute | solution.py:30
  109.7 8.8 %collective-permute-start.13 = (f32[2]{0:T(128)S(1)}, f32[2]{0:T(128)S(1)}, u32[]{:S(2)}, u32[]{:S(2)}) collective-permute-start(f32[2]{0:T(128)S(1)} %add.27), channel_id=1, source_target_pairs={{0,16},{1,17},{2,18},{3,19},{4,20},{5,21},{6,22},{7,23},{8,24},{9,... | collective-permute-start | bytes 32 | tf_op jit(solution)/shard_map/ppermute | solution.py:30

commit v2 on v1

v2 whole, which is shorter than its diff:
```python
import jax
import jax.numpy as jnp
from jax import lax
from jax.experimental import pallas as pl
from jax.experimental.pallas import tpu as pltpu
from jax.sharding import PartitionSpec as P

AXES = ("row", "col")
HALF = 13
BAND = 2 * HALF + 1
BS = 128
NEAR = HALF
FAR = 12
NCOL = NEAR + 1
NEAR_W, OWN_W, FAR_W = NCOL * BS, 4 * BS, FAR * BS
OWN_AT, FAR_AT = NEAR_W, NEAR_W + OWN_W
VMEM_LIMIT = 26 * 1024 * 1024

VM = pl.BlockSpec(memory_space=pltpu.VMEM)
SM = pl.BlockSpec(memory_space=pltpu.SMEM)
HB = pl.BlockSpec(memory_space=pl.ANY)


def params():
    return pltpu.CompilerParams(vmem_limit_bytes=VMEM_LIMIT)


def permute(value, target):
    devices = lax.axis_size(AXES)
    pairs = [(i, target(i)) for i in range(devices)]
    return lax.ppermute(value, AXES, [(i, j) for i, j in pairs if 0 <= j < devices])


def to_partner(value):
    return permute(value, lambda i: i ^ 1)


def to_side(value, distance, senders=lambda i: True):
    def target(i):
        chip, core = divmod(i, 2)
        if not senders(i):
            return -1
        return 2 * (chip + distance) if core else 2 * (chip - distance) + 1

    return permute(value, target)


def inner(i):
    return (i // 2 + i % 2) % 2 == 1


def add_over(value, *bits):
    first = bits[0]
    half = value + permute(value, lambda i: i ^ first)
    if len(bits) == 1:
        return half
    second = bits[1]
    other = permute(value, lambda i: i ^ second) + permute(value, lambda i: i ^ first ^ second)
    return half + other


def nn(a, b):
    return lax.dot_general(a, b, (((1,), (0,)), ((), ())), preferred_element_type=jnp.float32)


def nt(a, b):
    return lax.dot_general(a, b, (((1,), (1,)), ((), ())), preferred_element_type=jnp.float32)


def cut(i, n=1):
    return slice(i * BS, (i + n) * BS)


def own_kernel(meta, blocks, mine, other, mask):
    core = meta[2, 0]
    first_row = meta[2, 1]
    for r in range(2):
        for w in range(BAND):
            mask[r, w] = 0
    for r in range(2):

        @pl.loop(0, meta[2, 3 + r])
        def _(n):
            mask[r, meta[r, n] - first_row - r + HALF] = 1

    for r in range(2):
        e = jnp.where(core > 0, 1 - r, r)
        for a in range(BAND):
            x = jnp.where(mask[r, a] > 0, blocks[r, a], jnp.zeros((BS, BS), blocks.dtype))
            w = jnp.where(core > 0, BAND - 1 - a, a)
            mine[e, w] = x
            other[1 - e, BAND - 1 - w] = x


def own_rows(meta, blocks):
    shape = jax.ShapeDtypeStruct(blocks.shape, blocks.dtype)
    return pl.pallas_call(
        own_kernel,
        out_shape=(shape, shape, jax.ShapeDtypeStruct((2, BAND), jnp.int32)),
        in_specs=[SM, VM],
        out_specs=(VM, VM, SM),
        compiler_params=params(),
        name="own_rows",
    )(meta, blocks)


def low_slots(e):
    return [w for w in range(HALF, BAND - 1 - e) if e < 2 or not 5 <= w - HALF + 1 + e <= 8]


def first_kernel(mine, part, x1, z1, z2, direct):
    def put(out, at, e, slots):
        for w in slots:
            out[at] = mine[e, w] if e < 2 else part[e - 2, w]
            at += 1
        return at

    at1 = at2 = at3 = at4 = 0
    for e in range(4):
        at1 = put(x1, at1, e, range(9 - e))
        at2 = put(z1, at2, e, range(5 - e))
        at3 = put(z2, at3, e, range(HALF, BAND - 5 - e))
        at4 = put(direct, at4, 3 - e, range(HALF, HALF - 5 + e, -1))
    for e in range(4):
        at1 = put(x1, at1, e, low_slots(e))
        at2 = put(z1, at2, e, range(HALF, BAND - 1 - e))
    for e in range(4):
        at2 = put(z1, at2, e, range(HALF - 2 - e, HALF - e))
        at3 = put(z2, at3, e, range(HALF - 2 - e, HALF - e))


def first_packs(mine, part):
    return pl.pallas_call(
        first_kernel,
        out_shape=[jax.ShapeDtypeStruct((n, BS, BS), mine.dtype) for n in (68, 68, 38, 14)],
        in_specs=[VM] * 2,
        out_specs=[VM] * 4,
        compiler_params=params(),
        name="first_packs",
    )(mine, part)


def second_kernel(meta, x1, z1, corner, direct, _d4, _sums, cross, x2, d3):
    facing = meta[2, 2] > 0
    for n in range(30):
        cross[n] = x1[n]
    for n in range(14):
        cross[30 + n] = z1[n]
    cross[44] = corner[0]
    at, start = 0, 14
    for e in range(4):
        for w in low_slots(e):
            x2[at] = z1[start + w - HALF]
            at += 1
        start += 13 - e
    at, start = 0, 14
    for e in range(4):
        for n in range(5 - e):
            d3[at] = jnp.where(facing, z1[start + n], direct[at])
            at += 1
        start += 13 - e


def second_packs(meta, x1, z1, corner, direct, d4, sums):
    return pl.pallas_call(
        second_kernel,
        out_shape=[jax.ShapeDtypeStruct((n, BS, BS), x1.dtype) for n in (45, 38, 14)],
        in_specs=[SM] + [VM] * 6,
        out_specs=[VM] * 3,
        compiler_params=params(),
        name="second_packs",
    )(meta, x1, z1, corner, direct, d4, sums)


def turned(x):
    return jnp.transpose(x.astype(jnp.float32)).astype(x.dtype)


def fill_rows(mine, part, rows):
    zero = jnp.zeros((BS, BS), rows.dtype)

    def block(e, k):
        w = k - e + HALF
        if not 0 <= w < BAND:
            return zero
        return mine[e, w] if e < 2 else part[e - 2, w]

    for e in range(4):
        for t in range(1, NCOL + 1):
            rows[cut(e), cut(t - 1)] = block(e, -t)
        for k in range(4):
            rows[cut(e), OWN_AT + k * BS : OWN_AT + (k + 1) * BS] = block(e, k)
        for u in range(1, FAR + 1):
            rows[cut(e), FAR_AT + (u - 1) * BS : FAR_AT + u * BS] = block(e, 3 + u)


def near_start(t):
    first = 4 * ((t - 1) // 4) + 1
    return sum(14 - s for s in range(first, t))


def cross_start(t):
    return sum(10 - s for s in range(1, t))


def own_kernel_products(mine, part, own_sum, inner, near_rows, far_rows, sums, rows):
    fill_rows(mine, part, rows)
    near_rows[...] = rows[:, :NEAR_W]
    far_rows[...] = rows[:, FAR_AT : FAR_AT + 10 * BS]
    own = rows[:, OWN_AT:FAR_AT]
    third = jnp.zeros((1, 1), jnp.float32)
    for c in range(NCOL // 2):
        near = rows[:, cut(2 * c, 2)]
        value = nn(own, near)
        own_sum[:, cut(2 * c, 2)] = value
        third += jnp.sum(near.astype(jnp.float32) * value, keepdims=True)
    third = 3.0 * third
    top = rows[: 2 * BS, OWN_AT:FAR_AT]
    third += jnp.sum(top.astype(jnp.float32) * nn(top, own), keepdims=True)
    inner[...] = nt(rows[: 2 * BS, :], rows[...])
    second = jnp.zeros((1, 1), jnp.float32)
    for e in range(2):
        for w in range(BAND):
            x = mine[e, w].astype(jnp.float32)
            second += jnp.sum(x * x, keepdims=True)
    sums[0:1, :] = jnp.broadcast_to(second, (1, BS))
    sums[1:2, :] = jnp.broadcast_to(third, (1, BS))


def own_part(mine, part):
    return pl.pallas_call(
        own_kernel_products,
        out_shape=(
            jax.ShapeDtypeStruct((4 * BS, NEAR_W), jnp.float32),
            jax.ShapeDtypeStruct((2 * BS, OWN_W), jnp.float32),
            jax.ShapeDtypeStruct((4 * BS, NEAR_W), mine.dtype),
            jax.ShapeDtypeStruct((4 * BS, 10 * BS), mine.dtype),
            jax.ShapeDtypeStruct((2, BS), jnp.float32),
        ),
        in_specs=[VM] * 2,
        out_specs=(VM,) * 5,
        scratch_shapes=[pltpu.VMEM((4 * BS, FAR_AT + FAR_W), mine.dtype)],
        compiler_params=params(),
        cost_estimate=pl.CostEstimate(flops=2 * 10**9, bytes_accessed=10**6, transcendentals=0),
        name="own_part",
    )(mine, part)


def fill_cross(block, pairs):
    for c in range(5):
        for g in range(5 - c):
            for n in (2 * c + 1, 2 * c + 2):
                for m in (2 * g + 1, 2 * g + 2):
                    x = block(n, m) if n + m <= 10 else jnp.zeros((BS, BS), pairs.dtype)
                    pairs[cut(n - 1), cut(m - 1)] = x


def cross_kernel(near_rows, far_rows, own_sum, before, x1, z1, corner, first, sums, pairs):
    def block(t, u):
        at = cross_start(t) + 10 - t - u
        return x1[at] if t < 5 else z1[at - 30] if t < 9 else corner[0]

    fill_cross(block, pairs)
    third = jnp.zeros((1, 1), jnp.float32)
    for c in range(NCOL // 2):
        at = cut(2 * c, 2)
        if c < 5:
            width = (10 - 2 * c) * BS
            value = nt(far_rows[:, :width], pairs[at, :width])
            first[:, at] = own_sum[:, at] + value
            third += jnp.sum(near_rows[:, at].astype(jnp.float32) * value, keepdims=True)
        else:
            first[:, at] = own_sum[:, at]
    sums[0:1, :] = before[0:1, :]
    sums[1:2, :] = before[1:2, :] + 6.0 * third


def cross_part(near_rows, far_rows, own_sum, before, x1, z1, corner):
    return pl.pallas_call(
        cross_kernel,
        out_shape=(
            jax.ShapeDtypeStruct(own_sum.shape, jnp.float32),
            jax.ShapeDtypeStruct(before.shape, jnp.float32),
        ),
        in_specs=[VM] * 7,
        out_specs=(VM,) * 2,
        scratch_shapes=[pltpu.VMEM((10 * BS, 10 * BS), x1.dtype)],
        compiler_params=params(),
        cost_estimate=pl.CostEstimate(flops=10**9, bytes_accessed=10**6, transcendentals=0),
        name="cross_part",
    )(near_rows, far_rows, own_sum, before, x1, z1, corner)


LOW = 5


def mid_kernel(
    meta, near_rows, far_rows, before, swapped, z1, z2, d3, d4, partial, pairs, cross
):
    facing = meta[2, 2] > 0
    zero = jnp.zeros((BS, BS), pairs.dtype)
    fill_cross(lambda u, t: swapped[cross_start(u) + 10 - t - u], cross)

    def block(t, s):
        if s > NEAR:
            return zero
        if t == NEAR:
            return d4[0]
        if t > 8:
            return d3[near_start(t) + s - t]
        start = 14 + sum(13 - n for n in range(t - LOW))
        return jnp.where(facing, z1[start + s - t], z2[near_start(t) + s - t])

    for t in range(LOW, NCOL + 1):
        for s in range(t, NCOL + 1):
            pairs[cut(t - LOW), cut(s - LOW)] = block(t, s)
        if t % 2 == 0:
            pairs[cut(t - LOW), cut(t - 1 - LOW)] = turned(block(t - 1, t))
    low = (LOW - 1) * BS
    for c in range(NCOL // 2):
        at = 2 * c * BS
        value = before[:, at : at + 2 * BS]
        if c < 5:
            width = (10 - 2 * c) * BS
            value += nn(far_rows[:, :width], cross[:width, at : at + 2 * BS])
        if at >= low:
            value += nt(near_rows[:, at:], pairs[at - low : at - low + 2 * BS, at - low :])
        if at > low:
            value += nn(near_rows[:, low:at], pairs[: at - low, at - low : at - low + 2 * BS])
        partial[:, at : at + 2 * BS] = value


def mid_part(meta, near_rows, far_rows, before, swapped, z1, z2, d3, d4):
    return pl.pallas_call(
        mid_kernel,
        out_shape=jax.ShapeDtypeStruct(before.shape, before.dtype),
        in_specs=[SM] + [VM] * 8,
        out_specs=VM,
        scratch_shapes=[
            pltpu.VMEM((10 * BS, 10 * BS), near_rows.dtype),
            pltpu.VMEM((10 * BS, 10 * BS), near_rows.dtype),
        ],
        compiler_params=params(),
        cost_estimate=pl.CostEstimate(flops=3 * 10**9, bytes_accessed=10**6, transcendentals=0),
        name="mid_part",
    )(meta, near_rows, far_rows, before, swapped, z1, z2, d3, d4)


def fill_near(facing, x1, x2, z1, z2, pairs):
    def block(t, s):
        if t > 2 and 5 <= s <= 8:
            at = 2 * (s - LOW) + t - 3
            return turned(jnp.where(facing, z1[60 + at], z2[30 + at]))
        slots = low_slots(t - 1)
        at = sum(len(low_slots(n)) for n in range(t - 1)) + slots.index(HALF + s - t)
        return jnp.where(facing, x1[30 + at], x2[at])

    for t in range(1, 5):
        for s in range(1, NCOL + 1):
            if s > NEAR:
                x = jnp.zeros((BS, BS), pairs.dtype)
            else:
                x = turned(block(s, t)) if s < t else block(t, s)
            pairs[cut(t - 1), cut(s - 1)] = x


def near_products(half, near_rows, partial, pairs):
    rows = slice(2 * half * BS, (2 * half + 2) * BS)
    for c in range(NCOL // 2):
        value = partial[rows, cut(2 * c, 2)]
        if c < 2:
            value += nt(near_rows[rows, :], pairs[cut(2 * c, 2), :])
        else:
            value += nn(near_rows[rows, : 4 * BS], pairs[:, cut(2 * c, 2)])
        for n in range(2):
            t = 2 * c + 1 + n
            for e in range(2):
                if 2 * half + e + t <= HALF:
                    yield e, t, value[cut(e), cut(n)]


def away_kernel(meta, near_rows, partial, x1, x2, z1, z2, away, pairs):
    fill_near(meta[2, 2] > 0, x1, x2, z1, z2, pairs)
    for e, t, value in near_products(1, near_rows, partial, pairs):
        away[e * 11 + t - 1] = value.astype(away.dtype)


def away_part(meta, near_rows, partial, x1, x2, z1, z2):
    return pl.pallas_call(
        away_kernel,
        out_shape=jax.ShapeDtypeStruct((21, BS, BS), x1.dtype),
        in_specs=[SM] + [VM] * 6,
        out_specs=VM,
        scratch_shapes=[pltpu.VMEM((4 * BS, NEAR_W), x1.dtype)],
        compiler_params=params(),
        cost_estimate=pl.CostEstimate(flops=10**9, bytes_accessed=10**6, transcendentals=0),
        name="away_part",
    )(meta, near_rows, partial, x1, x2, z1, z2)


def near_kernel(meta, mask, near_rows, partial, inner, x1, x2, z1, z2, out, pairs):
    core = meta[2, 0]
    fill_near(meta[2, 2] > 0, x1, x2, z1, z2, pairs)

    def put(e, w, value):
        r = jnp.where(core > 0, 1 - e, e)
        a = jnp.where(core > 0, BAND - 1 - w, w)
        out[r, a] = jnp.where(mask[r, a] > 0, value, 0.0).astype(out.dtype)

    for e in range(2):
        for k in range(4):
            put(e, k - e + HALF, inner[cut(e), cut(k)])
    for e, t, value in near_products(0, near_rows, partial, pairs):
        put(e, HALF - e - t, value)


def near_part(meta, mask, near_rows, partial, inner, x1, x2, z1, z2):
    return pl.pallas_call(
        near_kernel,
        out_shape=jax.ShapeDtypeStruct((2, BAND, BS, BS), x1.dtype),
        in_specs=[SM] * 2 + [VM] * 7,
        out_specs=VM,
        scratch_shapes=[pltpu.VMEM((4 * BS, NEAR_W), x1.dtype)],
        compiler_params=params(),
        cost_estimate=pl.CostEstimate(flops=10**9, bytes_accessed=10**6, transcendentals=0),
        name="near_part",
    )(meta, mask, near_rows, partial, inner, x1, x2, z1, z2)


def join_kernel(meta, mask, came, _, out, held, sems):
    core = meta[2, 0]
    copies = []
    for e, count, base in ((0, 10, 11), (1, 11, 0)):
        r = jnp.where(core > 0, 1 - e, e)

        @pl.loop(0, count)
        def _(n):
            w = BAND - count + n
            a = jnp.where(core > 0, BAND - 1 - w, w)
            spot = jnp.where(core > 0, count - 1 - n, n)
            keep = mask[r, a]
            x = came[base + n]
            held[base + spot] = jnp.where(keep > 0, x, jnp.zeros_like(x))

        start = jnp.where(core > 0, 0, BAND - count)
        copy = pltpu.make_async_copy(
            held.at[pl.ds(base, count)], out.at[r, pl.ds(start, count)], sems.at[e]
        )
        copy.start()
        copies.append(copy)
    for copy in copies:
        copy.wait()


def join(meta, mask, came, out):
    anywhere = pl.BlockSpec(memory_space=pl.ANY)
    return pl.pallas_call(
        join_kernel,
        out_shape=jax.ShapeDtypeStruct(out.shape, out.dtype),
        in_specs=[SM, SM, VM, anywhere],
        out_specs=anywhere,
        scratch_shapes=[
            pltpu.VMEM(came.shape, came.dtype),
            pltpu.SemaphoreType.DMA((2,)),
        ],
        input_output_aliases={3: 0},
        compiler_params=params(),
        name="join",
    )(meta, mask, came, out)


def body(blocks, columns, counts):
    index = lax.axis_index(AXES)
    core, chip = index % 2, index // 2
    facing = (core + chip) % 2
    place = lax.broadcasted_iota(jnp.int32, (3, BAND), 1)
    scalars = jnp.where(place == 0, core, jnp.where(place == 1, index * 2, facing))
    table = jnp.pad(columns, ((0, 1), (0, 0))) + jnp.pad(counts[None], ((2, 0), (3, BAND - 5)))
    last = lax.broadcasted_iota(jnp.int32, (3, BAND), 0) == 2
    meta = jnp.where(last & (place < 3), scalars, table).astype(jnp.int32)
    mine, other, mask = own_rows(meta, blocks)
    part = to_partner(other)

    def outer(i):
        return not inner(i)

    x1, z1, z2, direct = first_packs(mine, part)
    x1 = to_side(x1, 1, inner)
    z1 = to_side(z1, 2, outer)
    corner = to_side(mine[0, :1], 3, inner)
    d4 = to_side(mine[0, HALF : HALF + 1], 4)
    z2 = to_side(z2, 2, inner)

    own_sum, inside, near_rows, far_rows, sums = own_part(mine, part)

    cross, x2, d3 = second_packs(meta, x1, z1, corner, direct, d4, sums)
    swapped = permute(cross, lambda i: i ^ 1 if inner(i) else -1)

    def across(i):
        chip, core = divmod(i, 2)
        return 2 * (chip + (1 if core else -1)) + core if inner(i) else -1

    x2 = permute(x2, across)

    def along(i):
        chip, core = divmod(i, 2)
        step = 1 if inner(i) else 3
        return 2 * (chip + (-step if core else step)) + core

    d3 = permute(d3, along)

    devices = lax.axis_size(AXES)
    first, sums = cross_part(near_rows, far_rows, own_sum, sums, x1, z1, corner)
    sums = sums[:, 0]
    steps = [1 << n for n in range(devices.bit_length() - 1)]
    steps = steps[:1] + steps[-1:] + steps[1:-1]
    for step in steps[:2] + steps[4:] + steps[2:3]:
        sums = add_over(sums, step)
    first, sums = lax.optimization_barrier((first, sums))
    partial = mid_part(meta, near_rows, far_rows, first, swapped, z1, z2, d3, d4)
    traces = add_over(sums, steps[3]) / (2 * BS * devices)
    away = away_part(meta, near_rows, partial, x1, x2, z1, z2)
    came = to_partner(away)
    out = near_part(meta, mask, near_rows, partial, inside, x1, x2, z1, z2)
    square = join(meta, mask, came, out)
    return square, traces


def solution(mesh):
    return jax.shard_map(
        body,
        mesh=mesh,
        in_specs=(P(AXES, None, None, None), P(AXES, None), P(AXES)),
        out_specs=(P(AXES, None, None, None), P()),
        check_vma=False,
    )
```

time: 121 us -> 97.3 us (0.80)
  starting transfers between devices: 84.3 us -> 49.4 us
  waiting for transfers between devices: 13.4 us -> 25.4 us
  local copies, waits for them, and re-layouts: 3.21 us -> 1.6 us
    ppermute x14 -> x15, starting transfers between devices: 84.3 us -> 49.4 us  [permute(): lax.ppermute(value, AXES, [(i, j) for i, j in pairs if 0 <= j < devices])]
    ppermute x14 -> x15, waiting for transfers between devices: 13.4 us -> 25.4 us  [permute(): lax.ppermute(value, AXES, [(i, j) for i, j in pairs if 0 <= j < devices])]
    unnamed x8 -> x2, local copies, waits for them, and re-layouts: 2.81 us -> 1.48 us
    pallas_call x2 -> x7, Pallas kernels: 13.5 us -> 14.6 us  [the longest x1 3.8 us: mid_part(): pl.pallas_call(mid_kernel, out_shape=jax.ShapeDtypeStruct(before.shape, b...]
  transfers between devices with their start and end apart: 14 -> 15, of which waited for: 6 -> 6; matrix products, arithmetic and copies ran while one was open for 1% -> 1% of each run, Pallas kernels for 5% -> 12%
where the time goes in v2:
time: 97.3 us; the launch traced here: 97 us
  starting transfers between devices  49.4 us (51%)
  waiting for transfers between devices  25.4 us (26%)
  Pallas kernels  18.2 us (19%)
  local copies, waits for them, and re-layouts  1.6 us (2%)
  other arithmetic  1.32 us (1%)
  between operations  1.04 us (1%)
    ppermute x15, starting transfers between devices, permute(): lax.ppermute(value, AXES, [(i, j) for i, j in pairs if 0 <= j < devices])  49.4 us
    ppermute x15, waiting for transfers between devices, permute(): lax.ppermute(value, AXES, [(i, j) for i, j in pairs if 0 <= j < devices])  25.4 us
    pallas_call x1, Pallas kernels, mid_part(): pl.pallas_call(mid_kernel, out_shape=jax.ShapeDtypeStruct(before.shape, b...  3.8 us
    pallas_call x1, Pallas kernels, near_part(): pl.pallas_call(near_kernel, out_shape=jax.ShapeDtypeStruct((2, BAND, BS,...  3.05 us
    pallas_call x1, Pallas kernels, own_part(): pl.pallas_call(own_kernel_products, out_shape=(jax.ShapeDtypeStruct((4 *...  2.93 us
  transfers between devices with their start and end apart: 15, of which 6 were waited for; matrix products, arithmetic and copies ran while one was open for 1% of the time, Pallas kernels for 12%

profile of v2, /device:TPU:0, one launch (start us, length us, event | category | flops | bytes accessed | tf_op | source)
XLA Modules:
  0.0 97.0 jit_solution(3449009415709800297)
XLA Ops:
  0.7 0.8 add_select_fusion.meta
  1.5 1.5 %copy-done = bf16[2,27,128,128]{3,2,1,0:T(8,128)(2,1)S(1)} copy-done((bf16[2,27,128,128]{3,2,1,0:T(8,128)(2,1)S(1)}, bf16[2,27,128,128]{3,2,1,0:T(8,128)(2,1)}, u32[]{:S(2)}) %copy-start) | copy-done | bytes 1769496
  3.0 1.9 %own_rows.1 = (bf16[2,27,128,128]{3,2,1,0:T(8,128)(2,1)S(1)}, bf16[2,27,128,128]{3,2,1,0:T(8,128)(2,1)S(1)}, s32[2,27]{1,0:T(2,128)S(1)}) custom-call(s32[3,27]{1,0:T(4,128)S(1)} %add_select_fusion.meta, bf16[2,27,128,128]{3,2,1,0:T(8,128)(2,1)S(1)} %copy-done), custom_call_target="tpu_custom_call" | custom-call | tf_op jit(solution)/shard_map/own_rows/pallas_call | solution.py:97
  4.9 0.5 collective-permute-start
  5.5 3.3 %collective-permute-done.part = bf16[2,27,128,128]{3,2,1,0:T(8,128)(2,1)S(1)} collective-permute-done((bf16[2,27,128,128]{3,2,1,0:T(8,128)(2,1)S(1)}, bf16[2,27,128,128]{3,2,1,0:T(8,128)(2,1)S(1)}, u32[]{:S(2)}, u32[]{:S(2)}) %collective-permute-start) | collective-permute-done | bytes 1769504 | tf_op jit(solution)/shard_map/ppermute | solution.py:31
  8.8 0.7 first_packs.1
  9.4 0.8 collective-permute-start.1
  10.2 0.8 collective-permute-start.2
  11.1 0.7 collective-permute-start.8
  11.7 0.7 collective-permute-start.3
  12.4 2.9 %own_part.1 = (f32[512,1792]{1,0:T(8,128)S(1)}, f32[256,512]{1,0:T(8,128)S(1)}, bf16[512,1792]{1,0:T(8,128)(2,1)S(1)}, bf16[512,1280]{1,0:T(8,128)(2,1)S(1)}, f32[2,128]{1,0:T(2,128)S(1)}) custom-call(bf16[2,27,128,128]{3,2,1,0:T(8,128)(2,1)S(1)} %get-tuple-element.22.mine, bf16[2,27,128,128]{3,2,1,0:T(8,128)(2,1)S(1)} %collective-permute-done.part), custom_call_target="tpu_custom_call" | custom-call | flops 2000000000 | bytes 1000000 | tf_op jit(solution)/shard_map/own_part/pallas_call | solution.py:231
  15.4 0.0 collective-permute-done.3.corner
  15.4 0.9 second_packs.1
  16.3 1.3 %collective-permute-start.9 = (bf16[45,128,128]{2,1,0:T(8,128)(2,1)S(1)}, bf16[45,128,128]{2,1,0:T(8,128)(2,1)S(1)}, u32[]{:S(2)}, u32[]{:S(2)}) collective-permute-start(bf16[45,128,128]{2,1,0:T(8,128)(2,1)S(1)} %get-tuple-element.34), channel_id=1, source_target_pairs={{1,0},{2,3},{5,4},{6,7},{9,8},{10,11},{13,12},{14,15},{17,16},{18,... | collective-permute-start | bytes 4423688 | tf_op jit(solution)/shard_map/ppermute | solution.py:31
  17.6 0.7 collective-permute-start.10
  18.3 1.3 %collective-permute-start.12 = (bf16[38,128,128]{2,1,0:T(8,128)(2,1)S(1)}, bf16[38,128,128]{2,1,0:T(8,128)(2,1)S(1)}, u32[]{:S(2)}, u32[]{:S(2)}) collective-permute-start(bf16[38,128,128]{2,1,0:T(8,128)(2,1)S(1)} %get-tuple-element.37), channel_id=1, source_target_pairs={{1,3},{2,0},{5,7},{6,4},{9,11},{10,8},{13,15},{14,12},{17,19},{18,... | collective-permute-start | bytes 3735560 | tf_op jit(solution)/shard_map/ppermute | solution.py:31
  19.6 36.7 %collective-permute-start.11 = (bf16[14,128,128]{2,1,0:T(8,128)(2,1)S(1)}, bf16[14,128,128]{2,1,0:T(8,128)(2,1)S(1)}, u32[]{:S(2)}, u32[]{:S(2)}) collective-permute-start(bf16[14,128,128]{2,1,0:T(8,128)(2,1)S(1)} %get-tuple-element.36), channel_id=1, source_target_pairs={{0,6},{2,4},{4,10},{5,3},{6,8},{7,1},{8,14},{9,7},{10,12},{11,5},{... | collective-permute-start | bytes 1376264 | tf_op jit(solution)/shard_map/ppermute | solution.py:31
  56.3 1.5 %cross_part.1 = (f32[512,1792]{1,0:T(8,128)S(1)}, f32[2,128]{1,0:T(2,128)S(1)}) custom-call(bf16[512,1792]{1,0:T(8,128)(2,1)S(1)} %get-tuple-element.24.near_rows, bf16[512,1280]{1,0:T(8,128)(2,1)S(1)} %get-tuple-element.25.far_rows, f32[512,1792]{1,0:T(8,128)S(1)} %get-tuple-element.26.own_sum, f32[2,128]{1,0:T(2,128)S(1)} %get-tuple-element.27.before._sums, ...), custom_call_target="tpu_custom_call" | custom-call | flops 1000000000 | bytes 1000000 | tf_op jit(solution)/shard_map/cross_part/pallas_call | solution.py:279
  57.8 0.1 slice_reduce_fusion
  57.9 0.1 collective-permute-start.4
  58.0 1.1 %collective-permute-done.4 = f32[2]{0:T(128)S(1)} collective-permute-done((f32[2]{0:T(128)S(1)}, f32[2]{0:T(128)S(1)}, u32[]{:S(2)}, u32[]{:S(2)}) %collective-permute-start.4) | collective-permute-done | bytes 40 | tf_op jit(solution)/shard_map/ppermute | solution.py:31
  59.1 3.5 %collective-permute-done.5 = f32[2]{0:T(128)S(1)} collective-permute-done((f32[2]{0:T(128)S(1)}, f32[2]{0:T(128)S(1)}, u32[]{:S(2)}, u32[]{:S(2)}) %collective-permute-start.5) | collective-permute-done | bytes 40 | tf_op jit(solution)/shard_map/ppermute | solution.py:31
  62.7 3.3 %collective-permute-start.6 = (f32[2]{0:T(128)S(1)}, f32[2]{0:T(128)S(1)}, u32[]{:S(2)}, u32[]{:S(2)}) collective-permute-start(f32[2]{0:T(128)S(1)} %add.42), channel_id=1, source_target_pairs={{0,8},{1,9},{2,10},{3,11},{4,12},{5,13},{6,14},{7,15},{8,0},{9,1},... | collective-permute-start | bytes 32 | tf_op jit(solution)/shard_map/ppermute | solution.py:31
  66.0 10.3 %collective-permute-done.6 = f32[2]{0:T(128)S(1)} collective-permute-done((f32[2]{0:T(128)S(1)}, f32[2]{0:T(128)S(1)}, u32[]{:S(2)}, u32[]{:S(2)}) %collective-permute-start.6) | collective-permute-done | bytes 40 | tf_op jit(solution)/shard_map/ppermute | solution.py:31
  76.3 3.5 %collective-permute-done.7 = f32[2]{0:T(128)S(1)} collective-permute-done((f32[2]{0:T(128)S(1)}, f32[2]{0:T(128)S(1)}, u32[]{:S(2)}, u32[]{:S(2)}) %collective-permute-start.7) | collective-permute-done | bytes 40 | tf_op jit(solution)/shard_map/ppermute | solution.py:31
  79.9 3.8 %mid_part.1.partial = f32[512,1792]{1,0:T(8,128)S(1)} custom-call(s32[3,27]{1,0:T(4,128)S(1)} %add_select_fusion.meta, bf16[512,1792]{1,0:T(8,128)(2,1)S(1)} %get-tuple-element.24.near_rows, bf16[512,1280]{1,0:T(8,128)(2,1)S(1)} %get-tuple-element.25.far_rows, f32[512,1792]{1,0:T(8,128)S(1)} %get-tuple-element.32.before, ...), custom_call_target="tpu_custom_call" | custom-call | flops 3000000000 | bytes 1000000 | tf_op jit(solution)/shard_map/mid_part/pallas_call | solution.py:334
  83.7 1.8 %away_part.1 = bf16[21,128,128]{2,1,0:T(8,128)(2,1)S(1)} custom-call(s32[3,27]{1,0:T(4,128)S(1)} %add_select_fusion.meta, bf16[512,1792]{1,0:T(8,128)(2,1)S(1)} %get-tuple-element.24.near_rows, f32[512,1792]{1,0:T(8,128)S(1)} %mid_part.1.partial, bf16[68,128,128]{2,1,0:T(8,128)(2,1)S(1)} %collective-permute-done.1.x1, ...), custom_call_target="tpu_custom_call" | custom-call | flops 1000000000 | bytes 1000000 | tf_op jit(solution)/shard_map/away_part/pallas_call | solution.py:389
  85.5 2.5 %collective-permute-start.13 = (bf16[21,128,128]{2,1,0:T(8,128)(2,1)S(1)}, bf16[21,128,128]{2,1,0:T(8,128)(2,1)S(1)}, u32[]{:S(2)}, u32[]{:S(2)}) collective-permute-start(bf16[21,128,128]{2,1,0:T(8,128)(2,1)S(1)} %away_part.1), channel_id=1, source_target_pairs={{0,1},{1,0},{2,3},{3,2},{4,5},{5,4},{6,7},{7,6},{8,9},{9,8},{10,11... | collective-permute-start | bytes 2064392 | tf_op jit(solution)/shard_map/ppermute | solution.py:31
  88.0 3.5 %collective-permute-done.14 = f32[2]{0:T(128)S(1)} collective-permute-done((f32[2]{0:T(128)S(1)}, f32[2]{0:T(128)S(1)}, u32[]{:S(2)}, u32[]{:S(2)}) %collective-permute-start.14) | collective-permute-done | bytes 40 | tf_op jit(solution)/shard_map/ppermute | solution.py:31
  91.6 0.5 add_multiply_fusion
  92.1 3.1 %near_part.1._ = bf16[2,27,128,128]{3,2,1,0:T(8,128)(2,1)} custom-call(s32[3,27]{1,0:T(4,128)S(1)} %add_select_fusion.meta, s32[2,27]{1,0:T(2,128)S(1)} %get-tuple-element.21.mask, bf16[512,1792]{1,0:T(8,128)(2,1)S(1)} %get-tuple-element.24.near_rows, f32[512,1792]{1,0:T(8,128)S(1)} %mid_part.1.partial, f32[256,512]{1,0:T(8,128)S(1)} %get-tuple-element.38.inner, ...), custom_call_target="tpu_custom_call" | custom-call | flops 1000000000 | bytes 1000000 | tf_op jit(solution)/shard_map/near_part/pallas_call | solution.py:418
  95.2 1.7 %join.1 = bf16[2,27,128,128]{3,2,1,0:T(8,128)(2,1)} custom-call(s32[3,27]{1,0:T(4,128)S(1)} %add_select_fusion.meta, s32[2,27]{1,0:T(2,128)S(1)} %get-tuple-element.21.mask, bf16[21,128,128]{2,1,0:T(8,128)(2,1)S(1)} %collective-permute-done.13.came, bf16[2,27,128,128]{3,2,1,0:T(8,128)(2,1)} %near_part.1._), custom_call_target="tpu_custom_call", output_to_operand_aliasing={{}: (3, {})} | custom-call | tf_op jit(solution)/shard_map/join/pallas_call | solution.py:457
  (20 shorter events, 0.1 us)
Async XLA Ops:
  1.5 1.5 %copy-start = (bf16[2,27,128,128]{3,2,1,0:T(8,128)(2,1)S(1)}, bf16[2,27,128,128]{3,2,1,0:T(8,128)(2,1)}, u32[]{:S(2)}) copy-start(bf16[2,27,128,128]{3,2,1,0:T(8,128)(2,1)} %blocks.1) | copy-start | bytes 5308420
  4.9 3.9 %collective-permute-start = (bf16[2,27,128,128]{3,2,1,0:T(8,128)(2,1)S(1)}, bf16[2,27,128,128]{3,2,1,0:T(8,128)(2,1)S(1)}, u32[]{:S(2)}, u32[]{:S(2)}) collective-permute-start(bf16[2,27,128,128]{3,2,1,0:T(8,128)(2,1)S(1)} %get-tuple-element.23), channel_id=1, source_target_pairs={{0,1},{1,0},{2,3},{3,2},{4,5},{5,4},{6,7},{7,6},{8,9},{9,8},{10,11... | collective-permute-start | bytes 5308424 | tf_op jit(solution)/shard_map/ppermute | solution.py:31
  9.4 5.9 %collective-permute-start.1 = (bf16[68,128,128]{2,1,0:T(8,128)(2,1)S(1)}, bf16[68,128,128]{2,1,0:T(8,128)(2,1)S(1)}, u32[]{:S(2)}, u32[]{:S(2)}) collective-permute-start(bf16[68,128,128]{2,1,0:T(8,128)(2,1)S(1)} %get-tuple-element.28), channel_id=1, source_target_pairs={{1,2},{2,1},{5,6},{6,5},{9,10},{10,9},{13,14},{14,13},{17,18},{18,... | collective-permute-start | bytes 6684680 | tf_op jit(solution)/shard_map/ppermute | solution.py:31
  10.2 5.1 %collective-permute-start.2 = (bf16[68,128,128]{2,1,0:T(8,128)(2,1)S(1)}, bf16[68,128,128]{2,1,0:T(8,128)(2,1)S(1)}, u32[]{:S(2)}, u32[]{:S(2)}) collective-permute-start(bf16[68,128,128]{2,1,0:T(8,128)(2,1)S(1)} %get-tuple-element.29), channel_id=1, source_target_pairs={{3,6},{4,1},{7,10},{8,5},{11,14},{12,9},{15,18},{16,13},{19,22},{2... | collective-permute-start | bytes 6684680 | tf_op jit(solution)/shard_map/ppermute | solution.py:31
  11.1 4.3 %collective-permute-start.8 = (bf16[1,128,128]{2,1,0:T(8,128)(2,1)S(1)}, bf16[1,128,128]{2,1,0:T(8,128)(2,1)S(1)}, u32[]{:S(2)}, u32[]{:S(2)}) collective-permute-start(bf16[1,128,128]{2,1,0:T(8,128)(2,1)S(1)} %get-tuple-element.40), channel_id=1, source_target_pairs={{1,8},{3,10},{5,12},{7,14},{8,1},{9,16},{10,3},{11,18},{12,5},{13,... | collective-permute-start | bytes 98312 | tf_op jit(solution)/shard_map/ppermute | solution.py:31
  11.7 3.6 %collective-permute-start.3 = (bf16[1,128,128]{2,1,0:T(8,128)(2,1)S(1)}, bf16[1,128,128]{2,1,0:T(8,128)(2,1)S(1)}, u32[]{:S(2)}, u32[]{:S(2)}) collective-permute-start(bf16[1,128,128]{2,1,0:T(8,128)(2,1)S(1)} %get-tuple-element.41), channel_id=1, source_target_pairs={{1,6},{5,10},{6,1},{9,14},{10,5},{13,18},{14,9},{17,22},{18,13},{2... | collective-permute-start | bytes 98312 | tf_op jit(solution)/shard_map/ppermute | solution.py:31
  16.3 63.6 %collective-permute-start.9 = (bf16[45,128,128]{2,1,0:T(8,128)(2,1)S(1)}, bf16[45,128,128]{2,1,0:T(8,128)(2,1)S(1)}, u32[]{:S(2)}, u32[]{:S(2)}) collective-permute-start(bf16[45,128,128]{2,1,0:T(8,128)(2,1)S(1)} %get-tuple-element.34), channel_id=1, source_target_pairs={{1,0},{2,3},{5,4},{6,7},{9,8},{10,11},{13,12},{14,15},{17,16},{18,... | collective-permute-start | bytes 4423688 | tf_op jit(solution)/shard_map/ppermute | solution.py:31
  17.6 62.3 %collective-permute-start.10 = (bf16[38,128,128]{2,1,0:T(8,128)(2,1)S(1)}, bf16[38,128,128]{2,1,0:T(8,128)(2,1)S(1)}, u32[]{:S(2)}, u32[]{:S(2)}) collective-permute-start(bf16[38,128,128]{2,1,0:T(8,128)(2,1)S(1)} %get-tuple-element.35), channel_id=1, source_target_pairs={{1,4},{5,8},{6,3},{9,12},{10,7},{13,16},{14,11},{17,20},{18,15},{2... | collective-permute-start | bytes 3735560 | tf_op jit(solution)/shard_map/ppermute | solution.py:31
  18.3 65.4 %collective-permute-start.12 = (bf16[38,128,128]{2,1,0:T(8,128)(2,1)S(1)}, bf16[38,128,128]{2,1,0:T(8,128)(2,1)S(1)}, u32[]{:S(2)}, u32[]{:S(2)}) collective-permute-start(bf16[38,128,128]{2,1,0:T(8,128)(2,1)S(1)} %get-tuple-element.37), channel_id=1, source_target_pairs={{1,3},{2,0},{5,7},{6,4},{9,11},{10,8},{13,15},{14,12},{17,19},{18,... | collective-permute-start | bytes 3735560 | tf_op jit(solution)/shard_map/ppermute | solution.py:31
  19.6 60.3 %collective-permute-start.11 = (bf16[14,128,128]{2,1,0:T(8,128)(2,1)S(1)}, bf16[14,128,128]{2,1,0:T(8,128)(2,1)S(1)}, u32[]{:S(2)}, u32[]{:S(2)}) collective-permute-start(bf16[14,128,128]{2,1,0:T(8,128)(2,1)S(1)} %get-tuple-element.36), channel_id=1, source_target_pairs={{0,6},{2,4},{4,10},{5,3},{6,8},{7,1},{8,14},{9,7},{10,12},{11,5},{... | collective-permute-start | bytes 1376264 | tf_op jit(solution)/shard_map/ppermute | solution.py:31
  57.9 1.2 %collective-permute-start.4 = (f32[2]{0:T(128)S(1)}, f32[2]{0:T(128)S(1)}, u32[]{:S(2)}, u32[]{:S(2)}) collective-permute-start(f32[2]{0:T(128)S(1)} %slice_reduce_fusion), channel_id=1, source_target_pairs={{0,1},{1,0},{2,3},{3,2},{4,5},{5,4},{6,7},{7,6},{8,9},{9,8},{10,11... | collective-permute-start | bytes 32 | tf_op jit(solution)/shard_map/ppermute | solution.py:31
  59.1 3.5 %collective-permute-start.5 = (f32[2]{0:T(128)S(1)}, f32[2]{0:T(128)S(1)}, u32[]{:S(2)}, u32[]{:S(2)}) collective-permute-start(f32[2]{0:T(128)S(1)} %add.41), channel_id=1, source_target_pairs={{0,16},{1,17},{2,18},{3,19},{4,20},{5,21},{6,22},{7,23},{8,24},{9,... | collective-permute-start | bytes 32 | tf_op jit(solution)/shard_map/ppermute | solution.py:31
  62.7 13.7 %collective-permute-start.6 = (f32[2]{0:T(128)S(1)}, f32[2]{0:T(128)S(1)}, u32[]{:S(2)}, u32[]{:S(2)}) collective-permute-start(f32[2]{0:T(128)S(1)} %add.42), channel_id=1, source_target_pairs={{0,8},{1,9},{2,10},{3,11},{4,12},{5,13},{6,14},{7,15},{8,0},{9,1},... | collective-permute-start | bytes 32 | tf_op jit(solution)/shard_map/ppermute | solution.py:31
  76.3 3.5 %collective-permute-start.7 = (f32[2]{0:T(128)S(1)}, f32[2]{0:T(128)S(1)}, u32[]{:S(2)}, u32[]{:S(2)}) collective-permute-start(f32[2]{0:T(128)S(1)} %add.43), channel_id=1, source_target_pairs={{0,2},{1,3},{2,0},{3,1},{4,6},{5,7},{6,4},{7,5},{8,10},{9,11},{10,... | collective-permute-start | bytes 32 | tf_op jit(solution)/shard_map/ppermute | solution.py:31
  85.5 9.7 %collective-permute-start.13 = (bf16[21,128,128]{2,1,0:T(8,128)(2,1)S(1)}, bf16[21,128,128]{2,1,0:T(8,128)(2,1)S(1)}, u32[]{:S(2)}, u32[]{:S(2)}) collective-permute-start(bf16[21,128,128]{2,1,0:T(8,128)(2,1)S(1)} %away_part.1), channel_id=1, source_target_pairs={{0,1},{1,0},{2,3},{3,2},{4,5},{5,4},{6,7},{7,6},{8,9},{9,8},{10,11... | collective-permute-start | bytes 2064392 | tf_op jit(solution)/shard_map/ppermute | solution.py:31
  88.0 3.5 %collective-permute-start.14 = (f32[2]{0:T(128)S(1)}, f32[2]{0:T(128)S(1)}, u32[]{:S(2)}, u32[]{:S(2)}) collective-permute-start(f32[2]{0:T(128)S(1)} %add.44), channel_id=1, source_target_pairs={{0,4},{1,5},{2,6},{3,7},{4,0},{5,1},{6,2},{7,3},{8,12},{9,13},{10,... | collective-permute-start | bytes 32 | tf_op jit(solution)/shard_map/ppermute | solution.py:31

commit v3 on v2

v3 whole, which is shorter than its diff:
```python
import jax
import jax.numpy as jnp
from jax import lax
from jax.experimental import pallas as pl
from jax.experimental.pallas import tpu as pltpu
from jax.sharding import PartitionSpec as P

AXES = ("row", "col")
HALF = 13
BAND = 2 * HALF + 1
BS = 128
NEAR = HALF
FAR = 12
NCOL = NEAR + 1
NEAR_W, OWN_W, FAR_W = NCOL * BS, 4 * BS, FAR * BS
OWN_AT, FAR_AT = NEAR_W, NEAR_W + OWN_W
VMEM_LIMIT = 20 * 1024 * 1024

VM = pl.BlockSpec(memory_space=pltpu.VMEM)
SM = pl.BlockSpec(memory_space=pltpu.SMEM)
HB = pl.BlockSpec(memory_space=pl.ANY)


def params():
    return pltpu.CompilerParams(vmem_limit_bytes=VMEM_LIMIT)


def permute(value, target):
    devices = lax.axis_size(AXES)
    pairs = [(i, target(i)) for i in range(devices)]
    return lax.ppermute(value, AXES, [(i, j) for i, j in pairs if 0 <= j < devices])


def to_partner(value):
    return permute(value, lambda i: i ^ 1)


def to_side(value, distance, senders=lambda i: True):
    def target(i):
        chip, core = divmod(i, 2)
        if not senders(i):
            return -1
        return 2 * (chip + distance) if core else 2 * (chip - distance) + 1

    return permute(value, target)


def inner(i):
    return (i // 2 + i % 2) % 2 == 1


def all_sums(value):
    devices = lax.axis_size(AXES)
    steps = [1 << n for n in range(devices.bit_length() - 1)]
    for step in steps[:1] + steps[4:] + steps[1:4]:
        value = value + permute(value, lambda i: i ^ step)
    return value


def nn(a, b):
    return lax.dot_general(a, b, (((1,), (0,)), ((), ())), preferred_element_type=jnp.float32)


def nt(a, b):
    return lax.dot_general(a, b, (((1,), (1,)), ((), ())), preferred_element_type=jnp.float32)


def cut(i, n=1):
    return slice(i * BS, (i + n) * BS)


def my_core():
    return lax.rem(lax.axis_index("col"), 2)


def faces_pair():
    index = lax.axis_index("row") * lax.axis_size("col") + lax.axis_index("col")
    return lax.rem(lax.div(index, 2) + lax.rem(index, 2), 2) > 0


def own_kernel(table, blocks, mine, other, mask, flags):
    core = my_core()
    first_row = 2 * (lax.axis_index("row") * lax.axis_size("col") + lax.axis_index("col"))
    for r in range(2):
        for w in range(BAND):
            flags[r, w] = 0
    for r in range(2):

        @pl.loop(0, table[2, r])
        def _(n):
            flags[r, table[r, n] - first_row - r + HALF] = 1

    for r in range(2):
        e = jnp.where(core > 0, 1 - r, r)
        for a in range(BAND):
            keep = flags[r, a]
            mask[r, a] = jnp.full((1, BS), keep, jnp.int32)
            x = jnp.where(keep > 0, blocks[r, a], jnp.zeros((BS, BS), blocks.dtype))
            w = jnp.where(core > 0, BAND - 1 - a, a)
            mine[e, w] = x
            other[1 - e, BAND - 1 - w] = x


def own_rows(table, blocks):
    shape = jax.ShapeDtypeStruct(blocks.shape, blocks.dtype)
    return pl.pallas_call(
        own_kernel,
        out_shape=(shape, shape, jax.ShapeDtypeStruct((2, BAND, 1, BS), jnp.int32)),
        in_specs=[SM, VM],
        out_specs=(VM, VM, VM),
        scratch_shapes=[pltpu.SMEM((2, BAND), jnp.int32)],
        compiler_params=params(),
        name="own_rows",
    )(table, blocks)


def low_slots(e):
    return [w for w in range(HALF, BAND - 1 - e) if e < 2 or not 5 <= w - HALF + 1 + e <= 8]


def first_kernel(mine, part, x1, z1, z2, single):
    at = {}

    def put(out, e, slots):
        for w in slots:
            n = at.get(id(out), 0)
            out[n] = mine[e, w] if e < 2 else part[e - 2, w]
            at[id(out)] = n + 1

    for e in range(4):
        put(x1, e, range(9 - e))
    for e in range(4):
        put(z1, e, range(5 - e))
    for e in range(4):
        put(z2, e, range(HALF, BAND - 5 - e))
    for e in range(4):
        put(x1, e, low_slots(e))
    for e in range(4):
        put(z1, e, range(HALF, BAND - 1 - e))
    for e in range(4):
        put(z1, e, range(HALF - 2 - e, HALF - e))
        put(z2, e, range(HALF - 2 - e, HALF - e))
    single[0] = jnp.where(faces_pair(), mine[0, 0], part[1, HALF])


def first_packs(mine, part):
    return pl.pallas_call(
        first_kernel,
        out_shape=[jax.ShapeDtypeStruct((n, BS, BS), mine.dtype) for n in (68, 68, 38, 1)],
        in_specs=[VM] * 2,
        out_specs=[VM] * 4,
        compiler_params=params(),
        name="first_packs",
    )(mine, part)


def second_kernel(x1, z1, single, _, cross, x2, g, h):
    for n in range(30):
        cross[n] = x1[n]
    for n in range(14):
        cross[30 + n] = z1[n]
    cross[44] = single[0]
    at1 = at2 = at3 = 0
    start_x, start_z = 30, 14
    for e in range(4):
        for w in low_slots(e):
            x2[at1] = z1[start_z + w - HALF]
            at1 += 1
        for n in range(5 - e):
            g[at2] = z1[start_z + n]
            if n < 4 - e or e < 2:
                h[at2] = x1[start_x + n]
            else:
                h[at2] = turned(z1[60 + e - 2])
            at2 += 1
        start_x += len(low_slots(e))
        start_z += 13 - e
    h[at2] = z1[14]


def second_packs(x1, z1, single, sums):
    return pl.pallas_call(
        second_kernel,
        out_shape=[jax.ShapeDtypeStruct((n, BS, BS), x1.dtype) for n in (45, 38, 14, 15)],
        in_specs=[VM] * 4,
        out_specs=[VM] * 4,
        compiler_params=params(),
        name="second_packs",
    )(x1, z1, single, sums)


def turned(x):
    return jnp.transpose(x.astype(jnp.float32)).astype(x.dtype)


def fill_rows(mine, part, rows):
    zero = jnp.zeros((BS, BS), rows.dtype)

    def block(e, k):
        w = k - e + HALF
        if not 0 <= w < BAND:
            return zero
        return mine[e, w] if e < 2 else part[e - 2, w]

    for e in range(4):
        for t in range(1, NCOL + 1):
            rows[cut(e), cut(t - 1)] = block(e, -t)
        for k in range(4):
            rows[cut(e), OWN_AT + k * BS : OWN_AT + (k + 1) * BS] = block(e, k)
        for u in range(1, FAR + 1):
            rows[cut(e), FAR_AT + (u - 1) * BS : FAR_AT + u * BS] = block(e, 3 + u)


def fill_pairs(block, near, low, pairs):
    for t in near:
        for s in range(low, NCOL + 1):
            if s > NEAR:
                x = jnp.zeros((BS, BS), pairs.dtype)
            else:
                x = turned(block(s, t)) if s < t else block(t, s)
            pairs[cut(t - low), cut(s - low)] = x


def near_start(t):
    first = 4 * ((t - 1) // 4) + 1
    return sum(14 - s for s in range(first, t))


def cross_start(t):
    return sum(10 - s for s in range(1, t))


def own_kernel_products(mine, part, own_rows, inner, near_rows, far_rows, sums, rows):
    fill_rows(mine, part, rows)
    own_rows[...] = rows[:, OWN_AT:FAR_AT]
    near_rows[...] = rows[:, :NEAR_W]
    far_rows[...] = rows[:, FAR_AT : FAR_AT + 10 * BS]
    own = rows[:, OWN_AT:FAR_AT]
    third = jnp.zeros((1, 1), jnp.float32)
    for c in range(NCOL // 2):
        near = rows[:, cut(2 * c, 2)]
        value = nn(own, near)
        third += jnp.sum(near.astype(jnp.float32) * value, keepdims=True)
    third = 3.0 * third
    top = rows[: 2 * BS, OWN_AT:FAR_AT]
    third += jnp.sum(top.astype(jnp.float32) * nn(top, own), keepdims=True)
    inner[...] = nt(rows[: 2 * BS, :], rows[...])
    second = jnp.zeros((1, 1), jnp.float32)
    for e in range(2):
        for w in range(BAND):
            x = mine[e, w].astype(jnp.float32)
            second += jnp.sum(x * x, keepdims=True)
    sums[0:1, :] = jnp.broadcast_to(second, (1, BS))
    sums[1:2, :] = jnp.broadcast_to(third, (1, BS))


def own_part(mine, part):
    return pl.pallas_call(
        own_kernel_products,
        out_shape=(
            jax.ShapeDtypeStruct((4 * BS, OWN_W), mine.dtype),
            jax.ShapeDtypeStruct((2 * BS, OWN_W), jnp.float32),
            jax.ShapeDtypeStruct((4 * BS, NEAR_W), mine.dtype),
            jax.ShapeDtypeStruct((4 * BS, 10 * BS), mine.dtype),
            jax.ShapeDtypeStruct((2, BS), jnp.float32),
        ),
        in_specs=[VM] * 2,
        out_specs=(VM,) * 5,
        scratch_shapes=[pltpu.VMEM((4 * BS, FAR_AT + FAR_W), mine.dtype)],
        compiler_params=params(),
        cost_estimate=pl.CostEstimate(flops=2 * 10**9, bytes_accessed=10**6, transcendentals=0),
        name="own_part",
    )(mine, part)


def fill_cross(block, pairs):
    for c in range(5):
        for g in range(5 - c):
            for n in (2 * c + 1, 2 * c + 2):
                for m in (2 * g + 1, 2 * g + 2):
                    x = block(n, m) if n + m <= 10 else jnp.zeros((BS, BS), pairs.dtype)
                    pairs[cut(n - 1), cut(m - 1)] = x


def cross_kernel(near_rows, far_rows, before, x1, z1, single, first, sums, pairs):
    def block(t, u):
        at = cross_start(t) + 10 - t - u
        if t == 9:
            return jnp.where(faces_pair(), single[0], jnp.zeros((BS, BS), pairs.dtype))
        return x1[at] if t < 5 else z1[at - 30]

    fill_cross(block, pairs)
    third = jnp.zeros((1, 1), jnp.float32)
    for c in range(5):
        at = cut(2 * c, 2)
        width = (10 - 2 * c) * BS
        value = nt(far_rows[:, :width], pairs[at, :width])
        first[:, at] = value
        third += jnp.sum(near_rows[:, at].astype(jnp.float32) * value, keepdims=True)
    sums[0:1, :] = before[0:1, :]
    sums[1:2, :] = before[1:2, :] + 6.0 * third


def cross_part(near_rows, far_rows, before, x1, z1, single):
    return pl.pallas_call(
        cross_kernel,
        out_shape=(
            jax.ShapeDtypeStruct((4 * BS, 10 * BS), jnp.float32),
            jax.ShapeDtypeStruct(before.shape, jnp.float32),
        ),
        in_specs=[VM] * 6,
        out_specs=(VM,) * 2,
        scratch_shapes=[pltpu.VMEM((10 * BS, 10 * BS), x1.dtype)],
        compiler_params=params(),
        cost_estimate=pl.CostEstimate(flops=10**9, bytes_accessed=10**6, transcendentals=0),
        name="cross_part",
    )(near_rows, far_rows, before, x1, z1, single)


def mid_kernel(own, near_rows, far_rows, first, swapped, partial, cross):
    fill_cross(lambda u, t: swapped[cross_start(u) + 10 - t - u], cross)
    for c in range(NCOL // 2):
        at = cut(2 * c, 2)
        value = nn(own[...], near_rows[:, at])
        if c < 5:
            width = (10 - 2 * c) * BS
            value += first[:, at]
            value += nn(far_rows[:, :width], cross[:width, at])
        partial[:, at] = value


def mid_part(own, near_rows, far_rows, first, swapped):
    return pl.pallas_call(
        mid_kernel,
        out_shape=jax.ShapeDtypeStruct(near_rows.shape, jnp.float32),
        in_specs=[VM] * 5,
        out_specs=VM,
        scratch_shapes=[pltpu.VMEM((10 * BS, 10 * BS), near_rows.dtype)],
        compiler_params=params(),
        cost_estimate=pl.CostEstimate(flops=2 * 10**9, bytes_accessed=10**6, transcendentals=0),
        name="mid_part",
    )(own, near_rows, far_rows, first, swapped)


LOW, LAST = 5, 9


def fill_near(facing, x1, x2, z1, z2, g, h, single, pairs1, pairs2, pairs3):
    def block(t, s):
        if t == NEAR:
            return jnp.where(facing, h[14], single[0])
        if t >= LAST:
            at = near_start(t) + s - t
            return jnp.where(facing, h[at], g[at])
        if t >= LOW:
            start = 14 + sum(13 - n for n in range(t - LOW))
            return jnp.where(facing, z1[start + s - t], z2[near_start(t) + s - t])
        if t > 2 and LOW <= s < LAST:
            at = 2 * (s - LOW) + t - 3
            return turned(jnp.where(facing, z1[60 + at], z2[30 + at]))
        slots = low_slots(t - 1)
        at = sum(len(low_slots(n)) for n in range(t - 1)) + slots.index(HALF + s - t)
        return jnp.where(facing, x1[30 + at], x2[at])

    fill_pairs(block, range(1, LOW), 1, pairs1)
    fill_pairs(block, range(LOW, LAST), LOW, pairs2)
    fill_pairs(block, range(LAST, NEAR + 1), LAST, pairs3)
    pairs3[cut(NCOL - LAST), :] = jnp.zeros((BS, (NCOL + 1 - LAST) * BS), pairs3.dtype)


def near_products(half, near_rows, partial, pairs1, pairs2, pairs3):
    rows = slice(2 * half * BS, (2 * half + 2) * BS)
    two, three = (LOW - 1) * BS, (LAST - 1) * BS
    for c in range(NCOL // 2):
        at = 2 * c * BS
        to = at + 2 * BS
        value = partial[rows, at:to]
        if at < two:
            value += nt(near_rows[rows, :], pairs1[at:to, :])
        else:
            value += nn(near_rows[rows, :two], pairs1[:, at:to])
        if two <= at < three:
            value += nt(near_rows[rows, two:], pairs2[at - two : to - two, :])
        elif at >= three:
            value += nn(near_rows[rows, two:three], pairs2[:, at - two : to - two])
            value += nt(near_rows[rows, three:], pairs3[at - three : to - three, :])
        for n in range(2):
            t = 2 * c + 1 + n
            for e in range(2):
                if 2 * half + e + t <= HALF:
                    yield e, t, value[cut(e), cut(n)]


def away_kernel(near_rows, partial, x1, x2, z1, z2, g, h, single, away, pairs1, pairs2, pairs3):
    fill_near(faces_pair(), x1, x2, z1, z2, g, h, single, pairs1, pairs2, pairs3)
    for e, t, value in near_products(1, near_rows, partial, pairs1, pairs2, pairs3):
        away[e * 11 + t - 1] = value.astype(away.dtype)


def away_part(near_rows, partial, x1, x2, z1, z2, g, h, single):
    shapes = (21, BS, BS), (4 * BS, NEAR_W), (4 * BS, 10 * BS), (6 * BS, 6 * BS)
    return pl.pallas_call(
        away_kernel,
        out_shape=[jax.ShapeDtypeStruct(shape, x1.dtype) for shape in shapes],
        in_specs=[VM] * 9,
        out_specs=[VM] * 4,
        compiler_params=params(),
        cost_estimate=pl.CostEstimate(flops=2 * 10**9, bytes_accessed=10**6, transcendentals=0),
        name="away_part",
    )(near_rows, partial, x1, x2, z1, z2, g, h, single)


def near_kernel(mask, near_rows, partial, inner, pairs1, pairs2, pairs3, out):
    core = my_core()

    def put(e, w, value):
        r = jnp.where(core > 0, 1 - e, e)
        a = jnp.where(core > 0, BAND - 1 - w, w)
        out[r, a] = jnp.where(mask[r, a] > 0, value, 0.0).astype(out.dtype)

    for e in range(2):
        for k in range(4):
            put(e, k - e + HALF, inner[cut(e), cut(k)])
    for e, t, value in near_products(0, near_rows, partial, pairs1, pairs2, pairs3):
        put(e, HALF - e - t, value)


def near_part(mask, near_rows, partial, inner, *pairs):
    return pl.pallas_call(
        near_kernel,
        out_shape=jax.ShapeDtypeStruct((2, BAND, BS, BS), near_rows.dtype),
        in_specs=[VM] * 7,
        out_specs=VM,
        compiler_params=params(),
        cost_estimate=pl.CostEstimate(flops=10**9, bytes_accessed=10**6, transcendentals=0),
        name="near_part",
    )(mask, near_rows, partial, inner, *pairs)


def join_kernel(mask, came, _, out, held, sems):
    core = my_core()
    copies = []
    for e, count, base in ((0, 10, 11), (1, 11, 0)):
        r = jnp.where(core > 0, 1 - e, e)

        @pl.loop(0, count)
        def _(n):
            w = BAND - count + n
            a = jnp.where(core > 0, BAND - 1 - w, w)
            spot = jnp.where(core > 0, count - 1 - n, n)
            x = came[base + n]
            held[base + spot] = jnp.where(mask[r, a] > 0, x, jnp.zeros_like(x))

        start = jnp.where(core > 0, 0, BAND - count)
        copy = pltpu.make_async_copy(
            held.at[pl.ds(base, count)], out.at[r, pl.ds(start, count)], sems.at[e]
        )
        copy.start()
        copies.append(copy)
    for copy in copies:
        copy.wait()


def join(mask, came, out):
    anywhere = pl.BlockSpec(memory_space=pl.ANY)
    return pl.pallas_call(
        join_kernel,
        out_shape=jax.ShapeDtypeStruct(out.shape, out.dtype),
        in_specs=[VM, VM, anywhere],
        out_specs=anywhere,
        scratch_shapes=[
            pltpu.VMEM(came.shape, came.dtype),
            pltpu.SemaphoreType.DMA((2,)),
        ],
        input_output_aliases={2: 0},
        compiler_params=params(),
        name="join",
    )(mask, came, out)


def body(blocks, columns, counts):
    table = jnp.pad(columns, ((0, 1), (0, 0))) + jnp.pad(counts[None], ((2, 0), (0, BAND - 2)))
    mine, other, mask = own_rows(table, blocks)
    part = to_partner(other)

    def outer(i):
        return not inner(i)

    x1, z1, z2, single = first_packs(mine, part)
    x1 = to_side(x1, 1, inner)
    z1 = to_side(z1, 2, outer)

    def singles(i):
        chip, core = divmod(i, 2)
        if inner(i):
            return 2 * (chip + 3) if core else 2 * (chip - 3) + 1
        return 2 * (chip - 4) + 1 if core else 2 * (chip + 4)

    single = permute(single, singles)
    own, inside, near_rows, far_rows, sums = own_part(mine, part)

    cross, x2, g, h = second_packs(x1, z1, single, sums)
    swapped = permute(cross, lambda i: i ^ 1 if inner(i) else -1)

    def along(pair, senders):
        def target(i):
            chip, core = divmod(i, 2)
            return 2 * (chip + (pair if core else -pair)) + core if senders(i) else -1

        return target

    z2 = to_side(z2, 2, inner)
    x2 = permute(x2, along(1, inner))
    g = permute(g, along(-1, inner))
    h = permute(h, along(-2, inner))

    first, sums = cross_part(near_rows, far_rows, sums, x1, z1, single)
    sums, swapped = lax.optimization_barrier((sums[:, 0], swapped))
    sums = all_sums(sums)
    partial = mid_part(own, near_rows, far_rows, first, swapped)
    partial, sums = lax.optimization_barrier((partial, sums))
    traces = sums / (2 * BS * lax.axis_size(AXES))
    away, *pairs = away_part(near_rows, partial, x1, x2, z1, z2, g, h, single)
    came = to_partner(away)
    out = near_part(mask, near_rows, partial, inside, *pairs)
    square = join(mask, came, out)
    return square, traces


def solution(mesh):
    return jax.shard_map(
        body,
        mesh=mesh,
        in_specs=(P(AXES, None, None, None), P(AXES, None), P(AXES)),
        out_specs=(P(AXES, None, None, None), P()),
        check_vma=False,
    )
```

time: 97.3 us -> 87.3 us (0.90)
  starting transfers between devices: 49.4 us -> 38.6 us
  waiting for transfers between devices: 25.4 us -> 29.6 us
  Pallas kernels: 18.2 us -> 14.9 us
    ppermute x15, starting transfers between devices: 49.4 us -> 38.6 us  [permute(): lax.ppermute(value, AXES, [(i, j) for i, j in pairs if 0 <= j < devices])]
    ppermute x15, waiting for transfers between devices: 25.4 us -> 29.6 us  [permute(): lax.ppermute(value, AXES, [(i, j) for i, j in pairs if 0 <= j < devices])]
    pallas_call x3, Pallas kernels: 7.07 us -> 5.76 us  [the longest x1 2.26 us: mid_part(): pl.pallas_call(mid_kernel, out_shape=jax.ShapeDtypeStruct(near_rows.shape...]
  transfers between devices with their start and end apart: 15 -> 15, of which waited for: 6 -> 6; matrix products, arithmetic and copies ran while one was open for 1% -> 1% of each run, Pallas kernels for 12% -> 11%
where the time goes in v3:
time: 87.3 us; the launch traced here: 87 us
  starting transfers between devices  38.6 us (44%)
  waiting for transfers between devices  29.6 us (34%)
  Pallas kernels  14.9 us (17%)
  local copies, waits for them, and re-layouts  1.59 us (2%)
  other arithmetic  1.23 us (1%)
  between operations  0.97 us (1%)
    ppermute x15, starting transfers between devices, permute(): lax.ppermute(value, AXES, [(i, j) for i, j in pairs if 0 <= j < devices])  38.6 us
    ppermute x15, waiting for transfers between devices, permute(): lax.ppermute(value, AXES, [(i, j) for i, j in pairs if 0 <= j < devices])  29.6 us
    pallas_call x1, Pallas kernels, near_part(): pl.pallas_call(near_kernel, out_shape=jax.ShapeDtypeStruct((2, BAND, BS,...  3.07 us
    pallas_call x1, Pallas kernels, own_part(): pl.pallas_call(own_kernel_products, out_shape=(jax.ShapeDtypeStruct((4 *...  3 us
    pallas_call x1, Pallas kernels, mid_part(): pl.pallas_call(mid_kernel, out_shape=jax.ShapeDtypeStruct(near_rows.shape...  2.26 us
    pallas_call x1, Pallas kernels, away_part(): pl.pallas_call(away_kernel, out_shape=[jax.ShapeDtypeStruct(shape, x1.dty...  2.02 us
  transfers between devices with their start and end apart: 15, of which 6 were waited for; matrix products, arithmetic and copies ran while one was open for 1% of the time, Pallas kernels for 11%

profile of v3, /device:TPU:0, one launch (start us, length us, event | category | flops | bytes accessed | tf_op | source)
XLA Modules:
  0.0 87.0 jit_solution(7115353652156589485)
XLA Ops:
  0.6 0.7 pad_add_fusion.table
  1.3 1.5 %copy-done = bf16[2,27,128,128]{3,2,1,0:T(8,128)(2,1)S(1)} copy-done((bf16[2,27,128,128]{3,2,1,0:T(8,128)(2,1)S(1)}, bf16[2,27,128,128]{3,2,1,0:T(8,128)(2,1)}, u32[]{:S(2)}) %copy-start) | copy-done | bytes 1769496
  2.8 1.4 %own_rows.1 = (bf16[2,27,128,128]{3,2,1,0:T(8,128)(2,1)S(1)}, bf16[2,27,128,128]{3,2,1,0:T(8,128)(2,1)S(1)}, s32[2,27,1,128]{3,2,1,0:T(1,128)S(1)}) custom-call(s32[3,27]{1,0:T(4,128)S(1)} %pad_add_fusion.table, bf16[2,27,128,128]{3,2,1,0:T(8,128)(2,1)S(1)} %copy-done), custom_call_target="tpu_custom_call" | custom-call | tf_op jit(solution)/shard_map/own_rows/pallas_call | solution.py:106
  4.2 0.5 collective-permute-start
  4.7 3.3 %collective-permute-done.part = bf16[2,27,128,128]{3,2,1,0:T(8,128)(2,1)S(1)} collective-permute-done((bf16[2,27,128,128]{3,2,1,0:T(8,128)(2,1)S(1)}, bf16[2,27,128,128]{3,2,1,0:T(8,128)(2,1)S(1)}, u32[]{:S(2)}, u32[]{:S(2)}) %collective-permute-start) | collective-permute-done | bytes 1769504 | tf_op jit(solution)/shard_map/ppermute | solution.py:31
  8.0 0.4 first_packs.1
  8.4 0.8 collective-permute-start.1
  9.2 0.8 collective-permute-start.2
  10.0 10.1 %collective-permute-start.3 = (bf16[1,128,128]{2,1,0:T(8,128)(2,1)S(1)}, bf16[1,128,128]{2,1,0:T(8,128)(2,1)S(1)}, u32[]{:S(2)}, u32[]{:S(2)}) collective-permute-start(bf16[1,128,128]{2,1,0:T(8,128)(2,1)S(1)} %get-tuple-element.37), channel_id=1, source_target_pairs={{0,8},{1,6},{4,12},{5,10},{6,1},{8,16},{9,14},{10,5},{11,3},{12,20... | collective-permute-start | bytes 98312 | tf_op jit(solution)/shard_map/ppermute | solution.py:31
  20.1 3.0 %own_part.1 = (bf16[512,512]{1,0:T(8,128)(2,1)S(1)}, f32[256,512]{1,0:T(8,128)S(1)}, bf16[512,1792]{1,0:T(8,128)(2,1)S(1)}, bf16[512,1280]{1,0:T(8,128)(2,1)S(1)}, f32[2,128]{1,0:T(2,128)S(1)}) custom-call(bf16[2,27,128,128]{3,2,1,0:T(8,128)(2,1)S(1)} %get-tuple-element.29.mine, bf16[2,27,128,128]{3,2,1,0:T(8,128)(2,1)S(1)} %collective-permute-done.part), custom_call_target="tpu_custom_call" | custom-call | flops 2000000000 | bytes 1000000 | tf_op jit(solution)/shard_map/own_part/pallas_call | solution.py:258
  23.2 0.3 second_packs.1
  23.5 1.3 %collective-permute-start.4 = (bf16[45,128,128]{2,1,0:T(8,128)(2,1)S(1)}, bf16[45,128,128]{2,1,0:T(8,128)(2,1)S(1)}, u32[]{:S(2)}, u32[]{:S(2)}) collective-permute-start(bf16[45,128,128]{2,1,0:T(8,128)(2,1)S(1)} %get-tuple-element.40), channel_id=1, source_target_pairs={{1,0},{2,3},{5,4},{6,7},{9,8},{10,11},{13,12},{14,15},{17,16},{18,... | collective-permute-start | bytes 4423688 | tf_op jit(solution)/shard_map/ppermute | solution.py:31
  24.8 0.7 collective-permute-start.11
  25.5 1.3 %collective-permute-start.10 = (bf16[38,128,128]{2,1,0:T(8,128)(2,1)S(1)}, bf16[38,128,128]{2,1,0:T(8,128)(2,1)S(1)}, u32[]{:S(2)}, u32[]{:S(2)}) collective-permute-start(bf16[38,128,128]{2,1,0:T(8,128)(2,1)S(1)} %get-tuple-element.44), channel_id=1, source_target_pairs={{1,3},{2,0},{5,7},{6,4},{9,11},{10,8},{13,15},{14,12},{17,19},{18,... | collective-permute-start | bytes 3735560 | tf_op jit(solution)/shard_map/ppermute | solution.py:31
  26.8 0.7 collective-permute-start.13
  27.5 0.9 %collective-permute-start.12 = (bf16[14,128,128]{2,1,0:T(8,128)(2,1)S(1)}, bf16[14,128,128]{2,1,0:T(8,128)(2,1)S(1)}, u32[]{:S(2)}, u32[]{:S(2)}) collective-permute-start(bf16[14,128,128]{2,1,0:T(8,128)(2,1)S(1)} %get-tuple-element.46), channel_id=1, source_target_pairs={{2,4},{5,3},{6,8},{9,7},{10,12},{13,11},{14,16},{17,15},{18,20},{2... | collective-permute-start | bytes 1376264 | tf_op jit(solution)/shard_map/ppermute | solution.py:31
  28.4 1.5 %cross_part.1 = (f32[512,1280]{1,0:T(8,128)S(1)}, f32[2,128]{1,0:T(2,128)S(1)}) custom-call(bf16[512,1792]{1,0:T(8,128)(2,1)S(1)} %get-tuple-element.31.near_rows, bf16[512,1280]{1,0:T(8,128)(2,1)S(1)} %get-tuple-element.33.far_rows, f32[2,128]{1,0:T(2,128)S(1)} %get-tuple-element.34.before._, bf16[68,128,128]{2,1,0:T(8,128)(2,1)S(1)} %collective-permute-done.1.x1, ...), custom_call_target="tpu_custom_call" | custom-call | flops 1000000000 | bytes 1000000 | tf_op jit(solution)/shard_map/cross_part/pallas_call | solution.py:305
  30.0 16.8 %collective-permute-done.4.swapped = bf16[45,128,128]{2,1,0:T(8,128)(2,1)S(1)} collective-permute-done((bf16[45,128,128]{2,1,0:T(8,128)(2,1)S(1)}, bf16[45,128,128]{2,1,0:T(8,128)(2,1)S(1)}, u32[]{:S(2)}, u32[]{:S(2)}) %collective-permute-start.4) | collective-permute-done | bytes 1474592 | tf_op jit(solution)/shard_map/ppermute | solution.py:31
  46.8 7.7 %collective-permute-start.5 = (f32[2]{0:T(128)S(1)}, f32[2]{0:T(128)S(1)}, u32[]{:S(2)}, u32[]{:S(2)}) collective-permute-start(f32[2]{0:T(128)S(1)} %slice_reduce_fusion), channel_id=1, source_target_pairs={{0,1},{1,0},{2,3},{3,2},{4,5},{5,4},{6,7},{7,6},{8,9},{9,8},{10,11... | collective-permute-start | bytes 32 | tf_op jit(solution)/shard_map/ppermute | solution.py:31
  54.6 2.3 %mid_part.1.partial = f32[512,1792]{1,0:T(8,128)S(1)} custom-call(bf16[512,512]{1,0:T(8,128)(2,1)S(1)} %get-tuple-element.32.own, bf16[512,1792]{1,0:T(8,128)(2,1)S(1)} %get-tuple-element.31.near_rows, bf16[512,1280]{1,0:T(8,128)(2,1)S(1)} %get-tuple-element.33.far_rows, f32[512,1280]{1,0:T(8,128)S(1)} %get-tuple-element.38.first, ...), custom_call_target="tpu_custom_call" | custom-call | flops 2000000000 | bytes 1000000 | tf_op jit(solution)/shard_map/mid_part/pallas_call | solution.py:333
  56.8 5.8 %collective-permute-start.6 = (f32[2]{0:T(128)S(1)}, f32[2]{0:T(128)S(1)}, u32[]{:S(2)}, u32[]{:S(2)}) collective-permute-start(f32[2]{0:T(128)S(1)} %add.23), channel_id=1, source_target_pairs={{0,16},{1,17},{2,18},{3,19},{4,20},{5,21},{6,22},{7,23},{8,24},{9,... | collective-permute-start | bytes 32 | tf_op jit(solution)/shard_map/ppermute | solution.py:31
  62.6 1.5 %collective-permute-done.6 = f32[2]{0:T(128)S(1)} collective-permute-done((f32[2]{0:T(128)S(1)}, f32[2]{0:T(128)S(1)}, u32[]{:S(2)}, u32[]{:S(2)}) %collective-permute-start.6) | collective-permute-done | bytes 40 | tf_op jit(solution)/shard_map/ppermute | solution.py:31
  64.2 3.5 %collective-permute-done.7 = f32[2]{0:T(128)S(1)} collective-permute-done((f32[2]{0:T(128)S(1)}, f32[2]{0:T(128)S(1)}, u32[]{:S(2)}, u32[]{:S(2)}) %collective-permute-start.7) | collective-permute-done | bytes 40 | tf_op jit(solution)/shard_map/ppermute | solution.py:31
  67.7 4.8 %collective-permute-start.8 = (f32[2]{0:T(128)S(1)}, f32[2]{0:T(128)S(1)}, u32[]{:S(2)}, u32[]{:S(2)}) collective-permute-start(f32[2]{0:T(128)S(1)} %add.25), channel_id=1, source_target_pairs={{0,4},{1,5},{2,6},{3,7},{4,0},{5,1},{6,2},{7,3},{8,12},{9,13},{10,... | collective-permute-start | bytes 32 | tf_op jit(solution)/shard_map/ppermute | solution.py:31
  72.5 1.6 %collective-permute-done.8 = f32[2]{0:T(128)S(1)} collective-permute-done((f32[2]{0:T(128)S(1)}, f32[2]{0:T(128)S(1)}, u32[]{:S(2)}, u32[]{:S(2)}) %collective-permute-start.8) | collective-permute-done | bytes 40 | tf_op jit(solution)/shard_map/ppermute | solution.py:31
  74.1 1.6 %collective-permute-start.9 = (f32[2]{0:T(128)S(1)}, f32[2]{0:T(128)S(1)}, u32[]{:S(2)}, u32[]{:S(2)}) collective-permute-start(f32[2]{0:T(128)S(1)} %add.26), channel_id=1, source_target_pairs={{0,8},{1,9},{2,10},{3,11},{4,12},{5,13},{6,14},{7,15},{8,0},{9,1},... | collective-permute-start | bytes 32 | tf_op jit(solution)/shard_map/ppermute | solution.py:31
  75.7 2.8 %collective-permute-done.9 = f32[2]{0:T(128)S(1)} collective-permute-done((f32[2]{0:T(128)S(1)}, f32[2]{0:T(128)S(1)}, u32[]{:S(2)}, u32[]{:S(2)}) %collective-permute-start.9) | collective-permute-done | bytes 40 | tf_op jit(solution)/shard_map/ppermute | solution.py:31
  78.5 2.0 %away_part.1 = (bf16[21,128,128]{2,1,0:T(8,128)(2,1)S(1)}, bf16[512,1792]{1,0:T(8,128)(2,1)S(1)}, bf16[512,1280]{1,0:T(8,128)(2,1)S(1)}, bf16[768,768]{1,0:T(8,128)(2,1)S(1)}) custom-call(bf16[512,1792]{1,0:T(8,128)(2,1)S(1)} %get-tuple-element.31.near_rows, f32[512,1792]{1,0:T(8,128)S(1)} %mid_part.1.partial, ...), custom_call_target="tpu_custom_call" | custom-call | flops 2000000000 | bytes 1000000 | tf_op jit(solution)/shard_map/away_part/pallas_call | solution.py:402
  80.6 1.6 %collective-permute-start.14 = (bf16[21,128,128]{2,1,0:T(8,128)(2,1)S(1)}, bf16[21,128,128]{2,1,0:T(8,128)(2,1)S(1)}, u32[]{:S(2)}, u32[]{:S(2)}) collective-permute-start(bf16[21,128,128]{2,1,0:T(8,128)(2,1)S(1)} %get-tuple-element.48), channel_id=1, source_target_pairs={{0,1},{1,0},{2,3},{3,2},{4,5},{5,4},{6,7},{7,6},{8,9},{9,8},{10,11... | collective-permute-start | bytes 2064392 | tf_op jit(solution)/shard_map/ppermute | solution.py:31
  82.2 3.1 %near_part.1._ = bf16[2,27,128,128]{3,2,1,0:T(8,128)(2,1)} custom-call(s32[2,27,1,128]{3,2,1,0:T(1,128)S(1)} %get-tuple-element.28.mask, bf16[512,1792]{1,0:T(8,128)(2,1)S(1)} %get-tuple-element.31.near_rows, f32[512,1792]{1,0:T(8,128)S(1)} %mid_part.1.partial, f32[256,512]{1,0:T(8,128)S(1)} %get-tuple-element.49.inner, ...), custom_call_target="tpu_custom_call" | custom-call | flops 1000000000 | bytes 1000000 | tf_op jit(solution)/shard_map/near_part/pallas_call | solution.py:429
  85.2 0.5 broadcast_multiply_fusion
  85.8 1.1 %join.1 = bf16[2,27,128,128]{3,2,1,0:T(8,128)(2,1)} custom-call(s32[2,27,1,128]{3,2,1,0:T(1,128)S(1)} %get-tuple-element.28.mask, bf16[21,128,128]{2,1,0:T(8,128)(2,1)S(1)} %collective-permute-done.14.came, bf16[2,27,128,128]{3,2,1,0:T(8,128)(2,1)} %near_part.1._), custom_call_target="tpu_custom_call", output_to_operand_aliasing={{}: (2, {})} | custom-call | tf_op jit(solution)/shard_map/join/pallas_call | solution.py:466
  (17 shorter events, 0.2 us)
Async XLA Ops:
  1.3 1.5 %copy-start = (bf16[2,27,128,128]{3,2,1,0:T(8,128)(2,1)S(1)}, bf16[2,27,128,128]{3,2,1,0:T(8,128)(2,1)}, u32[]{:S(2)}) copy-start(bf16[2,27,128,128]{3,2,1,0:T(8,128)(2,1)} %blocks.1) | copy-start | bytes 5308420
  4.2 3.8 %collective-permute-start = (bf16[2,27,128,128]{3,2,1,0:T(8,128)(2,1)S(1)}, bf16[2,27,128,128]{3,2,1,0:T(8,128)(2,1)S(1)}, u32[]{:S(2)}, u32[]{:S(2)}) collective-permute-start(bf16[2,27,128,128]{3,2,1,0:T(8,128)(2,1)S(1)} %get-tuple-element.30), channel_id=1, source_target_pairs={{0,1},{1,0},{2,3},{3,2},{4,5},{5,4},{6,7},{7,6},{8,9},{9,8},{10,11... | collective-permute-start | bytes 5308424 | tf_op jit(solution)/shard_map/ppermute | solution.py:31
  8.4 14.7 %collective-permute-start.1 = (bf16[68,128,128]{2,1,0:T(8,128)(2,1)S(1)}, bf16[68,128,128]{2,1,0:T(8,128)(2,1)S(1)}, u32[]{:S(2)}, u32[]{:S(2)}) collective-permute-start(bf16[68,128,128]{2,1,0:T(8,128)(2,1)S(1)} %get-tuple-element.35), channel_id=1, source_target_pairs={{1,2},{2,1},{5,6},{6,5},{9,10},{10,9},{13,14},{14,13},{17,18},{18,... | collective-permute-start | bytes 6684680 | tf_op jit(solution)/shard_map/ppermute | solution.py:31
  9.2 13.9 %collective-permute-start.2 = (bf16[68,128,128]{2,1,0:T(8,128)(2,1)S(1)}, bf16[68,128,128]{2,1,0:T(8,128)(2,1)S(1)}, u32[]{:S(2)}, u32[]{:S(2)}) collective-permute-start(bf16[68,128,128]{2,1,0:T(8,128)(2,1)S(1)} %get-tuple-element.36), channel_id=1, source_target_pairs={{3,6},{4,1},{7,10},{8,5},{11,14},{12,9},{15,18},{16,13},{19,22},{2... | collective-permute-start | bytes 6684680 | tf_op jit(solution)/shard_map/ppermute | solution.py:31
  10.0 13.1 %collective-permute-start.3 = (bf16[1,128,128]{2,1,0:T(8,128)(2,1)S(1)}, bf16[1,128,128]{2,1,0:T(8,128)(2,1)S(1)}, u32[]{:S(2)}, u32[]{:S(2)}) collective-permute-start(bf16[1,128,128]{2,1,0:T(8,128)(2,1)S(1)} %get-tuple-element.37), channel_id=1, source_target_pairs={{0,8},{1,6},{4,12},{5,10},{6,1},{8,16},{9,14},{10,5},{11,3},{12,20... | collective-permute-start | bytes 98312 | tf_op jit(solution)/shard_map/ppermute | solution.py:31
  23.5 23.3 %collective-permute-start.4 = (bf16[45,128,128]{2,1,0:T(8,128)(2,1)S(1)}, bf16[45,128,128]{2,1,0:T(8,128)(2,1)S(1)}, u32[]{:S(2)}, u32[]{:S(2)}) collective-permute-start(bf16[45,128,128]{2,1,0:T(8,128)(2,1)S(1)} %get-tuple-element.40), channel_id=1, source_target_pairs={{1,0},{2,3},{5,4},{6,7},{9,8},{10,11},{13,12},{14,15},{17,16},{18,... | collective-permute-start | bytes 4423688 | tf_op jit(solution)/shard_map/ppermute | solution.py:31
  24.8 53.7 %collective-permute-start.11 = (bf16[38,128,128]{2,1,0:T(8,128)(2,1)S(1)}, bf16[38,128,128]{2,1,0:T(8,128)(2,1)S(1)}, u32[]{:S(2)}, u32[]{:S(2)}) collective-permute-start(bf16[38,128,128]{2,1,0:T(8,128)(2,1)S(1)} %get-tuple-element.45), channel_id=1, source_target_pairs={{1,4},{5,8},{6,3},{9,12},{10,7},{13,16},{14,11},{17,20},{18,15},{2... | collective-permute-start | bytes 3735560 | tf_op jit(solution)/shard_map/ppermute | solution.py:31
  25.5 53.0 %collective-permute-start.10 = (bf16[38,128,128]{2,1,0:T(8,128)(2,1)S(1)}, bf16[38,128,128]{2,1,0:T(8,128)(2,1)S(1)}, u32[]{:S(2)}, u32[]{:S(2)}) collective-permute-start(bf16[38,128,128]{2,1,0:T(8,128)(2,1)S(1)} %get-tuple-element.44), channel_id=1, source_target_pairs={{1,3},{2,0},{5,7},{6,4},{9,11},{10,8},{13,15},{14,12},{17,19},{18,... | collective-permute-start | bytes 3735560 | tf_op jit(solution)/shard_map/ppermute | solution.py:31
  26.8 51.7 %collective-permute-start.13 = (bf16[15,128,128]{2,1,0:T(8,128)(2,1)S(1)}, bf16[15,128,128]{2,1,0:T(8,128)(2,1)S(1)}, u32[]{:S(2)}, u32[]{:S(2)}) collective-permute-start(bf16[15,128,128]{2,1,0:T(8,128)(2,1)S(1)} %get-tuple-element.47), channel_id=1, source_target_pairs={{2,6},{5,1},{6,10},{9,5},{10,14},{13,9},{14,18},{17,13},{18,22},{2... | collective-permute-start | bytes 1474568 | tf_op jit(solution)/shard_map/ppermute | solution.py:31
  27.5 51.0 %collective-permute-start.12 = (bf16[14,128,128]{2,1,0:T(8,128)(2,1)S(1)}, bf16[14,128,128]{2,1,0:T(8,128)(2,1)S(1)}, u32[]{:S(2)}, u32[]{:S(2)}) collective-permute-start(bf16[14,128,128]{2,1,0:T(8,128)(2,1)S(1)} %get-tuple-element.46), channel_id=1, source_target_pairs={{2,4},{5,3},{6,8},{9,7},{10,12},{13,11},{14,16},{17,15},{18,20},{2... | collective-permute-start | bytes 1376264 | tf_op jit(solution)/shard_map/ppermute | solution.py:31
  46.8 10.0 %collective-permute-start.5 = (f32[2]{0:T(128)S(1)}, f32[2]{0:T(128)S(1)}, u32[]{:S(2)}, u32[]{:S(2)}) collective-permute-start(f32[2]{0:T(128)S(1)} %slice_reduce_fusion), channel_id=1, source_target_pairs={{0,1},{1,0},{2,3},{3,2},{4,5},{5,4},{6,7},{7,6},{8,9},{9,8},{10,11... | collective-permute-start | bytes 32 | tf_op jit(solution)/shard_map/ppermute | solution.py:31
  56.8 7.3 %collective-permute-start.6 = (f32[2]{0:T(128)S(1)}, f32[2]{0:T(128)S(1)}, u32[]{:S(2)}, u32[]{:S(2)}) collective-permute-start(f32[2]{0:T(128)S(1)} %add.23), channel_id=1, source_target_pairs={{0,16},{1,17},{2,18},{3,19},{4,20},{5,21},{6,22},{7,23},{8,24},{9,... | collective-permute-start | bytes 32 | tf_op jit(solution)/shard_map/ppermute | solution.py:31
  64.2 3.5 %collective-permute-start.7 = (f32[2]{0:T(128)S(1)}, f32[2]{0:T(128)S(1)}, u32[]{:S(2)}, u32[]{:S(2)}) collective-permute-start(f32[2]{0:T(128)S(1)} %add.24), channel_id=1, source_target_pairs={{0,2},{1,3},{2,0},{3,1},{4,6},{5,7},{6,4},{7,5},{8,10},{9,11},{10,... | collective-permute-start | bytes 32 | tf_op jit(solution)/shard_map/ppermute | solution.py:31
  67.7 6.4 %collective-permute-start.8 = (f32[2]{0:T(128)S(1)}, f32[2]{0:T(128)S(1)}, u32[]{:S(2)}, u32[]{:S(2)}) collective-permute-start(f32[2]{0:T(128)S(1)} %add.25), channel_id=1, source_target_pairs={{0,4},{1,5},{2,6},{3,7},{4,0},{5,1},{6,2},{7,3},{8,12},{9,13},{10,... | collective-permute-start | bytes 32 | tf_op jit(solution)/shard_map/ppermute | solution.py:31
  74.1 4.4 %collective-permute-start.9 = (f32[2]{0:T(128)S(1)}, f32[2]{0:T(128)S(1)}, u32[]{:S(2)}, u32[]{:S(2)}) collective-permute-start(f32[2]{0:T(128)S(1)} %add.26), channel_id=1, source_target_pairs={{0,8},{1,9},{2,10},{3,11},{4,12},{5,13},{6,14},{7,15},{8,0},{9,1},... | collective-permute-start | bytes 32 | tf_op jit(solution)/shard_map/ppermute | solution.py:31
  80.6 5.2 %collective-permute-start.14 = (bf16[21,128,128]{2,1,0:T(8,128)(2,1)S(1)}, bf16[21,128,128]{2,1,0:T(8,128)(2,1)S(1)}, u32[]{:S(2)}, u32[]{:S(2)}) collective-permute-start(bf16[21,128,128]{2,1,0:T(8,128)(2,1)S(1)} %get-tuple-element.48), channel_id=1, source_target_pairs={{0,1},{1,0},{2,3},{3,2},{4,5},{5,4},{6,7},{7,6},{8,9},{9,8},{10,11... | collective-permute-start | bytes 2064392 | tf_op jit(solution)/shard_map/ppermute | solution.py:31

commit v4 on v3

--- a/solution.py
+++ b/solution.py
@@ -49,10 +49,8 @@
     return (i // 2 + i % 2) % 2 == 1
 
 
-def all_sums(value):
-    devices = lax.axis_size(AXES)
-    steps = [1 << n for n in range(devices.bit_length() - 1)]
-    for step in steps[:1] + steps[4:] + steps[1:4]:
+def sum_over(value, steps):
+    for step in steps:
         value = value + permute(value, lambda i: i ^ step)
     return value
 
@@ -115,7 +113,7 @@
 
 
 def low_slots(e):
-    return [w for w in range(HALF, BAND - 1 - e) if e < 2 or not 5 <= w - HALF + 1 + e <= 8]
+    return [w for w in range(HALF, BAND - 1 - e) if e < 3 or not 5 <= w - HALF + 1 + e <= 8]
 
 
 def first_kernel(mine, part, x1, z1, z2, single):
@@ -138,15 +136,15 @@
     for e in range(4):
         put(z1, e, range(HALF, BAND - 1 - e))
     for e in range(4):
-        put(z1, e, range(HALF - 2 - e, HALF - e))
-        put(z2, e, range(HALF - 2 - e, HALF - e))
+        put(z1, e, range(HALF - 1 - e, HALF - e))
+        put(z2, e, range(HALF - 1 - e, HALF - e))
     single[0] = jnp.where(faces_pair(), mine[0, 0], part[1, HALF])
 
 
 def first_packs(mine, part):
     return pl.pallas_call(
         first_kernel,
-        out_shape=[jax.ShapeDtypeStruct((n, BS, BS), mine.dtype) for n in (68, 68, 38, 1)],
+        out_shape=[jax.ShapeDtypeStruct((n, BS, BS), mine.dtype) for n in (72, 64, 34, 1)],
         in_specs=[VM] * 2,
         out_specs=[VM] * 4,
         compiler_params=params(),
@@ -154,38 +152,49 @@
     )(mine, part)
 
 
-def second_kernel(x1, z1, single, _, cross, x2, g, h):
+def second_kernel(x1, z1, _, x2, g, h):
+    at1 = at2 = 0
+    start_x, start_z = 30, 14
+    for e in range(4):
+        for w in low_slots(e):
+            x2[at1] = z1[start_z + w - HALF]
+            at1 += 1
+        for n in range(5 - e):
+            g[at2] = z1[start_z + n]
+            h[at2] = x1[start_x + n] if n < 4 - e or e < 3 else turned(z1[60])
+            at2 += 1
+        start_x += len(low_slots(e))
+        start_z += 13 - e
+    h[at2] = z1[14]
+
+
+def second_packs(x1, z1, sums):
+    return pl.pallas_call(
+        second_kernel,
+        out_shape=[jax.ShapeDtypeStruct((n, BS, BS), x1.dtype) for n in (42, 14, 15)],
+        in_specs=[VM] * 3,
+        out_specs=[VM] * 3,
+        compiler_params=params(),
+        name="second_packs",
+    )(x1, z1, sums)
+
+
+def join_cross_kernel(x1, z1, single, _, cross):
     for n in range(30):
         cross[n] = x1[n]
     for n in range(14):
         cross[30 + n] = z1[n]
     cross[44] = single[0]
-    at1 = at2 = at3 = 0
-    start_x, start_z = 30, 14
-    for e in range(4):
-        for w in low_slots(e):
-            x2[at1] = z1[start_z + w - HALF]
-            at1 += 1
-        for n in range(5 - e):
-            g[at2] = z1[start_z + n]
-            if n < 4 - e or e < 2:
-                h[at2] = x1[start_x + n]
-            else:
-                h[at2] = turned(z1[60 + e - 2])
-            at2 += 1
-        start_x += len(low_slots(e))
-        start_z += 13 - e
-    h[at2] = z1[14]
-
-
-def second_packs(x1, z1, single, sums):
-    return pl.pallas_call(
-        second_kernel,
-        out_shape=[jax.ShapeDtypeStruct((n, BS, BS), x1.dtype) for n in (45, 38, 14, 15)],
+
+
+def join_cross(x1, z1, single, sums):
+    return pl.pallas_call(
+        join_cross_kernel,
+        out_shape=jax.ShapeDtypeStruct((45, BS, BS), x1.dtype),
         in_specs=[VM] * 4,
-        out_specs=[VM] * 4,
-        compiler_params=params(),
-        name="second_packs",
+        out_specs=VM,
+        compiler_params=params(),
+        name="join_cross",
     )(x1, z1, single, sums)
 
 
@@ -297,8 +306,9 @@
         value = nt(far_rows[:, :width], pairs[at, :width])
         first[:, at] = value
         third += jnp.sum(near_rows[:, at].astype(jnp.float32) * value, keepdims=True)
-    sums[0:1, :] = before[0:1, :]
-    sums[1:2, :] = before[1:2, :] + 6.0 * third
+    scale = 1.0 / (2 * BS * lax.axis_size(AXES))
+    sums[0:1, :] = before[0:1, :] * scale
+    sums[1:2, :] = (before[1:2, :] + 6.0 * third) * scale
 
 
 def cross_part(near_rows, far_rows, before, x1, z1, single):
@@ -355,8 +365,8 @@
         if t >= LOW:
             start = 14 + sum(13 - n for n in range(t - LOW))
             return jnp.where(facing, z1[start + s - t], z2[near_start(t) + s - t])
-        if t > 2 and LOW <= s < LAST:
-            at = 2 * (s - LOW) + t - 3
+        if t == 4 and LOW <= s < LAST:
+            at = s - LOW
             return turned(jnp.where(facing, z1[60 + at], z2[30 + at]))
         slots = low_slots(t - 1)
         at = sum(len(low_slots(n)) for n in range(t - 1)) + slots.index(HALF + s - t)
@@ -499,8 +509,8 @@
     single = permute(single, singles)
     own, inside, near_rows, far_rows, sums = own_part(mine, part)
 
-    cross, x2, g, h = second_packs(x1, z1, single, sums)
-    swapped = permute(cross, lambda i: i ^ 1 if inner(i) else -1)
+    x2, g, h = second_packs(x1, z1, sums)
+    swapped = permute(join_cross(x1, z1, single, g), lambda i: i ^ 1 if inner(i) else -1)
 
     def along(pair, senders):
         def target(i):
@@ -516,13 +526,14 @@
 
     first, sums = cross_part(near_rows, far_rows, sums, x1, z1, single)
     sums, swapped = lax.optimization_barrier((sums[:, 0], swapped))
-    sums = all_sums(sums)
+    steps = [1 << n for n in range(lax.axis_size(AXES).bit_length() - 1)]
+    sums = sum_over(sums, steps[:1] + steps[4:] + steps[1:3])
     partial = mid_part(own, near_rows, far_rows, first, swapped)
     partial, sums = lax.optimization_barrier((partial, sums))
-    traces = sums / (2 * BS * lax.axis_size(AXES))
     away, *pairs = away_part(near_rows, partial, x1, x2, z1, z2, g, h, single)
     came = to_partner(away)
     out = near_part(mask, near_rows, partial, inside, *pairs)
+    traces = sum_over(sums, steps[3:4])
     square = join(mask, came, out)
     return square, traces
 

time: 87.3 us -> 83.6 us (0.958)
  waiting for transfers between devices: 29.6 us -> 26.2 us
    ppermute x15, waiting for transfers between devices: 29.6 us -> 26.2 us  [permute(): lax.ppermute(value, AXES, [(i, j) for i, j in pairs if 0 <= j < devices])]
  transfers between devices with their start and end apart: 15 -> 15, of which waited for: 6 -> 6; matrix products, arithmetic and copies ran while one was open for 1% -> 1% of each run, Pallas kernels for 11% -> 12%
where the time goes in v4:
time: 83.6 us; the launch traced here: 83.3 us
  starting transfers between devices  38.3 us (46%)
  waiting for transfers between devices  26.2 us (31%)
  Pallas kernels  14.9 us (18%)
  local copies, waits for them, and re-layouts  1.59 us (2%)
  other arithmetic  1.23 us (1%)
  between operations  0.98 us (1%)
    ppermute x15, starting transfers between devices, permute(): lax.ppermute(value, AXES, [(i, j) for i, j in pairs if 0 <= j < devices])  38.3 us
    ppermute x15, waiting for transfers between devices, permute(): lax.ppermute(value, AXES, [(i, j) for i, j in pairs if 0 <= j < devices])  26.2 us
    pallas_call x1, Pallas kernels, near_part(): pl.pallas_call(near_kernel, out_shape=jax.ShapeDtypeStruct((2, BAND, BS,...  3.08 us
    pallas_call x1, Pallas kernels, own_part(): pl.pallas_call(own_kernel_products, out_shape=(jax.ShapeDtypeStruct((4 *...  2.96 us
    pallas_call x1, Pallas kernels, mid_part(): pl.pallas_call(mid_kernel, out_shape=jax.ShapeDtypeStruct(near_rows.shape...  2.26 us
    pallas_call x1, Pallas kernels, away_part(): pl.pallas_call(away_kernel, out_shape=[jax.ShapeDtypeStruct(shape, x1.dty...  1.98 us
  transfers between devices with their start and end apart: 15, of which 6 were waited for; matrix products, arithmetic and copies ran while one was open for 1% of the time, Pallas kernels for 12%

profile of v4, /device:TPU:0, one launch (start us, length us, event | category | flops | bytes accessed | tf_op | source)
XLA Modules:
  0.0 83.3 jit_solution(2234032989356704972)
XLA Ops:
  0.6 0.7 pad_add_fusion.table
  1.3 1.5 %copy-done = bf16[2,27,128,128]{3,2,1,0:T(8,128)(2,1)S(1)} copy-done((bf16[2,27,128,128]{3,2,1,0:T(8,128)(2,1)S(1)}, bf16[2,27,128,128]{3,2,1,0:T(8,128)(2,1)}, u32[]{:S(2)}) %copy-start) | copy-done | bytes 1769496
  2.8 1.4 %own_rows.1 = (bf16[2,27,128,128]{3,2,1,0:T(8,128)(2,1)S(1)}, bf16[2,27,128,128]{3,2,1,0:T(8,128)(2,1)S(1)}, s32[2,27,1,128]{3,2,1,0:T(1,128)S(1)}) custom-call(s32[3,27]{1,0:T(4,128)S(1)} %pad_add_fusion.table, bf16[2,27,128,128]{3,2,1,0:T(8,128)(2,1)S(1)} %copy-done), custom_call_target="tpu_custom_call" | custom-call | tf_op jit(solution)/shard_map/own_rows/pallas_call | solution.py:104
  4.2 0.6 collective-permute-start
  4.7 3.3 %collective-permute-done.part = bf16[2,27,128,128]{3,2,1,0:T(8,128)(2,1)S(1)} collective-permute-done((bf16[2,27,128,128]{3,2,1,0:T(8,128)(2,1)S(1)}, bf16[2,27,128,128]{3,2,1,0:T(8,128)(2,1)S(1)}, u32[]{:S(2)}, u32[]{:S(2)}) %collective-permute-start) | collective-permute-done | bytes 1769504 | tf_op jit(solution)/shard_map/ppermute | solution.py:31
  8.1 0.4 first_packs.1
  8.5 0.8 collective-permute-start.1
  9.3 0.8 collective-permute-start.2
  10.1 10.0 %collective-permute-start.3 = (bf16[1,128,128]{2,1,0:T(8,128)(2,1)S(1)}, bf16[1,128,128]{2,1,0:T(8,128)(2,1)S(1)}, u32[]{:S(2)}, u32[]{:S(2)}) collective-permute-start(bf16[1,128,128]{2,1,0:T(8,128)(2,1)S(1)} %get-tuple-element.36), channel_id=1, source_target_pairs={{0,8},{1,6},{4,12},{5,10},{6,1},{8,16},{9,14},{10,5},{11,3},{12,20... | collective-permute-start | bytes 98312 | tf_op jit(solution)/shard_map/ppermute | solution.py:31
  20.1 3.0 %own_part.1 = (bf16[512,512]{1,0:T(8,128)(2,1)S(1)}, f32[256,512]{1,0:T(8,128)S(1)}, bf16[512,1792]{1,0:T(8,128)(2,1)S(1)}, bf16[512,1280]{1,0:T(8,128)(2,1)S(1)}, f32[2,128]{1,0:T(2,128)S(1)}) custom-call(bf16[2,27,128,128]{3,2,1,0:T(8,128)(2,1)S(1)} %get-tuple-element.28.mine, bf16[2,27,128,128]{3,2,1,0:T(8,128)(2,1)S(1)} %collective-permute-done.part), custom_call_target="tpu_custom_call" | custom-call | flops 2000000000 | bytes 1000000 | tf_op jit(solution)/shard_map/own_part/pallas_call | solution.py:267
  23.1 0.3 second_packs.1
  23.5 1.3 %collective-permute-start.4 = (bf16[45,128,128]{2,1,0:T(8,128)(2,1)S(1)}, bf16[45,128,128]{2,1,0:T(8,128)(2,1)S(1)}, u32[]{:S(2)}, u32[]{:S(2)}) collective-permute-start(bf16[45,128,128]{2,1,0:T(8,128)(2,1)S(1)} %join_cross.1), channel_id=1, source_target_pairs={{1,0},{2,3},{5,4},{6,7},{9,8},{10,11},{13,12},{14,15},{17,16},{18,... | collective-permute-start | bytes 4423688 | tf_op jit(solution)/shard_map/ppermute | solution.py:31
  24.8 1.3 %collective-permute-start.9 = (bf16[42,128,128]{2,1,0:T(8,128)(2,1)S(1)}, bf16[42,128,128]{2,1,0:T(8,128)(2,1)S(1)}, u32[]{:S(2)}, u32[]{:S(2)}) collective-permute-start(bf16[42,128,128]{2,1,0:T(8,128)(2,1)S(1)} %get-tuple-element.43), channel_id=1, source_target_pairs={{1,3},{2,0},{5,7},{6,4},{9,11},{10,8},{13,15},{14,12},{17,19},{18,... | collective-permute-start | bytes 4128776 | tf_op jit(solution)/shard_map/ppermute | solution.py:31
  26.1 0.7 collective-permute-start.10
  26.9 0.7 collective-permute-start.12
  27.6 0.9 %collective-permute-start.11 = (bf16[14,128,128]{2,1,0:T(8,128)(2,1)S(1)}, bf16[14,128,128]{2,1,0:T(8,128)(2,1)S(1)}, u32[]{:S(2)}, u32[]{:S(2)}) collective-permute-start(bf16[14,128,128]{2,1,0:T(8,128)(2,1)S(1)} %get-tuple-element.39._), channel_id=1, source_target_pairs={{2,4},{5,3},{6,8},{9,7},{10,12},{13,11},{14,16},{17,15},{18,20},{2... | collective-permute-start | bytes 1376264 | tf_op jit(solution)/shard_map/ppermute | solution.py:31
  28.4 1.5 %cross_part.1 = (f32[512,1280]{1,0:T(8,128)S(1)}, f32[2,128]{1,0:T(2,128)S(1)}) custom-call(bf16[512,1792]{1,0:T(8,128)(2,1)S(1)} %get-tuple-element.30.near_rows, bf16[512,1280]{1,0:T(8,128)(2,1)S(1)} %get-tuple-element.32.far_rows, f32[2,128]{1,0:T(2,128)S(1)} %get-tuple-element.33.before._, bf16[72,128,128]{2,1,0:T(8,128)(2,1)S(1)} %collective-permute-done.1.x1, ...), custom_call_target="tpu_custom_call" | custom-call | flops 1000000000 | bytes 1000000 | tf_op jit(solution)/shard_map/cross_part/pallas_call | solution.py:315
  30.0 15.5 %collective-permute-done.4.swapped = bf16[45,128,128]{2,1,0:T(8,128)(2,1)S(1)} collective-permute-done((bf16[45,128,128]{2,1,0:T(8,128)(2,1)S(1)}, bf16[45,128,128]{2,1,0:T(8,128)(2,1)S(1)}, u32[]{:S(2)}, u32[]{:S(2)}) %collective-permute-start.4) | collective-permute-done | bytes 1474592 | tf_op jit(solution)/shard_map/ppermute | solution.py:31
  45.5 7.6 %collective-permute-start.5 = (f32[2]{0:T(128)S(1)}, f32[2]{0:T(128)S(1)}, u32[]{:S(2)}, u32[]{:S(2)}) collective-permute-start(f32[2]{0:T(128)S(1)} %slice_reduce_fusion), channel_id=1, source_target_pairs={{0,1},{1,0},{2,3},{3,2},{4,5},{5,4},{6,7},{7,6},{8,9},{9,8},{10,11... | collective-permute-start | bytes 32 | tf_op jit(solution)/shard_map/ppermute | solution.py:31
  53.1 2.3 %mid_part.1.partial = f32[512,1792]{1,0:T(8,128)S(1)} custom-call(bf16[512,512]{1,0:T(8,128)(2,1)S(1)} %get-tuple-element.31.own, bf16[512,1792]{1,0:T(8,128)(2,1)S(1)} %get-tuple-element.30.near_rows, bf16[512,1280]{1,0:T(8,128)(2,1)S(1)} %get-tuple-element.32.far_rows, f32[512,1280]{1,0:T(8,128)S(1)} %get-tuple-element.37.first, ...), custom_call_target="tpu_custom_call" | custom-call | flops 2000000000 | bytes 1000000 | tf_op jit(solution)/shard_map/mid_part/pallas_call | solution.py:343
  55.4 5.6 %collective-permute-start.6 = (f32[2]{0:T(128)S(1)}, f32[2]{0:T(128)S(1)}, u32[]{:S(2)}, u32[]{:S(2)}) collective-permute-start(f32[2]{0:T(128)S(1)} %add.23), channel_id=1, source_target_pairs={{0,16},{1,17},{2,18},{3,19},{4,20},{5,21},{6,22},{7,23},{8,24},{9,... | collective-permute-start | bytes 32 | tf_op jit(solution)/shard_map/ppermute | solution.py:31
  60.9 1.5 %collective-permute-done.6 = f32[2]{0:T(128)S(1)} collective-permute-done((f32[2]{0:T(128)S(1)}, f32[2]{0:T(128)S(1)}, u32[]{:S(2)}, u32[]{:S(2)}) %collective-permute-start.6) | collective-permute-done | bytes 40 | tf_op jit(solution)/shard_map/ppermute | solution.py:31
  62.5 3.5 %collective-permute-done.7 = f32[2]{0:T(128)S(1)} collective-permute-done((f32[2]{0:T(128)S(1)}, f32[2]{0:T(128)S(1)}, u32[]{:S(2)}, u32[]{:S(2)}) %collective-permute-start.7) | collective-permute-done | bytes 40 | tf_op jit(solution)/shard_map/ppermute | solution.py:31
  66.0 3.6 %collective-permute-start.8 = (f32[2]{0:T(128)S(1)}, f32[2]{0:T(128)S(1)}, u32[]{:S(2)}, u32[]{:S(2)}) collective-permute-start(f32[2]{0:T(128)S(1)} %add.25), channel_id=1, source_target_pairs={{0,4},{1,5},{2,6},{3,7},{4,0},{5,1},{6,2},{7,3},{8,12},{9,13},{10,... | collective-permute-start | bytes 32 | tf_op jit(solution)/shard_map/ppermute | solution.py:31
  69.6 1.6 %collective-permute-done.8 = f32[2]{0:T(128)S(1)} collective-permute-done((f32[2]{0:T(128)S(1)}, f32[2]{0:T(128)S(1)}, u32[]{:S(2)}, u32[]{:S(2)}) %collective-permute-start.8) | collective-permute-done | bytes 40 | tf_op jit(solution)/shard_map/ppermute | solution.py:31
  71.2 2.0 %away_part.1 = (bf16[21,128,128]{2,1,0:T(8,128)(2,1)S(1)}, bf16[512,1792]{1,0:T(8,128)(2,1)S(1)}, bf16[512,1280]{1,0:T(8,128)(2,1)S(1)}, bf16[768,768]{1,0:T(8,128)(2,1)S(1)}) custom-call(bf16[512,1792]{1,0:T(8,128)(2,1)S(1)} %get-tuple-element.30.near_rows, f32[512,1792]{1,0:T(8,128)S(1)} %mid_part.1.partial, ...), custom_call_target="tpu_custom_call" | custom-call | flops 2000000000 | bytes 1000000 | tf_op jit(solution)/shard_map/away_part/pallas_call | solution.py:412
  73.2 3.9 %collective-permute-start.13 = (bf16[21,128,128]{2,1,0:T(8,128)(2,1)S(1)}, bf16[21,128,128]{2,1,0:T(8,128)(2,1)S(1)}, u32[]{:S(2)}, u32[]{:S(2)}) collective-permute-start(bf16[21,128,128]{2,1,0:T(8,128)(2,1)S(1)} %get-tuple-element.46), channel_id=1, source_target_pairs={{0,1},{1,0},{2,3},{3,2},{4,5},{5,4},{6,7},{7,6},{8,9},{9,8},{10,11... | collective-permute-start | bytes 2064392 | tf_op jit(solution)/shard_map/ppermute | solution.py:31
  77.1 0.6 collective-permute-start.14
  77.7 3.1 %near_part.1._ = bf16[2,27,128,128]{3,2,1,0:T(8,128)(2,1)} custom-call(s32[2,27,1,128]{3,2,1,0:T(1,128)S(1)} %get-tuple-element.27.mask, bf16[512,1792]{1,0:T(8,128)(2,1)S(1)} %get-tuple-element.30.near_rows, f32[512,1792]{1,0:T(8,128)S(1)} %mid_part.1.partial, f32[256,512]{1,0:T(8,128)S(1)} %get-tuple-element.47.inner, ...), custom_call_target="tpu_custom_call" | custom-call | flops 1000000000 | bytes 1000000 | tf_op jit(solution)/shard_map/near_part/pallas_call | solution.py:439
  80.8 0.8 collective-permute-done.14
  81.5 0.5 add.27
  82.1 1.1 %join.1 = bf16[2,27,128,128]{3,2,1,0:T(8,128)(2,1)} custom-call(s32[2,27,1,128]{3,2,1,0:T(1,128)S(1)} %get-tuple-element.27.mask, bf16[21,128,128]{2,1,0:T(8,128)(2,1)S(1)} %collective-permute-done.13.came, bf16[2,27,128,128]{3,2,1,0:T(8,128)(2,1)} %near_part.1._), custom_call_target="tpu_custom_call", output_to_operand_aliasing={{}: (2, {})} | custom-call | tf_op jit(solution)/shard_map/join/pallas_call | solution.py:476
  (17 shorter events, 0.3 us)
Async XLA Ops:
  1.3 1.5 %copy-start = (bf16[2,27,128,128]{3,2,1,0:T(8,128)(2,1)S(1)}, bf16[2,27,128,128]{3,2,1,0:T(8,128)(2,1)}, u32[]{:S(2)}) copy-start(bf16[2,27,128,128]{3,2,1,0:T(8,128)(2,1)} %blocks.1) | copy-start | bytes 5308420
  4.2 3.9 %collective-permute-start = (bf16[2,27,128,128]{3,2,1,0:T(8,128)(2,1)S(1)}, bf16[2,27,128,128]{3,2,1,0:T(8,128)(2,1)S(1)}, u32[]{:S(2)}, u32[]{:S(2)}) collective-permute-start(bf16[2,27,128,128]{3,2,1,0:T(8,128)(2,1)S(1)} %get-tuple-element.29), channel_id=1, source_target_pairs={{0,1},{1,0},{2,3},{3,2},{4,5},{5,4},{6,7},{7,6},{8,9},{9,8},{10,11... | collective-permute-start | bytes 5308424 | tf_op jit(solution)/shard_map/ppermute | solution.py:31
  8.5 14.7 %collective-permute-start.1 = (bf16[72,128,128]{2,1,0:T(8,128)(2,1)S(1)}, bf16[72,128,128]{2,1,0:T(8,128)(2,1)S(1)}, u32[]{:S(2)}, u32[]{:S(2)}) collective-permute-start(bf16[72,128,128]{2,1,0:T(8,128)(2,1)S(1)} %get-tuple-element.34), channel_id=1, source_target_pairs={{1,2},{2,1},{5,6},{6,5},{9,10},{10,9},{13,14},{14,13},{17,18},{18,... | collective-permute-start | bytes 7077896 | tf_op jit(solution)/shard_map/ppermute | solution.py:31
  9.3 13.8 %collective-permute-start.2 = (bf16[64,128,128]{2,1,0:T(8,128)(2,1)S(1)}, bf16[64,128,128]{2,1,0:T(8,128)(2,1)S(1)}, u32[]{:S(2)}, u32[]{:S(2)}) collective-permute-start(bf16[64,128,128]{2,1,0:T(8,128)(2,1)S(1)} %get-tuple-element.35), channel_id=1, source_target_pairs={{3,6},{4,1},{7,10},{8,5},{11,14},{12,9},{15,18},{16,13},{19,22},{2... | collective-permute-start | bytes 6291464 | tf_op jit(solution)/shard_map/ppermute | solution.py:31
  10.1 13.3 %collective-permute-start.3 = (bf16[1,128,128]{2,1,0:T(8,128)(2,1)S(1)}, bf16[1,128,128]{2,1,0:T(8,128)(2,1)S(1)}, u32[]{:S(2)}, u32[]{:S(2)}) collective-permute-start(bf16[1,128,128]{2,1,0:T(8,128)(2,1)S(1)} %get-tuple-element.36), channel_id=1, source_target_pairs={{0,8},{1,6},{4,12},{5,10},{6,1},{8,16},{9,14},{10,5},{11,3},{12,20... | collective-permute-start | bytes 98312 | tf_op jit(solution)/shard_map/ppermute | solution.py:31
  23.5 22.0 %collective-permute-start.4 = (bf16[45,128,128]{2,1,0:T(8,128)(2,1)S(1)}, bf16[45,128,128]{2,1,0:T(8,128)(2,1)S(1)}, u32[]{:S(2)}, u32[]{:S(2)}) collective-permute-start(bf16[45,128,128]{2,1,0:T(8,128)(2,1)S(1)} %join_cross.1), channel_id=1, source_target_pairs={{1,0},{2,3},{5,4},{6,7},{9,8},{10,11},{13,12},{14,15},{17,16},{18,... | collective-permute-start | bytes 4423688 | tf_op jit(solution)/shard_map/ppermute | solution.py:31
  24.8 46.4 %collective-permute-start.9 = (bf16[42,128,128]{2,1,0:T(8,128)(2,1)S(1)}, bf16[42,128,128]{2,1,0:T(8,128)(2,1)S(1)}, u32[]{:S(2)}, u32[]{:S(2)}) collective-permute-start(bf16[42,128,128]{2,1,0:T(8,128)(2,1)S(1)} %get-tuple-element.43), channel_id=1, source_target_pairs={{1,3},{2,0},{5,7},{6,4},{9,11},{10,8},{13,15},{14,12},{17,19},{18,... | collective-permute-start | bytes 4128776 | tf_op jit(solution)/shard_map/ppermute | solution.py:31
  26.1 45.0 %collective-permute-start.10 = (bf16[34,128,128]{2,1,0:T(8,128)(2,1)S(1)}, bf16[34,128,128]{2,1,0:T(8,128)(2,1)S(1)}, u32[]{:S(2)}, u32[]{:S(2)}) collective-permute-start(bf16[34,128,128]{2,1,0:T(8,128)(2,1)S(1)} %get-tuple-element.44), channel_id=1, source_target_pairs={{1,4},{5,8},{6,3},{9,12},{10,7},{13,16},{14,11},{17,20},{18,15},{2... | collective-permute-start | bytes 3342344 | tf_op jit(solution)/shard_map/ppermute | solution.py:31
  26.9 44.3 %collective-permute-start.12 = (bf16[15,128,128]{2,1,0:T(8,128)(2,1)S(1)}, bf16[15,128,128]{2,1,0:T(8,128)(2,1)S(1)}, u32[]{:S(2)}, u32[]{:S(2)}) collective-permute-start(bf16[15,128,128]{2,1,0:T(8,128)(2,1)S(1)} %get-tuple-element.45), channel_id=1, source_target_pairs={{2,6},{5,1},{6,10},{9,5},{10,14},{13,9},{14,18},{17,13},{18,22},{2... | collective-permute-start | bytes 1474568 | tf_op jit(solution)/shard_map/ppermute | solution.py:31
  27.6 43.6 %collective-permute-start.11 = (bf16[14,128,128]{2,1,0:T(8,128)(2,1)S(1)}, bf16[14,128,128]{2,1,0:T(8,128)(2,1)S(1)}, u32[]{:S(2)}, u32[]{:S(2)}) collective-permute-start(bf16[14,128,128]{2,1,0:T(8,128)(2,1)S(1)} %get-tuple-element.39._), channel_id=1, source_target_pairs={{2,4},{5,3},{6,8},{9,7},{10,12},{13,11},{14,16},{17,15},{18,20},{2... | collective-permute-start | bytes 1376264 | tf_op jit(solution)/shard_map/ppermute | solution.py:31
  45.5 9.8 %collective-permute-start.5 = (f32[2]{0:T(128)S(1)}, f32[2]{0:T(128)S(1)}, u32[]{:S(2)}, u32[]{:S(2)}) collective-permute-start(f32[2]{0:T(128)S(1)} %slice_reduce_fusion), channel_id=1, source_target_pairs={{0,1},{1,0},{2,3},{3,2},{4,5},{5,4},{6,7},{7,6},{8,9},{9,8},{10,11... | collective-permute-start | bytes 32 | tf_op jit(solution)/shard_map/ppermute | solution.py:31
  55.4 7.1 %collective-permute-start.6 = (f32[2]{0:T(128)S(1)}, f32[2]{0:T(128)S(1)}, u32[]{:S(2)}, u32[]{:S(2)}) collective-permute-start(f32[2]{0:T(128)S(1)} %add.23), channel_id=1, source_target_pairs={{0,16},{1,17},{2,18},{3,19},{4,20},{5,21},{6,22},{7,23},{8,24},{9,... | collective-permute-start | bytes 32 | tf_op jit(solution)/shard_map/ppermute | solution.py:31
  62.5 3.5 %collective-permute-start.7 = (f32[2]{0:T(128)S(1)}, f32[2]{0:T(128)S(1)}, u32[]{:S(2)}, u32[]{:S(2)}) collective-permute-start(f32[2]{0:T(128)S(1)} %add.24), channel_id=1, source_target_pairs={{0,2},{1,3},{2,0},{3,1},{4,6},{5,7},{6,4},{7,5},{8,10},{9,11},{10,... | collective-permute-start | bytes 32 | tf_op jit(solution)/shard_map/ppermute | solution.py:31
  66.0 5.1 %collective-permute-start.8 = (f32[2]{0:T(128)S(1)}, f32[2]{0:T(128)S(1)}, u32[]{:S(2)}, u32[]{:S(2)}) collective-permute-start(f32[2]{0:T(128)S(1)} %add.25), channel_id=1, source_target_pairs={{0,4},{1,5},{2,6},{3,7},{4,0},{5,1},{6,2},{7,3},{8,12},{9,13},{10,... | collective-permute-start | bytes 32 | tf_op jit(solution)/shard_map/ppermute | solution.py:31
  73.2 8.9 %collective-permute-start.13 = (bf16[21,128,128]{2,1,0:T(8,128)(2,1)S(1)}, bf16[21,128,128]{2,1,0:T(8,128)(2,1)S(1)}, u32[]{:S(2)}, u32[]{:S(2)}) collective-permute-start(bf16[21,128,128]{2,1,0:T(8,128)(2,1)S(1)} %get-tuple-element.46), channel_id=1, source_target_pairs={{0,1},{1,0},{2,3},{3,2},{4,5},{5,4},{6,7},{7,6},{8,9},{9,8},{10,11... | collective-permute-start | bytes 2064392 | tf_op jit(solution)/shard_map/ppermute | solution.py:31
  77.1 4.4 %collective-permute-start.14 = (f32[2]{0:T(128)S(1)}, f32[2]{0:T(128)S(1)}, u32[]{:S(2)}, u32[]{:S(2)}) collective-permute-start(f32[2]{0:T(128)S(1)} %add.26), channel_id=1, source_target_pairs={{0,8},{1,9},{2,10},{3,11},{4,12},{5,13},{6,14},{7,15},{8,0},{9,1},... | collective-permute-start | bytes 32 | tf_op jit(solution)/shard_map/ppermute | solution.py:31

commit v5 on v4

--- a/solution.py
+++ b/solution.py
@@ -76,7 +76,7 @@
     return lax.rem(lax.div(index, 2) + lax.rem(index, 2), 2) > 0
 
 
-def own_kernel(table, blocks, mine, other, mask, flags):
+def own_kernel(table, blocks, mine, soon, later, mask, flags):
     core = my_core()
     first_row = 2 * (lax.axis_index("row") * lax.axis_size("col") + lax.axis_index("col"))
     for r in range(2):
@@ -88,24 +88,38 @@
         def _(n):
             flags[r, table[r, n] - first_row - r + HALF] = 1
 
+    def block(e, w):
+        r = jnp.where(core > 0, 1 - e, e)
+        a = jnp.where(core > 0, BAND - 1 - w, w)
+        return jnp.where(flags[r, a] > 0, blocks[r, a], jnp.zeros((BS, BS), blocks.dtype))
+
     for r in range(2):
-        e = jnp.where(core > 0, 1 - r, r)
         for a in range(BAND):
-            keep = flags[r, a]
-            mask[r, a] = jnp.full((1, BS), keep, jnp.int32)
-            x = jnp.where(keep > 0, blocks[r, a], jnp.zeros((BS, BS), blocks.dtype))
-            w = jnp.where(core > 0, BAND - 1 - a, a)
-            mine[e, w] = x
-            other[1 - e, BAND - 1 - w] = x
+            mask[r, a] = jnp.full((1, BS), flags[r, a], jnp.int32)
+    for p in range(2):
+        for w in range(BAND):
+            mine[p, w] = block(p, w)
+    for out, first in ((soon, True), (later, False)):
+        for n, (p, w) in enumerate(part_slots(first)):
+            out[n] = block(1 - p, BAND - 1 - w)
+
+
+def part_slots(first):
+    soon = [set(range(9 - e)) | set(range(HALF, BAND - 1 - e)) | {HALF - 1 - e} for e in (2, 3)]
+    return [(p, w) for p in range(2) for w in range(BAND) if (w in soon[p]) == first]
 
 
 def own_rows(table, blocks):
     shape = jax.ShapeDtypeStruct(blocks.shape, blocks.dtype)
+    parts = [
+        jax.ShapeDtypeStruct((len(part_slots(first)), BS, BS), blocks.dtype)
+        for first in (True, False)
+    ]
     return pl.pallas_call(
         own_kernel,
-        out_shape=(shape, shape, jax.ShapeDtypeStruct((2, BAND, 1, BS), jnp.int32)),
+        out_shape=(shape, *parts, jax.ShapeDtypeStruct((2, BAND, 1, BS), jnp.int32)),
         in_specs=[SM, VM],
-        out_specs=(VM, VM, VM),
+        out_specs=(VM,) * 4,
         scratch_shapes=[pltpu.SMEM((2, BAND), jnp.int32)],
         compiler_params=params(),
         name="own_rows",
@@ -116,13 +130,13 @@
     return [w for w in range(HALF, BAND - 1 - e) if e < 3 or not 5 <= w - HALF + 1 + e <= 8]
 
 
-def first_kernel(mine, part, x1, z1, z2, single):
+def first_kernel(mine, soon, x1, z1, z2, single):
     at = {}
 
     def put(out, e, slots):
         for w in slots:
             n = at.get(id(out), 0)
-            out[n] = mine[e, w] if e < 2 else part[e - 2, w]
+            out[n] = mine[e, w] if e < 2 else soon[part_slots(True).index((e - 2, w))]
             at[id(out)] = n + 1
 
     for e in range(4):
@@ -138,10 +152,10 @@
     for e in range(4):
         put(z1, e, range(HALF - 1 - e, HALF - e))
         put(z2, e, range(HALF - 1 - e, HALF - e))
-    single[0] = jnp.where(faces_pair(), mine[0, 0], part[1, HALF])
-
-
-def first_packs(mine, part):
+    single[0] = jnp.where(faces_pair(), mine[0, 0], soon[part_slots(True).index((1, HALF))])
+
+
+def first_packs(mine, soon):
     return pl.pallas_call(
         first_kernel,
         out_shape=[jax.ShapeDtypeStruct((n, BS, BS), mine.dtype) for n in (72, 64, 34, 1)],
@@ -149,7 +163,7 @@
         out_specs=[VM] * 4,
         compiler_params=params(),
         name="first_packs",
-    )(mine, part)
+    )(mine, soon)
 
 
 def second_kernel(x1, z1, _, x2, g, h):
@@ -202,14 +216,18 @@
     return jnp.transpose(x.astype(jnp.float32)).astype(x.dtype)
 
 
-def fill_rows(mine, part, rows):
+def fill_rows(mine, soon, later, rows):
     zero = jnp.zeros((BS, BS), rows.dtype)
 
     def block(e, k):
         w = k - e + HALF
         if not 0 <= w < BAND:
             return zero
-        return mine[e, w] if e < 2 else part[e - 2, w]
+        if e < 2:
+            return mine[e, w]
+        for part, first in ((soon, True), (later, False)):
+            if (e - 2, w) in part_slots(first):
+                return part[part_slots(first).index((e - 2, w))]
 
     for e in range(4):
         for t in range(1, NCOL + 1):
@@ -239,8 +257,8 @@
     return sum(10 - s for s in range(1, t))
 
 
-def own_kernel_products(mine, part, own_rows, inner, near_rows, far_rows, sums, rows):
-    fill_rows(mine, part, rows)
+def own_kernel_products(mine, soon, later, own_rows, inner, near_rows, far_rows, sums, rows):
+    fill_rows(mine, soon, later, rows)
     own_rows[...] = rows[:, OWN_AT:FAR_AT]
     near_rows[...] = rows[:, :NEAR_W]
     far_rows[...] = rows[:, FAR_AT : FAR_AT + 10 * BS]
@@ -263,7 +281,7 @@
     sums[1:2, :] = jnp.broadcast_to(third, (1, BS))
 
 
-def own_part(mine, part):
+def own_part(mine, soon, later):
     return pl.pallas_call(
         own_kernel_products,
         out_shape=(
@@ -273,13 +291,13 @@
             jax.ShapeDtypeStruct((4 * BS, 10 * BS), mine.dtype),
             jax.ShapeDtypeStruct((2, BS), jnp.float32),
         ),
-        in_specs=[VM] * 2,
+        in_specs=[VM] * 3,
         out_specs=(VM,) * 5,
         scratch_shapes=[pltpu.VMEM((4 * BS, FAR_AT + FAR_W), mine.dtype)],
         compiler_params=params(),
         cost_estimate=pl.CostEstimate(flops=2 * 10**9, bytes_accessed=10**6, transcendentals=0),
         name="own_part",
-    )(mine, part)
+    )(mine, soon, later)
 
 
 def fill_cross(block, pairs):
@@ -420,19 +438,34 @@
     )(near_rows, partial, x1, x2, z1, z2, g, h, single)
 
 
-def near_kernel(mask, near_rows, partial, inner, pairs1, pairs2, pairs3, out):
+def near_kernel(mask, near_rows, partial, inner, pairs1, pairs2, pairs3, out, held, sems):
     core = my_core()
+    copies = []
 
     def put(e, w, value):
         r = jnp.where(core > 0, 1 - e, e)
         a = jnp.where(core > 0, BAND - 1 - w, w)
-        out[r, a] = jnp.where(mask[r, a] > 0, value, 0.0).astype(out.dtype)
+        held[r, a] = jnp.where(mask[r, a] > 0, value, 0.0).astype(held.dtype)
+
+    def send(e, lo, n):
+        r = jnp.where(core > 0, 1 - e, e)
+        part = pl.ds(jnp.where(core > 0, BAND - lo - n, lo), n)
+        copy = pltpu.make_async_copy(held.at[r, part], out.at[r, part], sems.at[len(copies)])
+        copy.start()
+        copies.append(copy)
 
     for e in range(2):
         for k in range(4):
             put(e, k - e + HALF, inner[cut(e), cut(k)])
+        send(e, HALF - e, 4)
     for e, t, value in near_products(0, near_rows, partial, pairs1, pairs2, pairs3):
         put(e, HALF - e - t, value)
+        if t % 2 == 0:
+            send(e, HALF - e - t, 2)
+        elif e + t == HALF:
+            send(e, 0, 1)
+    for copy in copies:
+        copy.wait()
 
 
 def near_part(mask, near_rows, partial, inner, *pairs):
@@ -440,7 +473,11 @@
         near_kernel,
         out_shape=jax.ShapeDtypeStruct((2, BAND, BS, BS), near_rows.dtype),
         in_specs=[VM] * 7,
-        out_specs=VM,
+        out_specs=HB,
+        scratch_shapes=[
+            pltpu.VMEM((2, BAND, BS, BS), near_rows.dtype),
+            pltpu.SemaphoreType.DMA((16,)),
+        ],
         compiler_params=params(),
         cost_estimate=pl.CostEstimate(flops=10**9, bytes_accessed=10**6, transcendentals=0),
         name="near_part",
@@ -490,13 +527,13 @@
 
 def body(blocks, columns, counts):
     table = jnp.pad(columns, ((0, 1), (0, 0))) + jnp.pad(counts[None], ((2, 0), (0, BAND - 2)))
-    mine, other, mask = own_rows(table, blocks)
-    part = to_partner(other)
+    mine, soon, later, mask = own_rows(table, blocks)
+    soon, later = to_partner(soon), to_partner(later)
 
     def outer(i):
         return not inner(i)
 
-    x1, z1, z2, single = first_packs(mine, part)
+    x1, z1, z2, single = first_packs(mine, soon)
     x1 = to_side(x1, 1, inner)
     z1 = to_side(z1, 2, outer)
 
@@ -507,7 +544,7 @@
         return 2 * (chip - 4) + 1 if core else 2 * (chip + 4)
 
     single = permute(single, singles)
-    own, inside, near_rows, far_rows, sums = own_part(mine, part)
+    own, inside, near_rows, far_rows, sums = own_part(mine, soon, later)
 
     x2, g, h = second_packs(x1, z1, sums)
     swapped = permute(join_cross(x1, z1, single, g), lambda i: i ^ 1 if inner(i) else -1)
@@ -527,13 +564,13 @@
     first, sums = cross_part(near_rows, far_rows, sums, x1, z1, single)
     sums, swapped = lax.optimization_barrier((sums[:, 0], swapped))
     steps = [1 << n for n in range(lax.axis_size(AXES).bit_length() - 1)]
-    sums = sum_over(sums, steps[:1] + steps[4:] + steps[1:3])
+    sums = sum_over(sums, steps[:1] + steps[4:] + steps[1:2] + steps[3:4])
     partial = mid_part(own, near_rows, far_rows, first, swapped)
     partial, sums = lax.optimization_barrier((partial, sums))
     away, *pairs = away_part(near_rows, partial, x1, x2, z1, z2, g, h, single)
     came = to_partner(away)
     out = near_part(mask, near_rows, partial, inside, *pairs)
-    traces = sum_over(sums, steps[3:4])
+    traces = sum_over(sums, steps[2:3])
     square = join(mask, came, out)
     return square, traces
 

time: 83.6 us -> 82.4 us (0.986)
  waiting for transfers between devices: 26.2 us -> 24.8 us
    ppermute x15 -> x16, waiting for transfers between devices: 26.2 us -> 24.8 us  [permute(): lax.ppermute(value, AXES, [(i, j) for i, j in pairs if 0 <= j < devices])]
    ppermute x15 -> x16, starting transfers between devices: 38.3 us -> 38.6 us  [permute(): lax.ppermute(value, AXES, [(i, j) for i, j in pairs if 0 <= j < devices])]
  transfers between devices with their start and end apart: 15 -> 16, of which waited for: 6 -> 6; matrix products, arithmetic and copies ran while one was open for 1% -> 1% of each run, Pallas kernels for 12% -> 12%
where the time goes in v5:
time: 82.4 us; the launch traced here: 82 us
  starting transfers between devices  38.6 us (47%)
  waiting for transfers between devices  24.8 us (30%)
  Pallas kernels  14.9 us (18%)
  local copies, waits for them, and re-layouts  1.59 us (2%)
  other arithmetic  1.23 us (1%)
  between operations  0.99 us (1%)
    ppermute x16, starting transfers between devices, permute(): lax.ppermute(value, AXES, [(i, j) for i, j in pairs if 0 <= j < devices])  38.6 us
    ppermute x16, waiting for transfers between devices, permute(): lax.ppermute(value, AXES, [(i, j) for i, j in pairs if 0 <= j < devices])  24.8 us
    pallas_call x1, Pallas kernels, own_part(): pl.pallas_call(own_kernel_products, out_shape=(jax.ShapeDtypeStruct((4 *...  2.97 us
    pallas_call x1, Pallas kernels, near_part(): pl.pallas_call(near_kernel, out_shape=jax.ShapeDtypeStruct((2, BAND, BS,...  2.67 us
    pallas_call x1, Pallas kernels, mid_part(): pl.pallas_call(mid_kernel, out_shape=jax.ShapeDtypeStruct(near_rows.shape...  2.26 us
    pallas_call x1, Pallas kernels, away_part(): pl.pallas_call(away_kernel, out_shape=[jax.ShapeDtypeStruct(shape, x1.dty...  1.98 us
    pallas_call x1, Pallas kernels, own_rows(): pl.pallas_call(own_kernel, out_shape=(shape, *parts, jax.ShapeDtypeStruct...  1.68 us
  transfers between devices with their start and end apart: 16, of which 6 were waited for; matrix products, arithmetic and copies ran while one was open for 1% of the time, Pallas kernels for 12%

profile of v5, /device:TPU:0, one launch (start us, length us, event | category | flops | bytes accessed | tf_op | source)
XLA Modules:
  0.0 82.0 jit_solution(11344786104803360207)
XLA Ops:
  0.6 0.7 pad_add_fusion.table
  1.3 1.5 %copy-done = bf16[2,27,128,128]{3,2,1,0:T(8,128)(2,1)S(1)} copy-done((bf16[2,27,128,128]{3,2,1,0:T(8,128)(2,1)S(1)}, bf16[2,27,128,128]{3,2,1,0:T(8,128)(2,1)}, u32[]{:S(2)}) %copy-start) | copy-done | bytes 1769496
  2.8 1.7 %own_rows.1 = (bf16[2,27,128,128]{3,2,1,0:T(8,128)(2,1)S(1)}, bf16[36,128,128]{2,1,0:T(8,128)(2,1)S(1)}, bf16[18,128,128]{2,1,0:T(8,128)(2,1)S(1)}, s32[2,27,1,128]{3,2,1,0:T(1,128)S(1)}) custom-call(s32[3,27]{1,0:T(4,128)S(1)} %pad_add_fusion.table, bf16[2,27,128,128]{3,2,1,0:T(8,128)(2,1)S(1)} %copy-done), custom_call_target="tpu_custom_call" | custom-call | tf_op jit(solution)/shard_map/own_rows/pallas_call | solution.py:118
  4.5 0.6 collective-permute-start
  5.1 2.5 %collective-permute-done.soon = bf16[36,128,128]{2,1,0:T(8,128)(2,1)S(1)} collective-permute-done((bf16[36,128,128]{2,1,0:T(8,128)(2,1)S(1)}, bf16[36,128,128]{2,1,0:T(8,128)(2,1)S(1)}, u32[]{:S(2)}, u32[]{:S(2)}) %collective-permute-start) | collective-permute-done | bytes 1179680 | tf_op jit(solution)/shard_map/ppermute | solution.py:31
  7.5 0.4 first_packs.1
  7.9 0.8 collective-permute-start.2
  8.7 0.8 collective-permute-start.3
  9.5 4.6 %collective-permute-start.1 = (bf16[18,128,128]{2,1,0:T(8,128)(2,1)S(1)}, bf16[18,128,128]{2,1,0:T(8,128)(2,1)S(1)}, u32[]{:S(2)}, u32[]{:S(2)}) collective-permute-start(bf16[18,128,128]{2,1,0:T(8,128)(2,1)S(1)} %get-tuple-element.31), channel_id=1, source_target_pairs={{0,1},{1,0},{2,3},{3,2},{4,5},{5,4},{6,7},{7,6},{8,9},{9,8},{10,11... | collective-permute-start | bytes 1769480 | tf_op jit(solution)/shard_map/ppermute | solution.py:31
  14.2 5.5 %collective-permute-start.4 = (bf16[1,128,128]{2,1,0:T(8,128)(2,1)S(1)}, bf16[1,128,128]{2,1,0:T(8,128)(2,1)S(1)}, u32[]{:S(2)}, u32[]{:S(2)}) collective-permute-start(bf16[1,128,128]{2,1,0:T(8,128)(2,1)S(1)} %get-tuple-element.38), channel_id=1, source_target_pairs={{0,8},{1,6},{4,12},{5,10},{6,1},{8,16},{9,14},{10,5},{11,3},{12,20... | collective-permute-start | bytes 98312 | tf_op jit(solution)/shard_map/ppermute | solution.py:31
  19.7 3.0 %own_part.1 = (bf16[512,512]{1,0:T(8,128)(2,1)S(1)}, f32[256,512]{1,0:T(8,128)S(1)}, bf16[512,1792]{1,0:T(8,128)(2,1)S(1)}, bf16[512,1280]{1,0:T(8,128)(2,1)S(1)}, f32[2,128]{1,0:T(2,128)S(1)}) custom-call(bf16[2,27,128,128]{3,2,1,0:T(8,128)(2,1)S(1)} %get-tuple-element.29.mine, bf16[36,128,128]{2,1,0:T(8,128)(2,1)S(1)} %collective-permute-done.soon, ...), custom_call_target="tpu_custom_call" | custom-call | flops 2000000000 | bytes 1000000 | tf_op jit(solution)/shard_map/own_part/pallas_call | solution.py:285
  22.7 0.3 second_packs.1
  23.0 1.3 %collective-permute-start.5 = (bf16[45,128,128]{2,1,0:T(8,128)(2,1)S(1)}, bf16[45,128,128]{2,1,0:T(8,128)(2,1)S(1)}, u32[]{:S(2)}, u32[]{:S(2)}) collective-permute-start(bf16[45,128,128]{2,1,0:T(8,128)(2,1)S(1)} %join_cross.1), channel_id=1, source_target_pairs={{1,0},{2,3},{5,4},{6,7},{9,8},{10,11},{13,12},{14,15},{17,16},{18,... | collective-permute-start | bytes 4423688 | tf_op jit(solution)/shard_map/ppermute | solution.py:31
  24.3 1.3 %collective-permute-start.10 = (bf16[42,128,128]{2,1,0:T(8,128)(2,1)S(1)}, bf16[42,128,128]{2,1,0:T(8,128)(2,1)S(1)}, u32[]{:S(2)}, u32[]{:S(2)}) collective-permute-start(bf16[42,128,128]{2,1,0:T(8,128)(2,1)S(1)} %get-tuple-element.45), channel_id=1, source_target_pairs={{1,3},{2,0},{5,7},{6,4},{9,11},{10,8},{13,15},{14,12},{17,19},{18,... | collective-permute-start | bytes 4128776 | tf_op jit(solution)/shard_map/ppermute | solution.py:31
  25.6 0.7 collective-permute-start.11
  26.4 0.7 collective-permute-start.13
  27.1 0.9 %collective-permute-start.12 = (bf16[14,128,128]{2,1,0:T(8,128)(2,1)S(1)}, bf16[14,128,128]{2,1,0:T(8,128)(2,1)S(1)}, u32[]{:S(2)}, u32[]{:S(2)}) collective-permute-start(bf16[14,128,128]{2,1,0:T(8,128)(2,1)S(1)} %get-tuple-element.41._), channel_id=1, source_target_pairs={{2,4},{5,3},{6,8},{9,7},{10,12},{13,11},{14,16},{17,15},{18,20},{2... | collective-permute-start | bytes 1376264 | tf_op jit(solution)/shard_map/ppermute | solution.py:31
  28.0 1.5 %cross_part.1 = (f32[512,1280]{1,0:T(8,128)S(1)}, f32[2,128]{1,0:T(2,128)S(1)}) custom-call(bf16[512,1792]{1,0:T(8,128)(2,1)S(1)} %get-tuple-element.32.near_rows, bf16[512,1280]{1,0:T(8,128)(2,1)S(1)} %get-tuple-element.34.far_rows, f32[2,128]{1,0:T(2,128)S(1)} %get-tuple-element.35.before._, bf16[72,128,128]{2,1,0:T(8,128)(2,1)S(1)} %collective-permute-done.2.x1, ...), custom_call_target="tpu_custom_call" | custom-call | flops 1000000000 | bytes 1000000 | tf_op jit(solution)/shard_map/cross_part/pallas_call | solution.py:333
  29.6 15.4 %collective-permute-done.5.swapped = bf16[45,128,128]{2,1,0:T(8,128)(2,1)S(1)} collective-permute-done((bf16[45,128,128]{2,1,0:T(8,128)(2,1)S(1)}, bf16[45,128,128]{2,1,0:T(8,128)(2,1)S(1)}, u32[]{:S(2)}, u32[]{:S(2)}) %collective-permute-start.5) | collective-permute-done | bytes 1474592 | tf_op jit(solution)/shard_map/ppermute | solution.py:31
  45.0 7.7 %collective-permute-start.6 = (f32[2]{0:T(128)S(1)}, f32[2]{0:T(128)S(1)}, u32[]{:S(2)}, u32[]{:S(2)}) collective-permute-start(f32[2]{0:T(128)S(1)} %slice_reduce_fusion), channel_id=1, source_target_pairs={{0,1},{1,0},{2,3},{3,2},{4,5},{5,4},{6,7},{7,6},{8,9},{9,8},{10,11... | collective-permute-start | bytes 32 | tf_op jit(solution)/shard_map/ppermute | solution.py:31
  52.6 2.3 %mid_part.1.partial = f32[512,1792]{1,0:T(8,128)S(1)} custom-call(bf16[512,512]{1,0:T(8,128)(2,1)S(1)} %get-tuple-element.33.own, bf16[512,1792]{1,0:T(8,128)(2,1)S(1)} %get-tuple-element.32.near_rows, bf16[512,1280]{1,0:T(8,128)(2,1)S(1)} %get-tuple-element.34.far_rows, f32[512,1280]{1,0:T(8,128)S(1)} %get-tuple-element.39.first, ...), custom_call_target="tpu_custom_call" | custom-call | flops 2000000000 | bytes 1000000 | tf_op jit(solution)/shard_map/mid_part/pallas_call | solution.py:361
  54.9 5.7 %collective-permute-start.7 = (f32[2]{0:T(128)S(1)}, f32[2]{0:T(128)S(1)}, u32[]{:S(2)}, u32[]{:S(2)}) collective-permute-start(f32[2]{0:T(128)S(1)} %add.23), channel_id=1, source_target_pairs={{0,16},{1,17},{2,18},{3,19},{4,20},{5,21},{6,22},{7,23},{8,24},{9,... | collective-permute-start | bytes 32 | tf_op jit(solution)/shard_map/ppermute | solution.py:31
  60.6 1.5 %collective-permute-done.7 = f32[2]{0:T(128)S(1)} collective-permute-done((f32[2]{0:T(128)S(1)}, f32[2]{0:T(128)S(1)}, u32[]{:S(2)}, u32[]{:S(2)}) %collective-permute-start.7) | collective-permute-done | bytes 40 | tf_op jit(solution)/shard_map/ppermute | solution.py:31
  62.2 3.5 %collective-permute-done.8 = f32[2]{0:T(128)S(1)} collective-permute-done((f32[2]{0:T(128)S(1)}, f32[2]{0:T(128)S(1)}, u32[]{:S(2)}, u32[]{:S(2)}) %collective-permute-start.8) | collective-permute-done | bytes 40 | tf_op jit(solution)/shard_map/ppermute | solution.py:31
  65.7 3.5 %collective-permute-start.9 = (f32[2]{0:T(128)S(1)}, f32[2]{0:T(128)S(1)}, u32[]{:S(2)}, u32[]{:S(2)}) collective-permute-start(f32[2]{0:T(128)S(1)} %add.25), channel_id=1, source_target_pairs={{0,8},{1,9},{2,10},{3,11},{4,12},{5,13},{6,14},{7,15},{8,0},{9,1},... | collective-permute-start | bytes 32 | tf_op jit(solution)/shard_map/ppermute | solution.py:31
  69.2 1.6 %collective-permute-done.9 = f32[2]{0:T(128)S(1)} collective-permute-done((f32[2]{0:T(128)S(1)}, f32[2]{0:T(128)S(1)}, u32[]{:S(2)}, u32[]{:S(2)}) %collective-permute-start.9) | collective-permute-done | bytes 40 | tf_op jit(solution)/shard_map/ppermute | solution.py:31
  70.8 2.0 %away_part.1 = (bf16[21,128,128]{2,1,0:T(8,128)(2,1)S(1)}, bf16[512,1792]{1,0:T(8,128)(2,1)S(1)}, bf16[512,1280]{1,0:T(8,128)(2,1)S(1)}, bf16[768,768]{1,0:T(8,128)(2,1)S(1)}) custom-call(bf16[512,1792]{1,0:T(8,128)(2,1)S(1)} %get-tuple-element.32.near_rows, f32[512,1792]{1,0:T(8,128)S(1)} %mid_part.1.partial, ...), custom_call_target="tpu_custom_call" | custom-call | flops 2000000000 | bytes 1000000 | tf_op jit(solution)/shard_map/away_part/pallas_call | solution.py:430
  72.8 4.0 %collective-permute-start.14 = (bf16[21,128,128]{2,1,0:T(8,128)(2,1)S(1)}, bf16[21,128,128]{2,1,0:T(8,128)(2,1)S(1)}, u32[]{:S(2)}, u32[]{:S(2)}) collective-permute-start(bf16[21,128,128]{2,1,0:T(8,128)(2,1)S(1)} %get-tuple-element.48), channel_id=1, source_target_pairs={{0,1},{1,0},{2,3},{3,2},{4,5},{5,4},{6,7},{7,6},{8,9},{9,8},{10,11... | collective-permute-start | bytes 2064392 | tf_op jit(solution)/shard_map/ppermute | solution.py:31
  76.8 0.6 collective-permute-start.15
  77.4 2.7 %near_part.1._ = bf16[2,27,128,128]{3,2,1,0:T(8,128)(2,1)} custom-call(s32[2,27,1,128]{3,2,1,0:T(1,128)S(1)} %get-tuple-element.28.mask, bf16[512,1792]{1,0:T(8,128)(2,1)S(1)} %get-tuple-element.32.near_rows, f32[512,1792]{1,0:T(8,128)S(1)} %mid_part.1.partial, f32[256,512]{1,0:T(8,128)S(1)} %get-tuple-element.49.inner, ...), custom_call_target="tpu_custom_call" | custom-call | flops 1000000000 | bytes 1000000 | tf_op jit(solution)/shard_map/near_part/pallas_call | solution.py:472
  80.3 0.5 add.27
  80.8 1.1 %join.1 = bf16[2,27,128,128]{3,2,1,0:T(8,128)(2,1)} custom-call(s32[2,27,1,128]{3,2,1,0:T(1,128)S(1)} %get-tuple-element.28.mask, bf16[21,128,128]{2,1,0:T(8,128)(2,1)S(1)} %collective-permute-done.14.came, bf16[2,27,128,128]{3,2,1,0:T(8,128)(2,1)} %near_part.1._), custom_call_target="tpu_custom_call", output_to_operand_aliasing={{}: (2, {})} | custom-call | tf_op jit(solution)/shard_map/join/pallas_call | solution.py:513
  (19 shorter events, 0.5 us)
Async XLA Ops:
  1.3 1.5 %copy-start = (bf16[2,27,128,128]{3,2,1,0:T(8,128)(2,1)S(1)}, bf16[2,27,128,128]{3,2,1,0:T(8,128)(2,1)}, u32[]{:S(2)}) copy-start(bf16[2,27,128,128]{3,2,1,0:T(8,128)(2,1)} %blocks.1) | copy-start | bytes 5308420
  4.5 3.0 %collective-permute-start = (bf16[36,128,128]{2,1,0:T(8,128)(2,1)S(1)}, bf16[36,128,128]{2,1,0:T(8,128)(2,1)S(1)}, u32[]{:S(2)}, u32[]{:S(2)}) collective-permute-start(bf16[36,128,128]{2,1,0:T(8,128)(2,1)S(1)} %get-tuple-element.30), channel_id=1, source_target_pairs={{0,1},{1,0},{2,3},{3,2},{4,5},{5,4},{6,7},{7,6},{8,9},{9,8},{10,11... | collective-permute-start | bytes 3538952 | tf_op jit(solution)/shard_map/ppermute | solution.py:31
  7.9 14.7 %collective-permute-start.2 = (bf16[72,128,128]{2,1,0:T(8,128)(2,1)S(1)}, bf16[72,128,128]{2,1,0:T(8,128)(2,1)S(1)}, u32[]{:S(2)}, u32[]{:S(2)}) collective-permute-start(bf16[72,128,128]{2,1,0:T(8,128)(2,1)S(1)} %get-tuple-element.36), channel_id=1, source_target_pairs={{1,2},{2,1},{5,6},{6,5},{9,10},{10,9},{13,14},{14,13},{17,18},{18,... | collective-permute-start | bytes 7077896 | tf_op jit(solution)/shard_map/ppermute | solution.py:31
  8.7 13.9 %collective-permute-start.3 = (bf16[64,128,128]{2,1,0:T(8,128)(2,1)S(1)}, bf16[64,128,128]{2,1,0:T(8,128)(2,1)S(1)}, u32[]{:S(2)}, u32[]{:S(2)}) collective-permute-start(bf16[64,128,128]{2,1,0:T(8,128)(2,1)S(1)} %get-tuple-element.37), channel_id=1, source_target_pairs={{3,6},{4,1},{7,10},{8,5},{11,14},{12,9},{15,18},{16,13},{19,22},{2... | collective-permute-start | bytes 6291464 | tf_op jit(solution)/shard_map/ppermute | solution.py:31
  9.5 10.1 %collective-permute-start.1 = (bf16[18,128,128]{2,1,0:T(8,128)(2,1)S(1)}, bf16[18,128,128]{2,1,0:T(8,128)(2,1)S(1)}, u32[]{:S(2)}, u32[]{:S(2)}) collective-permute-start(bf16[18,128,128]{2,1,0:T(8,128)(2,1)S(1)} %get-tuple-element.31), channel_id=1, source_target_pairs={{0,1},{1,0},{2,3},{3,2},{4,5},{5,4},{6,7},{7,6},{8,9},{9,8},{10,11... | collective-permute-start | bytes 1769480 | tf_op jit(solution)/shard_map/ppermute | solution.py:31
  14.2 8.8 %collective-permute-start.4 = (bf16[1,128,128]{2,1,0:T(8,128)(2,1)S(1)}, bf16[1,128,128]{2,1,0:T(8,128)(2,1)S(1)}, u32[]{:S(2)}, u32[]{:S(2)}) collective-permute-start(bf16[1,128,128]{2,1,0:T(8,128)(2,1)S(1)} %get-tuple-element.38), channel_id=1, source_target_pairs={{0,8},{1,6},{4,12},{5,10},{6,1},{8,16},{9,14},{10,5},{11,3},{12,20... | collective-permute-start | bytes 98312 | tf_op jit(solution)/shard_map/ppermute | solution.py:31
  23.0 21.9 %collective-permute-start.5 = (bf16[45,128,128]{2,1,0:T(8,128)(2,1)S(1)}, bf16[45,128,128]{2,1,0:T(8,128)(2,1)S(1)}, u32[]{:S(2)}, u32[]{:S(2)}) collective-permute-start(bf16[45,128,128]{2,1,0:T(8,128)(2,1)S(1)} %join_cross.1), channel_id=1, source_target_pairs={{1,0},{2,3},{5,4},{6,7},{9,8},{10,11},{13,12},{14,15},{17,16},{18,... | collective-permute-start | bytes 4423688 | tf_op jit(solution)/shard_map/ppermute | solution.py:31
  24.3 46.5 %collective-permute-start.10 = (bf16[42,128,128]{2,1,0:T(8,128)(2,1)S(1)}, bf16[42,128,128]{2,1,0:T(8,128)(2,1)S(1)}, u32[]{:S(2)}, u32[]{:S(2)}) collective-permute-start(bf16[42,128,128]{2,1,0:T(8,128)(2,1)S(1)} %get-tuple-element.45), channel_id=1, source_target_pairs={{1,3},{2,0},{5,7},{6,4},{9,11},{10,8},{13,15},{14,12},{17,19},{18,... | collective-permute-start | bytes 4128776 | tf_op jit(solution)/shard_map/ppermute | solution.py:31
  25.6 45.2 %collective-permute-start.11 = (bf16[34,128,128]{2,1,0:T(8,128)(2,1)S(1)}, bf16[34,128,128]{2,1,0:T(8,128)(2,1)S(1)}, u32[]{:S(2)}, u32[]{:S(2)}) collective-permute-start(bf16[34,128,128]{2,1,0:T(8,128)(2,1)S(1)} %get-tuple-element.46), channel_id=1, source_target_pairs={{1,4},{5,8},{6,3},{9,12},{10,7},{13,16},{14,11},{17,20},{18,15},{2... | collective-permute-start | bytes 3342344 | tf_op jit(solution)/shard_map/ppermute | solution.py:31
  26.4 44.4 %collective-permute-start.13 = (bf16[15,128,128]{2,1,0:T(8,128)(2,1)S(1)}, bf16[15,128,128]{2,1,0:T(8,128)(2,1)S(1)}, u32[]{:S(2)}, u32[]{:S(2)}) collective-permute-start(bf16[15,128,128]{2,1,0:T(8,128)(2,1)S(1)} %get-tuple-element.47), channel_id=1, source_target_pairs={{2,6},{5,1},{6,10},{9,5},{10,14},{13,9},{14,18},{17,13},{18,22},{2... | collective-permute-start | bytes 1474568 | tf_op jit(solution)/shard_map/ppermute | solution.py:31
  27.1 43.7 %collective-permute-start.12 = (bf16[14,128,128]{2,1,0:T(8,128)(2,1)S(1)}, bf16[14,128,128]{2,1,0:T(8,128)(2,1)S(1)}, u32[]{:S(2)}, u32[]{:S(2)}) collective-permute-start(bf16[14,128,128]{2,1,0:T(8,128)(2,1)S(1)} %get-tuple-element.41._), channel_id=1, source_target_pairs={{2,4},{5,3},{6,8},{9,7},{10,12},{13,11},{14,16},{17,15},{18,20},{2... | collective-permute-start | bytes 1376264 | tf_op jit(solution)/shard_map/ppermute | solution.py:31
  45.0 9.9 %collective-permute-start.6 = (f32[2]{0:T(128)S(1)}, f32[2]{0:T(128)S(1)}, u32[]{:S(2)}, u32[]{:S(2)}) collective-permute-start(f32[2]{0:T(128)S(1)} %slice_reduce_fusion), channel_id=1, source_target_pairs={{0,1},{1,0},{2,3},{3,2},{4,5},{5,4},{6,7},{7,6},{8,9},{9,8},{10,11... | collective-permute-start | bytes 32 | tf_op jit(solution)/shard_map/ppermute | solution.py:31
  54.9 7.2 %collective-permute-start.7 = (f32[2]{0:T(128)S(1)}, f32[2]{0:T(128)S(1)}, u32[]{:S(2)}, u32[]{:S(2)}) collective-permute-start(f32[2]{0:T(128)S(1)} %add.23), channel_id=1, source_target_pairs={{0,16},{1,17},{2,18},{3,19},{4,20},{5,21},{6,22},{7,23},{8,24},{9,... | collective-permute-start | bytes 32 | tf_op jit(solution)/shard_map/ppermute | solution.py:31
  62.2 3.5 %collective-permute-start.8 = (f32[2]{0:T(128)S(1)}, f32[2]{0:T(128)S(1)}, u32[]{:S(2)}, u32[]{:S(2)}) collective-permute-start(f32[2]{0:T(128)S(1)} %add.24), channel_id=1, source_target_pairs={{0,2},{1,3},{2,0},{3,1},{4,6},{5,7},{6,4},{7,5},{8,10},{9,11},{10,... | collective-permute-start | bytes 32 | tf_op jit(solution)/shard_map/ppermute | solution.py:31
  65.7 5.1 %collective-permute-start.9 = (f32[2]{0:T(128)S(1)}, f32[2]{0:T(128)S(1)}, u32[]{:S(2)}, u32[]{:S(2)}) collective-permute-start(f32[2]{0:T(128)S(1)} %add.25), channel_id=1, source_target_pairs={{0,8},{1,9},{2,10},{3,11},{4,12},{5,13},{6,14},{7,15},{8,0},{9,1},... | collective-permute-start | bytes 32 | tf_op jit(solution)/shard_map/ppermute | solution.py:31
  72.8 8.0 %collective-permute-start.14 = (bf16[21,128,128]{2,1,0:T(8,128)(2,1)S(1)}, bf16[21,128,128]{2,1,0:T(8,128)(2,1)S(1)}, u32[]{:S(2)}, u32[]{:S(2)}) collective-permute-start(bf16[21,128,128]{2,1,0:T(8,128)(2,1)S(1)} %get-tuple-element.48), channel_id=1, source_target_pairs={{0,1},{1,0},{2,3},{3,2},{4,5},{5,4},{6,7},{7,6},{8,9},{9,8},{10,11... | collective-permute-start | bytes 2064392 | tf_op jit(solution)/shard_map/ppermute | solution.py:31
  76.8 3.5 %collective-permute-start.15 = (f32[2]{0:T(128)S(1)}, f32[2]{0:T(128)S(1)}, u32[]{:S(2)}, u32[]{:S(2)}) collective-permute-start(f32[2]{0:T(128)S(1)} %add.26), channel_id=1, source_target_pairs={{0,4},{1,5},{2,6},{3,7},{4,0},{5,1},{6,2},{7,3},{8,12},{9,13},{10,... | collective-permute-start | bytes 32 | tf_op jit(solution)/shard_map/ppermute | solution.py:31

commit v6 on v4

--- a/solution.py
+++ b/solution.py
@@ -116,7 +116,7 @@
     return [w for w in range(HALF, BAND - 1 - e) if e < 3 or not 5 <= w - HALF + 1 + e <= 8]
 
 
-def first_kernel(mine, part, x1, z1, z2, single):
+def first_kernel(mine, part, x1, z1, z2, corner, diagonal):
     at = {}
 
     def put(out, e, slots):
@@ -128,31 +128,32 @@
     for e in range(4):
         put(x1, e, range(9 - e))
     for e in range(4):
-        put(z1, e, range(5 - e))
+        put(z1, 3 - e, range(BAND - 1, BAND - 6 + e, -1))
     for e in range(4):
         put(z2, e, range(HALF, BAND - 5 - e))
     for e in range(4):
         put(x1, e, low_slots(e))
     for e in range(4):
-        put(z1, e, range(HALF, BAND - 1 - e))
-    for e in range(4):
-        put(z1, e, range(HALF - 1 - e, HALF - e))
-        put(z2, e, range(HALF - 1 - e, HALF - e))
-    single[0] = jnp.where(faces_pair(), mine[0, 0], part[1, HALF])
+        put(z1, 3 - e, range(HALF, e, -1))
+    for e in range(4):
+        put(z1, 3 - e, [HALF + 1 + e])
+        put(z2, e, [HALF - 1 - e])
+    corner[0] = part[1, BAND - 1]
+    diagonal[0] = part[1, HALF]
 
 
 def first_packs(mine, part):
     return pl.pallas_call(
         first_kernel,
-        out_shape=[jax.ShapeDtypeStruct((n, BS, BS), mine.dtype) for n in (72, 64, 34, 1)],
+        out_shape=[jax.ShapeDtypeStruct((n, BS, BS), mine.dtype) for n in (72, 64, 34, 1, 1)],
         in_specs=[VM] * 2,
-        out_specs=[VM] * 4,
+        out_specs=[VM] * 5,
         compiler_params=params(),
         name="first_packs",
     )(mine, part)
 
 
-def second_kernel(x1, z1, _, x2, g, h):
+def second_kernel(x1, z1, _sums, _diagonal, x2, g, h):
     at1 = at2 = 0
     start_x, start_z = 30, 14
     for e in range(4):
@@ -168,15 +169,15 @@
     h[at2] = z1[14]
 
 
-def second_packs(x1, z1, sums):
+def second_packs(x1, z1, sums, diagonal):
     return pl.pallas_call(
         second_kernel,
         out_shape=[jax.ShapeDtypeStruct((n, BS, BS), x1.dtype) for n in (42, 14, 15)],
-        in_specs=[VM] * 3,
+        in_specs=[VM] * 4,
         out_specs=[VM] * 3,
         compiler_params=params(),
         name="second_packs",
-    )(x1, z1, sums)
+    )(x1, z1, sums, diagonal)
 
 
 def join_cross_kernel(x1, z1, single, _, cross):
@@ -291,7 +292,7 @@
                     pairs[cut(n - 1), cut(m - 1)] = x
 
 
-def cross_kernel(near_rows, far_rows, before, x1, z1, single, first, sums, pairs):
+def cross_kernel(near_rows, far_rows, before, x1, z1, single, _diagonal, first, sums, pairs):
     def block(t, u):
         at = cross_start(t) + 10 - t - u
         if t == 9:
@@ -311,20 +312,20 @@
     sums[1:2, :] = (before[1:2, :] + 6.0 * third) * scale
 
 
-def cross_part(near_rows, far_rows, before, x1, z1, single):
+def cross_part(near_rows, far_rows, before, x1, z1, single, diagonal):
     return pl.pallas_call(
         cross_kernel,
         out_shape=(
             jax.ShapeDtypeStruct((4 * BS, 10 * BS), jnp.float32),
             jax.ShapeDtypeStruct(before.shape, jnp.float32),
         ),
-        in_specs=[VM] * 6,
+        in_specs=[VM] * 7,
         out_specs=(VM,) * 2,
         scratch_shapes=[pltpu.VMEM((10 * BS, 10 * BS), x1.dtype)],
         compiler_params=params(),
         cost_estimate=pl.CostEstimate(flops=10**9, bytes_accessed=10**6, transcendentals=0),
         name="cross_part",
-    )(near_rows, far_rows, before, x1, z1, single)
+    )(near_rows, far_rows, before, x1, z1, single, diagonal)
 
 
 def mid_kernel(own, near_rows, far_rows, first, swapped, partial, cross):
@@ -420,19 +421,34 @@
     )(near_rows, partial, x1, x2, z1, z2, g, h, single)
 
 
-def near_kernel(mask, near_rows, partial, inner, pairs1, pairs2, pairs3, out):
+def near_kernel(mask, near_rows, partial, inner, pairs1, pairs2, pairs3, out, held, sems):
     core = my_core()
+    copies = []
 
     def put(e, w, value):
         r = jnp.where(core > 0, 1 - e, e)
         a = jnp.where(core > 0, BAND - 1 - w, w)
-        out[r, a] = jnp.where(mask[r, a] > 0, value, 0.0).astype(out.dtype)
+        held[r, a] = jnp.where(mask[r, a] > 0, value, 0.0).astype(held.dtype)
+
+    def send(e, lo, n):
+        r = jnp.where(core > 0, 1 - e, e)
+        part = pl.ds(jnp.where(core > 0, BAND - lo - n, lo), n)
+        copy = pltpu.make_async_copy(held.at[r, part], out.at[r, part], sems.at[len(copies)])
+        copy.start()
+        copies.append(copy)
 
     for e in range(2):
         for k in range(4):
             put(e, k - e + HALF, inner[cut(e), cut(k)])
+        send(e, HALF - e, 4)
     for e, t, value in near_products(0, near_rows, partial, pairs1, pairs2, pairs3):
         put(e, HALF - e - t, value)
+        if t % 2 == 0:
+            send(e, HALF - e - t, 2)
+        elif e + t == HALF:
+            send(e, 0, 1)
+    for copy in copies:
+        copy.wait()
 
 
 def near_part(mask, near_rows, partial, inner, *pairs):
@@ -440,7 +456,11 @@
         near_kernel,
         out_shape=jax.ShapeDtypeStruct((2, BAND, BS, BS), near_rows.dtype),
         in_specs=[VM] * 7,
-        out_specs=VM,
+        out_specs=HB,
+        scratch_shapes=[
+            pltpu.VMEM((2, BAND, BS, BS), near_rows.dtype),
+            pltpu.SemaphoreType.DMA((16,)),
+        ],
         compiler_params=params(),
         cost_estimate=pl.CostEstimate(flops=10**9, bytes_accessed=10**6, transcendentals=0),
         name="near_part",
@@ -496,21 +516,7 @@
     def outer(i):
         return not inner(i)
 
-    x1, z1, z2, single = first_packs(mine, part)
-    x1 = to_side(x1, 1, inner)
-    z1 = to_side(z1, 2, outer)
-
-    def singles(i):
-        chip, core = divmod(i, 2)
-        if inner(i):
-            return 2 * (chip + 3) if core else 2 * (chip - 3) + 1
-        return 2 * (chip - 4) + 1 if core else 2 * (chip + 4)
-
-    single = permute(single, singles)
-    own, inside, near_rows, far_rows, sums = own_part(mine, part)
-
-    x2, g, h = second_packs(x1, z1, sums)
-    swapped = permute(join_cross(x1, z1, single, g), lambda i: i ^ 1 if inner(i) else -1)
+    x1, z1, z2, corner, diagonal = first_packs(mine, part)
 
     def along(pair, senders):
         def target(i):
@@ -519,21 +525,30 @@
 
         return target
 
+    x1 = to_side(x1, 1, inner)
+    z1 = permute(z1, along(-2, inner))
+    corner = permute(corner, along(-3, outer))
+    diagonal = permute(diagonal, along(-4, outer))
+    own, inside, near_rows, far_rows, sums = own_part(mine, part)
+
+    x2, g, h = second_packs(x1, z1, sums, sums)
+    swapped = permute(join_cross(x1, z1, corner, g), lambda i: i ^ 1 if inner(i) else -1)
+
     z2 = to_side(z2, 2, inner)
     x2 = permute(x2, along(1, inner))
     g = permute(g, along(-1, inner))
     h = permute(h, along(-2, inner))
 
-    first, sums = cross_part(near_rows, far_rows, sums, x1, z1, single)
+    first, sums = cross_part(near_rows, far_rows, sums, x1, z1, corner, diagonal)
     sums, swapped = lax.optimization_barrier((sums[:, 0], swapped))
     steps = [1 << n for n in range(lax.axis_size(AXES).bit_length() - 1)]
-    sums = sum_over(sums, steps[:1] + steps[4:] + steps[1:3])
+    sums = sum_over(sums, steps[4:] + steps[:1] + steps[1:2] + steps[3:4])
     partial = mid_part(own, near_rows, far_rows, first, swapped)
     partial, sums = lax.optimization_barrier((partial, sums))
-    away, *pairs = away_part(near_rows, partial, x1, x2, z1, z2, g, h, single)
+    away, *pairs = away_part(near_rows, partial, x1, x2, z1, z2, g, h, diagonal)
     came = to_partner(away)
     out = near_part(mask, near_rows, partial, inside, *pairs)
-    traces = sum_over(sums, steps[3:4])
+    traces = sum_over(sums, steps[2:3])
     square = join(mask, came, out)
     return square, traces
 

time: 83.6 us -> 82.2 us (0.983)
  waiting for transfers between devices: 26.2 us -> 19.9 us
  starting transfers between devices: 38.3 us -> 43.6 us
    ppermute x15 -> x16, waiting for transfers between devices: 26.2 us -> 19.9 us  [permute(): lax.ppermute(value, AXES, [(i, j) for i, j in pairs if 0 <= j < devices])]
    ppermute x15 -> x16, starting transfers between devices: 38.3 us -> 43.6 us  [permute(): lax.ppermute(value, AXES, [(i, j) for i, j in pairs if 0 <= j < devices])]
  transfers between devices with their start and end apart: 15 -> 16, of which waited for: 6 -> 6; matrix products, arithmetic and copies ran while one was open for 1% -> 1% of each run, Pallas kernels for 12% -> 12%
where the time goes in v6:
time: 82.2 us; the launch traced here: 81.9 us
  starting transfers between devices  43.6 us (53%)
  waiting for transfers between devices  19.9 us (24%)
  Pallas kernels  14.5 us (18%)
  local copies, waits for them, and re-layouts  1.59 us (2%)
  other arithmetic  1.23 us (1%)
  between operations  1 us (1%)
    ppermute x16, starting transfers between devices, permute(): lax.ppermute(value, AXES, [(i, j) for i, j in pairs if 0 <= j < devices])  43.6 us
    ppermute x16, waiting for transfers between devices, permute(): lax.ppermute(value, AXES, [(i, j) for i, j in pairs if 0 <= j < devices])  19.9 us
    pallas_call x1, Pallas kernels, own_part(): pl.pallas_call(own_kernel_products, out_shape=(jax.ShapeDtypeStruct((4 *...  2.96 us
    pallas_call x1, Pallas kernels, near_part(): pl.pallas_call(near_kernel, out_shape=jax.ShapeDtypeStruct((2, BAND, BS,...  2.69 us
    pallas_call x1, Pallas kernels, mid_part(): pl.pallas_call(mid_kernel, out_shape=jax.ShapeDtypeStruct(near_rows.shape...  2.26 us
    pallas_call x1, Pallas kernels, away_part(): pl.pallas_call(away_kernel, out_shape=[jax.ShapeDtypeStruct(shape, x1.dty...  1.98 us
  transfers between devices with their start and end apart: 16, of which 6 were waited for; matrix products, arithmetic and copies ran while one was open for 1% of the time, Pallas kernels for 12%

profile of v6, /device:TPU:0, one launch (start us, length us, event | category | flops | bytes accessed | tf_op | source)
XLA Modules:
  0.0 81.9 jit_solution(8030039546409837466)
XLA Ops:
  0.6 0.7 pad_add_fusion.table
  1.3 1.5 %copy-done = bf16[2,27,128,128]{3,2,1,0:T(8,128)(2,1)S(1)} copy-done((bf16[2,27,128,128]{3,2,1,0:T(8,128)(2,1)S(1)}, bf16[2,27,128,128]{3,2,1,0:T(8,128)(2,1)}, u32[]{:S(2)}) %copy-start) | copy-done | bytes 1769496
  2.8 1.4 %own_rows.1 = (bf16[2,27,128,128]{3,2,1,0:T(8,128)(2,1)S(1)}, bf16[2,27,128,128]{3,2,1,0:T(8,128)(2,1)S(1)}, s32[2,27,1,128]{3,2,1,0:T(1,128)S(1)}) custom-call(s32[3,27]{1,0:T(4,128)S(1)} %pad_add_fusion.table, bf16[2,27,128,128]{3,2,1,0:T(8,128)(2,1)S(1)} %copy-done), custom_call_target="tpu_custom_call" | custom-call | tf_op jit(solution)/shard_map/own_rows/pallas_call | solution.py:104
  4.2 0.5 collective-permute-start
  4.7 3.3 %collective-permute-done.part = bf16[2,27,128,128]{3,2,1,0:T(8,128)(2,1)S(1)} collective-permute-done((bf16[2,27,128,128]{3,2,1,0:T(8,128)(2,1)S(1)}, bf16[2,27,128,128]{3,2,1,0:T(8,128)(2,1)S(1)}, u32[]{:S(2)}, u32[]{:S(2)}) %collective-permute-start) | collective-permute-done | bytes 1769504 | tf_op jit(solution)/shard_map/ppermute | solution.py:31
  8.1 0.4 first_packs.1
  8.4 0.8 collective-permute-start.1
  9.2 0.8 collective-permute-start.2
  10.1 10.0 %collective-permute-start.3 = (bf16[1,128,128]{2,1,0:T(8,128)(2,1)S(1)}, bf16[1,128,128]{2,1,0:T(8,128)(2,1)S(1)}, u32[]{:S(2)}, u32[]{:S(2)}) collective-permute-start(bf16[1,128,128]{2,1,0:T(8,128)(2,1)S(1)} %get-tuple-element.37), channel_id=1, source_target_pairs={{0,6},{4,10},{7,1},{8,14},{11,5},{12,18},{15,9},{16,22},{19,13},{2... | collective-permute-start | bytes 98312 | tf_op jit(solution)/shard_map/ppermute | solution.py:31
  20.1 3.0 %own_part.1 = (bf16[512,512]{1,0:T(8,128)(2,1)S(1)}, f32[256,512]{1,0:T(8,128)S(1)}, bf16[512,1792]{1,0:T(8,128)(2,1)S(1)}, bf16[512,1280]{1,0:T(8,128)(2,1)S(1)}, f32[2,128]{1,0:T(2,128)S(1)}) custom-call(bf16[2,27,128,128]{3,2,1,0:T(8,128)(2,1)S(1)} %get-tuple-element.29.mine, bf16[2,27,128,128]{3,2,1,0:T(8,128)(2,1)S(1)} %collective-permute-done.part), custom_call_target="tpu_custom_call" | custom-call | flops 2000000000 | bytes 1000000 | tf_op jit(solution)/shard_map/own_part/pallas_call | solution.py:268
  23.4 1.3 %collective-permute-start.5 = (bf16[45,128,128]{2,1,0:T(8,128)(2,1)S(1)}, bf16[45,128,128]{2,1,0:T(8,128)(2,1)S(1)}, u32[]{:S(2)}, u32[]{:S(2)}) collective-permute-start(bf16[45,128,128]{2,1,0:T(8,128)(2,1)S(1)} %join_cross.1), channel_id=1, source_target_pairs={{1,0},{2,3},{5,4},{6,7},{9,8},{10,11},{13,12},{14,15},{17,16},{18,... | collective-permute-start | bytes 4423688 | tf_op jit(solution)/shard_map/ppermute | solution.py:31
  24.7 1.3 %collective-permute-start.10 = (bf16[42,128,128]{2,1,0:T(8,128)(2,1)S(1)}, bf16[42,128,128]{2,1,0:T(8,128)(2,1)S(1)}, u32[]{:S(2)}, u32[]{:S(2)}) collective-permute-start(bf16[42,128,128]{2,1,0:T(8,128)(2,1)S(1)} %get-tuple-element.45), channel_id=1, source_target_pairs={{1,3},{2,0},{5,7},{6,4},{9,11},{10,8},{13,15},{14,12},{17,19},{18,... | collective-permute-start | bytes 4128776 | tf_op jit(solution)/shard_map/ppermute | solution.py:31
  26.0 0.7 collective-permute-start.11
  26.8 4.7 %collective-permute-start.4 = (bf16[1,128,128]{2,1,0:T(8,128)(2,1)S(1)}, bf16[1,128,128]{2,1,0:T(8,128)(2,1)S(1)}, u32[]{:S(2)}, u32[]{:S(2)}) collective-permute-start(bf16[1,128,128]{2,1,0:T(8,128)(2,1)S(1)} %get-tuple-element.38), channel_id=1, source_target_pairs={{0,8},{4,12},{8,16},{11,3},{12,20},{15,7},{16,24},{19,11},{20,28},... | collective-permute-start | bytes 98312 | tf_op jit(solution)/shard_map/ppermute | solution.py:31
  31.5 0.7 collective-permute-start.13
  32.2 0.9 %collective-permute-done.4._diagonal.single = bf16[1,128,128]{2,1,0:T(8,128)(2,1)S(1)} collective-permute-done((bf16[1,128,128]{2,1,0:T(8,128)(2,1)S(1)}, bf16[1,128,128]{2,1,0:T(8,128)(2,1)S(1)}, u32[]{:S(2)}, u32[]{:S(2)}) %collective-permute-start.4) | collective-permute-done | bytes 32800 | tf_op jit(solution)/shard_map/ppermute | solution.py:31
  33.1 0.9 %collective-permute-start.12 = (bf16[14,128,128]{2,1,0:T(8,128)(2,1)S(1)}, bf16[14,128,128]{2,1,0:T(8,128)(2,1)S(1)}, u32[]{:S(2)}, u32[]{:S(2)}) collective-permute-start(bf16[14,128,128]{2,1,0:T(8,128)(2,1)S(1)} %get-tuple-element.41._), channel_id=1, source_target_pairs={{2,4},{5,3},{6,8},{9,7},{10,12},{13,11},{14,16},{17,15},{18,20},{2... | collective-permute-start | bytes 1376264 | tf_op jit(solution)/shard_map/ppermute | solution.py:31
  33.9 1.5 %cross_part.1 = (f32[512,1280]{1,0:T(8,128)S(1)}, f32[2,128]{1,0:T(2,128)S(1)}) custom-call(bf16[512,1792]{1,0:T(8,128)(2,1)S(1)} %get-tuple-element.31.near_rows, bf16[512,1280]{1,0:T(8,128)(2,1)S(1)} %get-tuple-element.33.far_rows, f32[2,128]{1,0:T(2,128)S(1)} %get-tuple-element.34.before._sums._diagonal, ...), custom_call_target="tpu_custom_call" | custom-call | flops 1000000000 | bytes 1000000 | tf_op jit(solution)/shard_map/cross_part/pallas_call | solution.py:316
  35.5 9.7 %collective-permute-done.5.swapped = bf16[45,128,128]{2,1,0:T(8,128)(2,1)S(1)} collective-permute-done((bf16[45,128,128]{2,1,0:T(8,128)(2,1)S(1)}, bf16[45,128,128]{2,1,0:T(8,128)(2,1)S(1)}, u32[]{:S(2)}, u32[]{:S(2)}) %collective-permute-start.5) | collective-permute-done | bytes 1474592 | tf_op jit(solution)/shard_map/ppermute | solution.py:31
  45.3 3.2 %collective-permute-start.6 = (f32[2]{0:T(128)S(1)}, f32[2]{0:T(128)S(1)}, u32[]{:S(2)}, u32[]{:S(2)}) collective-permute-start(f32[2]{0:T(128)S(1)} %slice_reduce_fusion), channel_id=1, source_target_pairs={{0,16},{1,17},{2,18},{3,19},{4,20},{5,21},{6,22},{7,23},{8,24},{9,... | collective-permute-start | bytes 32 | tf_op jit(solution)/shard_map/ppermute | solution.py:31
  48.5 2.3 %mid_part.1.partial = f32[512,1792]{1,0:T(8,128)S(1)} custom-call(bf16[512,512]{1,0:T(8,128)(2,1)S(1)} %get-tuple-element.32.own, bf16[512,1792]{1,0:T(8,128)(2,1)S(1)} %get-tuple-element.31.near_rows, bf16[512,1280]{1,0:T(8,128)(2,1)S(1)} %get-tuple-element.33.far_rows, f32[512,1280]{1,0:T(8,128)S(1)} %get-tuple-element.39.first, ...), custom_call_target="tpu_custom_call" | custom-call | flops 2000000000 | bytes 1000000 | tf_op jit(solution)/shard_map/mid_part/pallas_call | solution.py:344
  50.8 10.3 %collective-permute-start.7 = (f32[2]{0:T(128)S(1)}, f32[2]{0:T(128)S(1)}, u32[]{:S(2)}, u32[]{:S(2)}) collective-permute-start(f32[2]{0:T(128)S(1)} %add.23), channel_id=1, source_target_pairs={{0,1},{1,0},{2,3},{3,2},{4,5},{5,4},{6,7},{7,6},{8,9},{9,8},{10,11... | collective-permute-start | bytes 32 | tf_op jit(solution)/shard_map/ppermute | solution.py:31
  61.1 0.8 %collective-permute-done.7 = f32[2]{0:T(128)S(1)} collective-permute-done((f32[2]{0:T(128)S(1)}, f32[2]{0:T(128)S(1)}, u32[]{:S(2)}, u32[]{:S(2)}) %collective-permute-start.7) | collective-permute-done | bytes 40 | tf_op jit(solution)/shard_map/ppermute | solution.py:31
  61.9 3.5 %collective-permute-done.8 = f32[2]{0:T(128)S(1)} collective-permute-done((f32[2]{0:T(128)S(1)}, f32[2]{0:T(128)S(1)}, u32[]{:S(2)}, u32[]{:S(2)}) %collective-permute-start.8) | collective-permute-done | bytes 40 | tf_op jit(solution)/shard_map/ppermute | solution.py:31
  65.5 3.4 %collective-permute-start.9 = (f32[2]{0:T(128)S(1)}, f32[2]{0:T(128)S(1)}, u32[]{:S(2)}, u32[]{:S(2)}) collective-permute-start(f32[2]{0:T(128)S(1)} %add.25), channel_id=1, source_target_pairs={{0,8},{1,9},{2,10},{3,11},{4,12},{5,13},{6,14},{7,15},{8,0},{9,1},... | collective-permute-start | bytes 32 | tf_op jit(solution)/shard_map/ppermute | solution.py:31
  68.9 1.6 %collective-permute-done.9 = f32[2]{0:T(128)S(1)} collective-permute-done((f32[2]{0:T(128)S(1)}, f32[2]{0:T(128)S(1)}, u32[]{:S(2)}, u32[]{:S(2)}) %collective-permute-start.9) | collective-permute-done | bytes 40 | tf_op jit(solution)/shard_map/ppermute | solution.py:31
  70.5 2.0 %away_part.1 = (bf16[21,128,128]{2,1,0:T(8,128)(2,1)S(1)}, bf16[512,1792]{1,0:T(8,128)(2,1)S(1)}, bf16[512,1280]{1,0:T(8,128)(2,1)S(1)}, bf16[768,768]{1,0:T(8,128)(2,1)S(1)}) custom-call(bf16[512,1792]{1,0:T(8,128)(2,1)S(1)} %get-tuple-element.31.near_rows, f32[512,1792]{1,0:T(8,128)S(1)} %mid_part.1.partial, ...), custom_call_target="tpu_custom_call" | custom-call | flops 2000000000 | bytes 1000000 | tf_op jit(solution)/shard_map/away_part/pallas_call | solution.py:413
  72.5 3.6 %collective-permute-start.14 = (bf16[21,128,128]{2,1,0:T(8,128)(2,1)S(1)}, bf16[21,128,128]{2,1,0:T(8,128)(2,1)S(1)}, u32[]{:S(2)}, u32[]{:S(2)}) collective-permute-start(bf16[21,128,128]{2,1,0:T(8,128)(2,1)S(1)} %get-tuple-element.48), channel_id=1, source_target_pairs={{0,1},{1,0},{2,3},{3,2},{4,5},{5,4},{6,7},{7,6},{8,9},{9,8},{10,11... | collective-permute-start | bytes 2064392 | tf_op jit(solution)/shard_map/ppermute | solution.py:31
  76.1 1.4 %collective-permute-start.15 = (f32[2]{0:T(128)S(1)}, f32[2]{0:T(128)S(1)}, u32[]{:S(2)}, u32[]{:S(2)}) collective-permute-start(f32[2]{0:T(128)S(1)} %add.26), channel_id=1, source_target_pairs={{0,4},{1,5},{2,6},{3,7},{4,0},{5,1},{6,2},{7,3},{8,12},{9,13},{10,... | collective-permute-start | bytes 32 | tf_op jit(solution)/shard_map/ppermute | solution.py:31
  77.4 2.7 %near_part.1._ = bf16[2,27,128,128]{3,2,1,0:T(8,128)(2,1)} custom-call(s32[2,27,1,128]{3,2,1,0:T(1,128)S(1)} %get-tuple-element.28.mask, bf16[512,1792]{1,0:T(8,128)(2,1)S(1)} %get-tuple-element.31.near_rows, f32[512,1792]{1,0:T(8,128)S(1)} %mid_part.1.partial, f32[256,512]{1,0:T(8,128)S(1)} %get-tuple-element.49.inner, ...), custom_call_target="tpu_custom_call" | custom-call | flops 1000000000 | bytes 1000000 | tf_op jit(solution)/shard_map/near_part/pallas_call | solution.py:455
  80.2 0.5 add.27
  80.7 1.1 %join.1 = bf16[2,27,128,128]{3,2,1,0:T(8,128)(2,1)} custom-call(s32[2,27,1,128]{3,2,1,0:T(1,128)S(1)} %get-tuple-element.28.mask, bf16[21,128,128]{2,1,0:T(8,128)(2,1)S(1)} %collective-permute-done.14.came, bf16[2,27,128,128]{3,2,1,0:T(8,128)(2,1)} %near_part.1._), custom_call_target="tpu_custom_call", output_to_operand_aliasing={{}: (2, {})} | custom-call | tf_op jit(solution)/shard_map/join/pallas_call | solution.py:496
  (19 shorter events, 0.5 us)
Async XLA Ops:
  1.3 1.5 %copy-start = (bf16[2,27,128,128]{3,2,1,0:T(8,128)(2,1)S(1)}, bf16[2,27,128,128]{3,2,1,0:T(8,128)(2,1)}, u32[]{:S(2)}) copy-start(bf16[2,27,128,128]{3,2,1,0:T(8,128)(2,1)} %blocks.1) | copy-start | bytes 5308420
  4.2 3.9 %collective-permute-start = (bf16[2,27,128,128]{3,2,1,0:T(8,128)(2,1)S(1)}, bf16[2,27,128,128]{3,2,1,0:T(8,128)(2,1)S(1)}, u32[]{:S(2)}, u32[]{:S(2)}) collective-permute-start(bf16[2,27,128,128]{3,2,1,0:T(8,128)(2,1)S(1)} %get-tuple-element.30), channel_id=1, source_target_pairs={{0,1},{1,0},{2,3},{3,2},{4,5},{5,4},{6,7},{7,6},{8,9},{9,8},{10,11... | collective-permute-start | bytes 5308424 | tf_op jit(solution)/shard_map/ppermute | solution.py:31
  8.4 14.6 %collective-permute-start.1 = (bf16[72,128,128]{2,1,0:T(8,128)(2,1)S(1)}, bf16[72,128,128]{2,1,0:T(8,128)(2,1)S(1)}, u32[]{:S(2)}, u32[]{:S(2)}) collective-permute-start(bf16[72,128,128]{2,1,0:T(8,128)(2,1)S(1)} %get-tuple-element.35), channel_id=1, source_target_pairs={{1,2},{2,1},{5,6},{6,5},{9,10},{10,9},{13,14},{14,13},{17,18},{18,... | collective-permute-start | bytes 7077896 | tf_op jit(solution)/shard_map/ppermute | solution.py:31
  9.2 13.8 %collective-permute-start.2 = (bf16[64,128,128]{2,1,0:T(8,128)(2,1)S(1)}, bf16[64,128,128]{2,1,0:T(8,128)(2,1)S(1)}, u32[]{:S(2)}, u32[]{:S(2)}) collective-permute-start(bf16[64,128,128]{2,1,0:T(8,128)(2,1)S(1)} %get-tuple-element.36), channel_id=1, source_target_pairs={{2,6},{5,1},{6,10},{9,5},{10,14},{13,9},{14,18},{17,13},{18,22},{2... | collective-permute-start | bytes 6291464 | tf_op jit(solution)/shard_map/ppermute | solution.py:31
  10.1 13.3 %collective-permute-start.3 = (bf16[1,128,128]{2,1,0:T(8,128)(2,1)S(1)}, bf16[1,128,128]{2,1,0:T(8,128)(2,1)S(1)}, u32[]{:S(2)}, u32[]{:S(2)}) collective-permute-start(bf16[1,128,128]{2,1,0:T(8,128)(2,1)S(1)} %get-tuple-element.37), channel_id=1, source_target_pairs={{0,6},{4,10},{7,1},{8,14},{11,5},{12,18},{15,9},{16,22},{19,13},{2... | collective-permute-start | bytes 98312 | tf_op jit(solution)/shard_map/ppermute | solution.py:31
  23.4 21.8 %collective-permute-start.5 = (bf16[45,128,128]{2,1,0:T(8,128)(2,1)S(1)}, bf16[45,128,128]{2,1,0:T(8,128)(2,1)S(1)}, u32[]{:S(2)}, u32[]{:S(2)}) collective-permute-start(bf16[45,128,128]{2,1,0:T(8,128)(2,1)S(1)} %join_cross.1), channel_id=1, source_target_pairs={{1,0},{2,3},{5,4},{6,7},{9,8},{10,11},{13,12},{14,15},{17,16},{18,... | collective-permute-start | bytes 4423688 | tf_op jit(solution)/shard_map/ppermute | solution.py:31
  24.7 45.7 %collective-permute-start.10 = (bf16[42,128,128]{2,1,0:T(8,128)(2,1)S(1)}, bf16[42,128,128]{2,1,0:T(8,128)(2,1)S(1)}, u32[]{:S(2)}, u32[]{:S(2)}) collective-permute-start(bf16[42,128,128]{2,1,0:T(8,128)(2,1)S(1)} %get-tuple-element.45), channel_id=1, source_target_pairs={{1,3},{2,0},{5,7},{6,4},{9,11},{10,8},{13,15},{14,12},{17,19},{18,... | collective-permute-start | bytes 4128776 | tf_op jit(solution)/shard_map/ppermute | solution.py:31
  26.0 44.4 %collective-permute-start.11 = (bf16[34,128,128]{2,1,0:T(8,128)(2,1)S(1)}, bf16[34,128,128]{2,1,0:T(8,128)(2,1)S(1)}, u32[]{:S(2)}, u32[]{:S(2)}) collective-permute-start(bf16[34,128,128]{2,1,0:T(8,128)(2,1)S(1)} %get-tuple-element.46), channel_id=1, source_target_pairs={{1,4},{5,8},{6,3},{9,12},{10,7},{13,16},{14,11},{17,20},{18,15},{2... | collective-permute-start | bytes 3342344 | tf_op jit(solution)/shard_map/ppermute | solution.py:31
  26.8 6.3 %collective-permute-start.4 = (bf16[1,128,128]{2,1,0:T(8,128)(2,1)S(1)}, bf16[1,128,128]{2,1,0:T(8,128)(2,1)S(1)}, u32[]{:S(2)}, u32[]{:S(2)}) collective-permute-start(bf16[1,128,128]{2,1,0:T(8,128)(2,1)S(1)} %get-tuple-element.38), channel_id=1, source_target_pairs={{0,8},{4,12},{8,16},{11,3},{12,20},{15,7},{16,24},{19,11},{20,28},... | collective-permute-start | bytes 98312 | tf_op jit(solution)/shard_map/ppermute | solution.py:31
  31.5 39.0 %collective-permute-start.13 = (bf16[15,128,128]{2,1,0:T(8,128)(2,1)S(1)}, bf16[15,128,128]{2,1,0:T(8,128)(2,1)S(1)}, u32[]{:S(2)}, u32[]{:S(2)}) collective-permute-start(bf16[15,128,128]{2,1,0:T(8,128)(2,1)S(1)} %get-tuple-element.47), channel_id=1, source_target_pairs={{2,6},{5,1},{6,10},{9,5},{10,14},{13,9},{14,18},{17,13},{18,22},{2... | collective-permute-start | bytes 1474568 | tf_op jit(solution)/shard_map/ppermute | solution.py:31
  33.1 37.4 %collective-permute-start.12 = (bf16[14,128,128]{2,1,0:T(8,128)(2,1)S(1)}, bf16[14,128,128]{2,1,0:T(8,128)(2,1)S(1)}, u32[]{:S(2)}, u32[]{:S(2)}) collective-permute-start(bf16[14,128,128]{2,1,0:T(8,128)(2,1)S(1)} %get-tuple-element.41._), channel_id=1, source_target_pairs={{2,4},{5,3},{6,8},{9,7},{10,12},{13,11},{14,16},{17,15},{18,20},{2... | collective-permute-start | bytes 1376264 | tf_op jit(solution)/shard_map/ppermute | solution.py:31
  45.3 5.5 %collective-permute-start.6 = (f32[2]{0:T(128)S(1)}, f32[2]{0:T(128)S(1)}, u32[]{:S(2)}, u32[]{:S(2)}) collective-permute-start(f32[2]{0:T(128)S(1)} %slice_reduce_fusion), channel_id=1, source_target_pairs={{0,16},{1,17},{2,18},{3,19},{4,20},{5,21},{6,22},{7,23},{8,24},{9,... | collective-permute-start | bytes 32 | tf_op jit(solution)/shard_map/ppermute | solution.py:31
  50.8 11.1 %collective-permute-start.7 = (f32[2]{0:T(128)S(1)}, f32[2]{0:T(128)S(1)}, u32[]{:S(2)}, u32[]{:S(2)}) collective-permute-start(f32[2]{0:T(128)S(1)} %add.23), channel_id=1, source_target_pairs={{0,1},{1,0},{2,3},{3,2},{4,5},{5,4},{6,7},{7,6},{8,9},{9,8},{10,11... | collective-permute-start | bytes 32 | tf_op jit(solution)/shard_map/ppermute | solution.py:31
  61.9 3.5 %collective-permute-start.8 = (f32[2]{0:T(128)S(1)}, f32[2]{0:T(128)S(1)}, u32[]{:S(2)}, u32[]{:S(2)}) collective-permute-start(f32[2]{0:T(128)S(1)} %add.24), channel_id=1, source_target_pairs={{0,2},{1,3},{2,0},{3,1},{4,6},{5,7},{6,4},{7,5},{8,10},{9,11},{10,... | collective-permute-start | bytes 32 | tf_op jit(solution)/shard_map/ppermute | solution.py:31
  65.5 5.0 %collective-permute-start.9 = (f32[2]{0:T(128)S(1)}, f32[2]{0:T(128)S(1)}, u32[]{:S(2)}, u32[]{:S(2)}) collective-permute-start(f32[2]{0:T(128)S(1)} %add.25), channel_id=1, source_target_pairs={{0,8},{1,9},{2,10},{3,11},{4,12},{5,13},{6,14},{7,15},{8,0},{9,1},... | collective-permute-start | bytes 32 | tf_op jit(solution)/shard_map/ppermute | solution.py:31
  72.5 8.2 %collective-permute-start.14 = (bf16[21,128,128]{2,1,0:T(8,128)(2,1)S(1)}, bf16[21,128,128]{2,1,0:T(8,128)(2,1)S(1)}, u32[]{:S(2)}, u32[]{:S(2)}) collective-permute-start(bf16[21,128,128]{2,1,0:T(8,128)(2,1)S(1)} %get-tuple-element.48), channel_id=1, source_target_pairs={{0,1},{1,0},{2,3},{3,2},{4,5},{5,4},{6,7},{7,6},{8,9},{9,8},{10,11... | collective-permute-start | bytes 2064392 | tf_op jit(solution)/shard_map/ppermute | solution.py:31
  76.1 4.1 %collective-permute-start.15 = (f32[2]{0:T(128)S(1)}, f32[2]{0:T(128)S(1)}, u32[]{:S(2)}, u32[]{:S(2)}) collective-permute-start(f32[2]{0:T(128)S(1)} %add.26), channel_id=1, source_target_pairs={{0,4},{1,5},{2,6},{3,7},{4,0},{5,1},{6,2},{7,3},{8,12},{9,13},{10,... | collective-permute-start | bytes 32 | tf_op jit(solution)/shard_map/ppermute | solution.py:31

commit v7 on v6

--- a/solution.py
+++ b/solution.py
@@ -10,6 +10,7 @@
 BAND = 2 * HALF + 1
 BS = 128
 NEAR = HALF
+MOVED = 2
 FAR = 12
 NCOL = NEAR + 1
 NEAR_W, OWN_W, FAR_W = NCOL * BS, 4 * BS, FAR * BS
@@ -113,7 +114,7 @@
 
 
 def low_slots(e):
-    return [w for w in range(HALF, BAND - 1 - e) if e < 3 or not 5 <= w - HALF + 1 + e <= 8]
+    return [w for w in range(HALF, BAND - 1 - e) if e < 3 or not 5 <= w - HALF + 1 + e < 5 + MOVED]
 
 
 def first_kernel(mine, part, x1, z1, z2, corner, diagonal):
@@ -135,7 +136,7 @@
         put(x1, e, low_slots(e))
     for e in range(4):
         put(z1, 3 - e, range(HALF, e, -1))
-    for e in range(4):
+    for e in range(MOVED):
         put(z1, 3 - e, [HALF + 1 + e])
         put(z2, e, [HALF - 1 - e])
     corner[0] = part[1, BAND - 1]
@@ -145,7 +146,7 @@
 def first_packs(mine, part):
     return pl.pallas_call(
         first_kernel,
-        out_shape=[jax.ShapeDtypeStruct((n, BS, BS), mine.dtype) for n in (72, 64, 34, 1, 1)],
+        out_shape=[jax.ShapeDtypeStruct((n, BS, BS), mine.dtype) for n in (76 - MOVED, 60 + MOVED, 30 + MOVED, 1, 1)],
         in_specs=[VM] * 2,
         out_specs=[VM] * 5,
         compiler_params=params(),
@@ -162,7 +163,7 @@
             at1 += 1
         for n in range(5 - e):
             g[at2] = z1[start_z + n]
-            h[at2] = x1[start_x + n] if n < 4 - e or e < 3 else turned(z1[60])
+            h[at2] = x1[start_x + n] if n < 4 - e or e < 3 or not MOVED else turned(z1[60])
             at2 += 1
         start_x += len(low_slots(e))
         start_z += 13 - e
@@ -172,7 +173,7 @@
 def second_packs(x1, z1, sums, diagonal):
     return pl.pallas_call(
         second_kernel,
-        out_shape=[jax.ShapeDtypeStruct((n, BS, BS), x1.dtype) for n in (42, 14, 15)],
+        out_shape=[jax.ShapeDtypeStruct((n, BS, BS), x1.dtype) for n in (46 - MOVED, 14, 15)],
         in_specs=[VM] * 4,
         out_specs=[VM] * 3,
         compiler_params=params(),
@@ -366,7 +367,7 @@
         if t >= LOW:
             start = 14 + sum(13 - n for n in range(t - LOW))
             return jnp.where(facing, z1[start + s - t], z2[near_start(t) + s - t])
-        if t == 4 and LOW <= s < LAST:
+        if t == 4 and LOW <= s < LOW + MOVED:
             at = s - LOW
             return turned(jnp.where(facing, z1[60 + at], z2[30 + at]))
         slots = low_slots(t - 1)

time: 82.2 us -> 80.8 us (0.983)
  starting transfers between devices: 43.6 us -> 42.1 us
    ppermute x16, starting transfers between devices: 43.6 us -> 42.1 us  [permute(): lax.ppermute(value, AXES, [(i, j) for i, j in pairs if 0 <= j < devices])]
  transfers between devices with their start and end apart: 16 -> 16, of which waited for: 6 -> 7; matrix products, arithmetic and copies ran while one was open for 1% -> 1% of each run, Pallas kernels for 12% -> 12%
where the time goes in v7:
time: 80.8 us; the launch traced here: 80.5 us
  starting transfers between devices  42.1 us (52%)
  waiting for transfers between devices  20.1 us (25%)
  Pallas kernels  14.5 us (18%)
  local copies, waits for them, and re-layouts  1.59 us (2%)
  other arithmetic  1.23 us (2%)
  between operations  0.99 us (1%)
    ppermute x16, starting transfers between devices, permute(): lax.ppermute(value, AXES, [(i, j) for i, j in pairs if 0 <= j < devices])  42.1 us
    ppermute x16, waiting for transfers between devices, permute(): lax.ppermute(value, AXES, [(i, j) for i, j in pairs if 0 <= j < devices])  20.1 us
    pallas_call x1, Pallas kernels, own_part(): pl.pallas_call(own_kernel_products, out_shape=(jax.ShapeDtypeStruct((4 *...  2.96 us
    pallas_call x1, Pallas kernels, near_part(): pl.pallas_call(near_kernel, out_shape=jax.ShapeDtypeStruct((2, BAND, BS,...  2.68 us
    pallas_call x1, Pallas kernels, mid_part(): pl.pallas_call(mid_kernel, out_shape=jax.ShapeDtypeStruct(near_rows.shape...  2.26 us
    pallas_call x1, Pallas kernels, away_part(): pl.pallas_call(away_kernel, out_shape=[jax.ShapeDtypeStruct(shape, x1.dty...  1.94 us
  transfers between devices with their start and end apart: 16, of which 7 were waited for; matrix products, arithmetic and copies ran while one was open for 1% of the time, Pallas kernels for 12%

profile of v7, /device:TPU:0, one launch (start us, length us, event | category | flops | bytes accessed | tf_op | source)
XLA Modules:
  0.0 80.5 jit_solution(2106066312838663707)
XLA Ops:
  0.6 0.7 pad_add_fusion.table
  1.3 1.5 %copy-done = bf16[2,27,128,128]{3,2,1,0:T(8,128)(2,1)S(1)} copy-done((bf16[2,27,128,128]{3,2,1,0:T(8,128)(2,1)S(1)}, bf16[2,27,128,128]{3,2,1,0:T(8,128)(2,1)}, u32[]{:S(2)}) %copy-start) | copy-done | bytes 1769496
  2.8 1.4 %own_rows.1 = (bf16[2,27,128,128]{3,2,1,0:T(8,128)(2,1)S(1)}, bf16[2,27,128,128]{3,2,1,0:T(8,128)(2,1)S(1)}, s32[2,27,1,128]{3,2,1,0:T(1,128)S(1)}) custom-call(s32[3,27]{1,0:T(4,128)S(1)} %pad_add_fusion.table, bf16[2,27,128,128]{3,2,1,0:T(8,128)(2,1)S(1)} %copy-done), custom_call_target="tpu_custom_call" | custom-call | tf_op jit(solution)/shard_map/own_rows/pallas_call | solution.py:105
  4.2 0.6 collective-permute-start
  4.7 3.3 %collective-permute-done.part = bf16[2,27,128,128]{3,2,1,0:T(8,128)(2,1)S(1)} collective-permute-done((bf16[2,27,128,128]{3,2,1,0:T(8,128)(2,1)S(1)}, bf16[2,27,128,128]{3,2,1,0:T(8,128)(2,1)S(1)}, u32[]{:S(2)}, u32[]{:S(2)}) %collective-permute-start) | collective-permute-done | bytes 1769504 | tf_op jit(solution)/shard_map/ppermute | solution.py:32
  8.1 0.4 first_packs.1
  8.4 0.8 %collective-permute-start.1 = (bf16[74,128,128]{2,1,0:T(8,128)(2,1)S(1)}, bf16[74,128,128]{2,1,0:T(8,128)(2,1)S(1)}, u32[]{:S(2)}, u32[]{:S(2)}) collective-permute-start(bf16[74,128,128]{2,1,0:T(8,128)(2,1)S(1)} %get-tuple-element.35), channel_id=1, source_target_pairs={{1,2},{2,1},{5,6},{6,5},{9,10},{10,9},{13,14},{14,13},{17,18},{18,... | collective-permute-start | bytes 7274504 | tf_op jit(solution)/shard_map/ppermute | solution.py:32
  9.3 0.8 collective-permute-start.2
  10.1 10.0 %collective-permute-start.3 = (bf16[1,128,128]{2,1,0:T(8,128)(2,1)S(1)}, bf16[1,128,128]{2,1,0:T(8,128)(2,1)S(1)}, u32[]{:S(2)}, u32[]{:S(2)}) collective-permute-start(bf16[1,128,128]{2,1,0:T(8,128)(2,1)S(1)} %get-tuple-element.37), channel_id=1, source_target_pairs={{0,6},{4,10},{7,1},{8,14},{11,5},{12,18},{15,9},{16,22},{19,13},{2... | collective-permute-start | bytes 98312 | tf_op jit(solution)/shard_map/ppermute | solution.py:32
  20.1 3.0 %own_part.1 = (bf16[512,512]{1,0:T(8,128)(2,1)S(1)}, f32[256,512]{1,0:T(8,128)S(1)}, bf16[512,1792]{1,0:T(8,128)(2,1)S(1)}, bf16[512,1280]{1,0:T(8,128)(2,1)S(1)}, f32[2,128]{1,0:T(2,128)S(1)}) custom-call(bf16[2,27,128,128]{3,2,1,0:T(8,128)(2,1)S(1)} %get-tuple-element.29.mine, bf16[2,27,128,128]{3,2,1,0:T(8,128)(2,1)S(1)} %collective-permute-done.part), custom_call_target="tpu_custom_call" | custom-call | flops 2000000000 | bytes 1000000 | tf_op jit(solution)/shard_map/own_part/pallas_call | solution.py:269
  23.5 1.3 %collective-permute-start.5 = (bf16[45,128,128]{2,1,0:T(8,128)(2,1)S(1)}, bf16[45,128,128]{2,1,0:T(8,128)(2,1)S(1)}, u32[]{:S(2)}, u32[]{:S(2)}) collective-permute-start(bf16[45,128,128]{2,1,0:T(8,128)(2,1)S(1)} %join_cross.1), channel_id=1, source_target_pairs={{1,0},{2,3},{5,4},{6,7},{9,8},{10,11},{13,12},{14,15},{17,16},{18,... | collective-permute-start | bytes 4423688 | tf_op jit(solution)/shard_map/ppermute | solution.py:32
  24.8 1.3 %collective-permute-start.10 = (bf16[44,128,128]{2,1,0:T(8,128)(2,1)S(1)}, bf16[44,128,128]{2,1,0:T(8,128)(2,1)S(1)}, u32[]{:S(2)}, u32[]{:S(2)}) collective-permute-start(bf16[44,128,128]{2,1,0:T(8,128)(2,1)S(1)} %get-tuple-element.45), channel_id=1, source_target_pairs={{1,3},{2,0},{5,7},{6,4},{9,11},{10,8},{13,15},{14,12},{17,19},{18,... | collective-permute-start | bytes 4325384 | tf_op jit(solution)/shard_map/ppermute | solution.py:32
  26.1 0.7 collective-permute-start.11
  26.8 4.7 %collective-permute-start.4 = (bf16[1,128,128]{2,1,0:T(8,128)(2,1)S(1)}, bf16[1,128,128]{2,1,0:T(8,128)(2,1)S(1)}, u32[]{:S(2)}, u32[]{:S(2)}) collective-permute-start(bf16[1,128,128]{2,1,0:T(8,128)(2,1)S(1)} %get-tuple-element.38), channel_id=1, source_target_pairs={{0,8},{4,12},{8,16},{11,3},{12,20},{15,7},{16,24},{19,11},{20,28},... | collective-permute-start | bytes 98312 | tf_op jit(solution)/shard_map/ppermute | solution.py:32
  31.5 0.7 collective-permute-start.13
  32.2 0.9 %collective-permute-done.4._diagonal.single = bf16[1,128,128]{2,1,0:T(8,128)(2,1)S(1)} collective-permute-done((bf16[1,128,128]{2,1,0:T(8,128)(2,1)S(1)}, bf16[1,128,128]{2,1,0:T(8,128)(2,1)S(1)}, u32[]{:S(2)}, u32[]{:S(2)}) %collective-permute-start.4) | collective-permute-done | bytes 32800 | tf_op jit(solution)/shard_map/ppermute | solution.py:32
  33.0 0.9 %collective-permute-start.12 = (bf16[14,128,128]{2,1,0:T(8,128)(2,1)S(1)}, bf16[14,128,128]{2,1,0:T(8,128)(2,1)S(1)}, u32[]{:S(2)}, u32[]{:S(2)}) collective-permute-start(bf16[14,128,128]{2,1,0:T(8,128)(2,1)S(1)} %get-tuple-element.41._), channel_id=1, source_target_pairs={{2,4},{5,3},{6,8},{9,7},{10,12},{13,11},{14,16},{17,15},{18,20},{2... | collective-permute-start | bytes 1376264 | tf_op jit(solution)/shard_map/ppermute | solution.py:32
  33.9 1.5 %cross_part.1 = (f32[512,1280]{1,0:T(8,128)S(1)}, f32[2,128]{1,0:T(2,128)S(1)}) custom-call(bf16[512,1792]{1,0:T(8,128)(2,1)S(1)} %get-tuple-element.31.near_rows, bf16[512,1280]{1,0:T(8,128)(2,1)S(1)} %get-tuple-element.33.far_rows, f32[2,128]{1,0:T(2,128)S(1)} %get-tuple-element.34.before._sums._diagonal, ...), custom_call_target="tpu_custom_call" | custom-call | flops 1000000000 | bytes 1000000 | tf_op jit(solution)/shard_map/cross_part/pallas_call | solution.py:317
  35.5 9.8 %collective-permute-done.5.swapped = bf16[45,128,128]{2,1,0:T(8,128)(2,1)S(1)} collective-permute-done((bf16[45,128,128]{2,1,0:T(8,128)(2,1)S(1)}, bf16[45,128,128]{2,1,0:T(8,128)(2,1)S(1)}, u32[]{:S(2)}, u32[]{:S(2)}) %collective-permute-start.5) | collective-permute-done | bytes 1474592 | tf_op jit(solution)/shard_map/ppermute | solution.py:32
  45.3 2.5 %collective-permute-start.6 = (f32[2]{0:T(128)S(1)}, f32[2]{0:T(128)S(1)}, u32[]{:S(2)}, u32[]{:S(2)}) collective-permute-start(f32[2]{0:T(128)S(1)} %slice_reduce_fusion), channel_id=1, source_target_pairs={{0,16},{1,17},{2,18},{3,19},{4,20},{5,21},{6,22},{7,23},{8,24},{9,... | collective-permute-start | bytes 32 | tf_op jit(solution)/shard_map/ppermute | solution.py:32
  47.8 2.3 %mid_part.1.partial = f32[512,1792]{1,0:T(8,128)S(1)} custom-call(bf16[512,512]{1,0:T(8,128)(2,1)S(1)} %get-tuple-element.32.own, bf16[512,1792]{1,0:T(8,128)(2,1)S(1)} %get-tuple-element.31.near_rows, bf16[512,1280]{1,0:T(8,128)(2,1)S(1)} %get-tuple-element.33.far_rows, f32[512,1280]{1,0:T(8,128)S(1)} %get-tuple-element.39.first, ...), custom_call_target="tpu_custom_call" | custom-call | flops 2000000000 | bytes 1000000 | tf_op jit(solution)/shard_map/mid_part/pallas_call | solution.py:345
  50.1 10.3 %collective-permute-start.7 = (f32[2]{0:T(128)S(1)}, f32[2]{0:T(128)S(1)}, u32[]{:S(2)}, u32[]{:S(2)}) collective-permute-start(f32[2]{0:T(128)S(1)} %add.23), channel_id=1, source_target_pairs={{0,1},{1,0},{2,3},{3,2},{4,5},{5,4},{6,7},{7,6},{8,9},{9,8},{10,11... | collective-permute-start | bytes 32 | tf_op jit(solution)/shard_map/ppermute | solution.py:32
  60.4 0.8 %collective-permute-done.7 = f32[2]{0:T(128)S(1)} collective-permute-done((f32[2]{0:T(128)S(1)}, f32[2]{0:T(128)S(1)}, u32[]{:S(2)}, u32[]{:S(2)}) %collective-permute-start.7) | collective-permute-done | bytes 40 | tf_op jit(solution)/shard_map/ppermute | solution.py:32
  61.2 3.5 %collective-permute-done.8 = f32[2]{0:T(128)S(1)} collective-permute-done((f32[2]{0:T(128)S(1)}, f32[2]{0:T(128)S(1)}, u32[]{:S(2)}, u32[]{:S(2)}) %collective-permute-start.8) | collective-permute-done | bytes 40 | tf_op jit(solution)/shard_map/ppermute | solution.py:32
  64.8 5.5 %collective-permute-start.9 = (f32[2]{0:T(128)S(1)}, f32[2]{0:T(128)S(1)}, u32[]{:S(2)}, u32[]{:S(2)}) collective-permute-start(f32[2]{0:T(128)S(1)} %add.25), channel_id=1, source_target_pairs={{0,8},{1,9},{2,10},{3,11},{4,12},{5,13},{6,14},{7,15},{8,0},{9,1},... | collective-permute-start | bytes 32 | tf_op jit(solution)/shard_map/ppermute | solution.py:32
  70.3 1.6 %collective-permute-done.9 = f32[2]{0:T(128)S(1)} collective-permute-done((f32[2]{0:T(128)S(1)}, f32[2]{0:T(128)S(1)}, u32[]{:S(2)}, u32[]{:S(2)}) %collective-permute-start.9) | collective-permute-done | bytes 40 | tf_op jit(solution)/shard_map/ppermute | solution.py:32
  71.9 1.9 %away_part.1 = (bf16[21,128,128]{2,1,0:T(8,128)(2,1)S(1)}, bf16[512,1792]{1,0:T(8,128)(2,1)S(1)}, bf16[512,1280]{1,0:T(8,128)(2,1)S(1)}, bf16[768,768]{1,0:T(8,128)(2,1)S(1)}) custom-call(bf16[512,1792]{1,0:T(8,128)(2,1)S(1)} %get-tuple-element.31.near_rows, f32[512,1792]{1,0:T(8,128)S(1)} %mid_part.1.partial, ...), custom_call_target="tpu_custom_call" | custom-call | flops 2000000000 | bytes 1000000 | tf_op jit(solution)/shard_map/away_part/pallas_call | solution.py:414
  73.9 1.4 %collective-permute-start.14 = (bf16[21,128,128]{2,1,0:T(8,128)(2,1)S(1)}, bf16[21,128,128]{2,1,0:T(8,128)(2,1)S(1)}, u32[]{:S(2)}, u32[]{:S(2)}) collective-permute-start(bf16[21,128,128]{2,1,0:T(8,128)(2,1)S(1)} %get-tuple-element.48), channel_id=1, source_target_pairs={{0,1},{1,0},{2,3},{3,2},{4,5},{5,4},{6,7},{7,6},{8,9},{9,8},{10,11... | collective-permute-start | bytes 2064392 | tf_op jit(solution)/shard_map/ppermute | solution.py:32
  75.3 0.8 collective-permute-start.15
  76.0 2.7 %near_part.1._ = bf16[2,27,128,128]{3,2,1,0:T(8,128)(2,1)} custom-call(s32[2,27,1,128]{3,2,1,0:T(1,128)S(1)} %get-tuple-element.28.mask, bf16[512,1792]{1,0:T(8,128)(2,1)S(1)} %get-tuple-element.31.near_rows, f32[512,1792]{1,0:T(8,128)S(1)} %mid_part.1.partial, f32[256,512]{1,0:T(8,128)S(1)} %get-tuple-element.49.inner, ...), custom_call_target="tpu_custom_call" | custom-call | flops 1000000000 | bytes 1000000 | tf_op jit(solution)/shard_map/near_part/pallas_call | solution.py:456
  78.8 0.5 add.27
  79.3 1.1 %join.1 = bf16[2,27,128,128]{3,2,1,0:T(8,128)(2,1)} custom-call(s32[2,27,1,128]{3,2,1,0:T(1,128)S(1)} %get-tuple-element.28.mask, bf16[21,128,128]{2,1,0:T(8,128)(2,1)S(1)} %collective-permute-done.14.came, bf16[2,27,128,128]{3,2,1,0:T(8,128)(2,1)} %near_part.1._), custom_call_target="tpu_custom_call", output_to_operand_aliasing={{}: (2, {})} | custom-call | tf_op jit(solution)/shard_map/join/pallas_call | solution.py:497
  (19 shorter events, 0.6 us)
Async XLA Ops:
  1.3 1.5 %copy-start = (bf16[2,27,128,128]{3,2,1,0:T(8,128)(2,1)S(1)}, bf16[2,27,128,128]{3,2,1,0:T(8,128)(2,1)}, u32[]{:S(2)}) copy-start(bf16[2,27,128,128]{3,2,1,0:T(8,128)(2,1)} %blocks.1) | copy-start | bytes 5308420
  4.2 3.9 %collective-permute-start = (bf16[2,27,128,128]{3,2,1,0:T(8,128)(2,1)S(1)}, bf16[2,27,128,128]{3,2,1,0:T(8,128)(2,1)S(1)}, u32[]{:S(2)}, u32[]{:S(2)}) collective-permute-start(bf16[2,27,128,128]{3,2,1,0:T(8,128)(2,1)S(1)} %get-tuple-element.30), channel_id=1, source_target_pairs={{0,1},{1,0},{2,3},{3,2},{4,5},{5,4},{6,7},{7,6},{8,9},{9,8},{10,11... | collective-permute-start | bytes 5308424 | tf_op jit(solution)/shard_map/ppermute | solution.py:32
  8.4 14.6 %collective-permute-start.1 = (bf16[74,128,128]{2,1,0:T(8,128)(2,1)S(1)}, bf16[74,128,128]{2,1,0:T(8,128)(2,1)S(1)}, u32[]{:S(2)}, u32[]{:S(2)}) collective-permute-start(bf16[74,128,128]{2,1,0:T(8,128)(2,1)S(1)} %get-tuple-element.35), channel_id=1, source_target_pairs={{1,2},{2,1},{5,6},{6,5},{9,10},{10,9},{13,14},{14,13},{17,18},{18,... | collective-permute-start | bytes 7274504 | tf_op jit(solution)/shard_map/ppermute | solution.py:32
  9.3 13.8 %collective-permute-start.2 = (bf16[62,128,128]{2,1,0:T(8,128)(2,1)S(1)}, bf16[62,128,128]{2,1,0:T(8,128)(2,1)S(1)}, u32[]{:S(2)}, u32[]{:S(2)}) collective-permute-start(bf16[62,128,128]{2,1,0:T(8,128)(2,1)S(1)} %get-tuple-element.36), channel_id=1, source_target_pairs={{2,6},{5,1},{6,10},{9,5},{10,14},{13,9},{14,18},{17,13},{18,22},{2... | collective-permute-start | bytes 6094856 | tf_op jit(solution)/shard_map/ppermute | solution.py:32
  10.1 13.3 %collective-permute-start.3 = (bf16[1,128,128]{2,1,0:T(8,128)(2,1)S(1)}, bf16[1,128,128]{2,1,0:T(8,128)(2,1)S(1)}, u32[]{:S(2)}, u32[]{:S(2)}) collective-permute-start(bf16[1,128,128]{2,1,0:T(8,128)(2,1)S(1)} %get-tuple-element.37), channel_id=1, source_target_pairs={{0,6},{4,10},{7,1},{8,14},{11,5},{12,18},{15,9},{16,22},{19,13},{2... | collective-permute-start | bytes 98312 | tf_op jit(solution)/shard_map/ppermute | solution.py:32
  23.5 21.9 %collective-permute-start.5 = (bf16[45,128,128]{2,1,0:T(8,128)(2,1)S(1)}, bf16[45,128,128]{2,1,0:T(8,128)(2,1)S(1)}, u32[]{:S(2)}, u32[]{:S(2)}) collective-permute-start(bf16[45,128,128]{2,1,0:T(8,128)(2,1)S(1)} %join_cross.1), channel_id=1, source_target_pairs={{1,0},{2,3},{5,4},{6,7},{9,8},{10,11},{13,12},{14,15},{17,16},{18,... | collective-permute-start | bytes 4423688 | tf_op jit(solution)/shard_map/ppermute | solution.py:32
  24.8 47.1 %collective-permute-start.10 = (bf16[44,128,128]{2,1,0:T(8,128)(2,1)S(1)}, bf16[44,128,128]{2,1,0:T(8,128)(2,1)S(1)}, u32[]{:S(2)}, u32[]{:S(2)}) collective-permute-start(bf16[44,128,128]{2,1,0:T(8,128)(2,1)S(1)} %get-tuple-element.45), channel_id=1, source_target_pairs={{1,3},{2,0},{5,7},{6,4},{9,11},{10,8},{13,15},{14,12},{17,19},{18,... | collective-permute-start | bytes 4325384 | tf_op jit(solution)/shard_map/ppermute | solution.py:32
  26.1 45.8 %collective-permute-start.11 = (bf16[32,128,128]{2,1,0:T(8,128)(2,1)S(1)}, bf16[32,128,128]{2,1,0:T(8,128)(2,1)S(1)}, u32[]{:S(2)}, u32[]{:S(2)}) collective-permute-start(bf16[32,128,128]{2,1,0:T(8,128)(2,1)S(1)} %get-tuple-element.46), channel_id=1, source_target_pairs={{1,4},{5,8},{6,3},{9,12},{10,7},{13,16},{14,11},{17,20},{18,15},{2... | collective-permute-start | bytes 3145736 | tf_op jit(solution)/shard_map/ppermute | solution.py:32
  26.8 6.2 %collective-permute-start.4 = (bf16[1,128,128]{2,1,0:T(8,128)(2,1)S(1)}, bf16[1,128,128]{2,1,0:T(8,128)(2,1)S(1)}, u32[]{:S(2)}, u32[]{:S(2)}) collective-permute-start(bf16[1,128,128]{2,1,0:T(8,128)(2,1)S(1)} %get-tuple-element.38), channel_id=1, source_target_pairs={{0,8},{4,12},{8,16},{11,3},{12,20},{15,7},{16,24},{19,11},{20,28},... | collective-permute-start | bytes 98312 | tf_op jit(solution)/shard_map/ppermute | solution.py:32
  31.5 40.4 %collective-permute-start.13 = (bf16[15,128,128]{2,1,0:T(8,128)(2,1)S(1)}, bf16[15,128,128]{2,1,0:T(8,128)(2,1)S(1)}, u32[]{:S(2)}, u32[]{:S(2)}) collective-permute-start(bf16[15,128,128]{2,1,0:T(8,128)(2,1)S(1)} %get-tuple-element.47), channel_id=1, source_target_pairs={{2,6},{5,1},{6,10},{9,5},{10,14},{13,9},{14,18},{17,13},{18,22},{2... | collective-permute-start | bytes 1474568 | tf_op jit(solution)/shard_map/ppermute | solution.py:32
  33.0 38.8 %collective-permute-start.12 = (bf16[14,128,128]{2,1,0:T(8,128)(2,1)S(1)}, bf16[14,128,128]{2,1,0:T(8,128)(2,1)S(1)}, u32[]{:S(2)}, u32[]{:S(2)}) collective-permute-start(bf16[14,128,128]{2,1,0:T(8,128)(2,1)S(1)} %get-tuple-element.41._), channel_id=1, source_target_pairs={{2,4},{5,3},{6,8},{9,7},{10,12},{13,11},{14,16},{17,15},{18,20},{2... | collective-permute-start | bytes 1376264 | tf_op jit(solution)/shard_map/ppermute | solution.py:32
  45.3 4.7 %collective-permute-start.6 = (f32[2]{0:T(128)S(1)}, f32[2]{0:T(128)S(1)}, u32[]{:S(2)}, u32[]{:S(2)}) collective-permute-start(f32[2]{0:T(128)S(1)} %slice_reduce_fusion), channel_id=1, source_target_pairs={{0,16},{1,17},{2,18},{3,19},{4,20},{5,21},{6,22},{7,23},{8,24},{9,... | collective-permute-start | bytes 32 | tf_op jit(solution)/shard_map/ppermute | solution.py:32
  50.1 11.1 %collective-permute-start.7 = (f32[2]{0:T(128)S(1)}, f32[2]{0:T(128)S(1)}, u32[]{:S(2)}, u32[]{:S(2)}) collective-permute-start(f32[2]{0:T(128)S(1)} %add.23), channel_id=1, source_target_pairs={{0,1},{1,0},{2,3},{3,2},{4,5},{5,4},{6,7},{7,6},{8,9},{9,8},{10,11... | collective-permute-start | bytes 32 | tf_op jit(solution)/shard_map/ppermute | solution.py:32
  61.2 3.5 %collective-permute-start.8 = (f32[2]{0:T(128)S(1)}, f32[2]{0:T(128)S(1)}, u32[]{:S(2)}, u32[]{:S(2)}) collective-permute-start(f32[2]{0:T(128)S(1)} %add.24), channel_id=1, source_target_pairs={{0,2},{1,3},{2,0},{3,1},{4,6},{5,7},{6,4},{7,5},{8,10},{9,11},{10,... | collective-permute-start | bytes 32 | tf_op jit(solution)/shard_map/ppermute | solution.py:32
  64.8 7.1 %collective-permute-start.9 = (f32[2]{0:T(128)S(1)}, f32[2]{0:T(128)S(1)}, u32[]{:S(2)}, u32[]{:S(2)}) collective-permute-start(f32[2]{0:T(128)S(1)} %add.25), channel_id=1, source_target_pairs={{0,8},{1,9},{2,10},{3,11},{4,12},{5,13},{6,14},{7,15},{8,0},{9,1},... | collective-permute-start | bytes 32 | tf_op jit(solution)/shard_map/ppermute | solution.py:32
  73.9 5.5 %collective-permute-start.14 = (bf16[21,128,128]{2,1,0:T(8,128)(2,1)S(1)}, bf16[21,128,128]{2,1,0:T(8,128)(2,1)S(1)}, u32[]{:S(2)}, u32[]{:S(2)}) collective-permute-start(bf16[21,128,128]{2,1,0:T(8,128)(2,1)S(1)} %get-tuple-element.48), channel_id=1, source_target_pairs={{0,1},{1,0},{2,3},{3,2},{4,5},{5,4},{6,7},{7,6},{8,9},{9,8},{10,11... | collective-permute-start | bytes 2064392 | tf_op jit(solution)/shard_map/ppermute | solution.py:32
  75.3 3.5 %collective-permute-start.15 = (f32[2]{0:T(128)S(1)}, f32[2]{0:T(128)S(1)}, u32[]{:S(2)}, u32[]{:S(2)}) collective-permute-start(f32[2]{0:T(128)S(1)} %add.26), channel_id=1, source_target_pairs={{0,4},{1,5},{2,6},{3,7},{4,0},{5,1},{6,2},{7,3},{8,12},{9,13},{10,... | collective-permute-start | bytes 32 | tf_op jit(solution)/shard_map/ppermute | solution.py:32

commit v8 on v6

--- a/solution.py
+++ b/solution.py
@@ -10,6 +10,7 @@
 BAND = 2 * HALF + 1
 BS = 128
 NEAR = HALF
+MOVED = (3, 1)
 FAR = 12
 NCOL = NEAR + 1
 NEAR_W, OWN_W, FAR_W = NCOL * BS, 4 * BS, FAR * BS
@@ -112,8 +113,8 @@
     )(table, blocks)
 
 
-def low_slots(e):
-    return [w for w in range(HALF, BAND - 1 - e) if e < 3 or not 5 <= w - HALF + 1 + e <= 8]
+def low_slots(e, moved):
+    return [w for w in range(HALF, BAND - 1 - e) if e < 3 or not 5 <= w - HALF + 1 + e < 5 + moved]
 
 
 def first_kernel(mine, part, x1, z1, z2, corner, diagonal):
@@ -132,20 +133,22 @@
     for e in range(4):
         put(z2, e, range(HALF, BAND - 5 - e))
     for e in range(4):
-        put(x1, e, low_slots(e))
+        put(x1, e, low_slots(e, MOVED[0]))
     for e in range(4):
         put(z1, 3 - e, range(HALF, e, -1))
-    for e in range(4):
+    for e in range(MOVED[0]):
         put(z1, 3 - e, [HALF + 1 + e])
+    for e in range(MOVED[1]):
         put(z2, e, [HALF - 1 - e])
     corner[0] = part[1, BAND - 1]
     diagonal[0] = part[1, HALF]
 
 
 def first_packs(mine, part):
+    sizes = (76 - MOVED[0], 60 + MOVED[0], 30 + MOVED[1], 1, 1)
     return pl.pallas_call(
         first_kernel,
-        out_shape=[jax.ShapeDtypeStruct((n, BS, BS), mine.dtype) for n in (72, 64, 34, 1, 1)],
+        out_shape=[jax.ShapeDtypeStruct((n, BS, BS), mine.dtype) for n in sizes],
         in_specs=[VM] * 2,
         out_specs=[VM] * 5,
         compiler_params=params(),
@@ -157,14 +160,14 @@
     at1 = at2 = 0
     start_x, start_z = 30, 14
     for e in range(4):
-        for w in low_slots(e):
+        for w in low_slots(e, MOVED[1]):
             x2[at1] = z1[start_z + w - HALF]
             at1 += 1
         for n in range(5 - e):
             g[at2] = z1[start_z + n]
-            h[at2] = x1[start_x + n] if n < 4 - e or e < 3 else turned(z1[60])
+            h[at2] = x1[start_x + n] if n < 4 - e or e < 3 or not MOVED[0] else turned(z1[60])
             at2 += 1
-        start_x += len(low_slots(e))
+        start_x += len(low_slots(e, MOVED[0]))
         start_z += 13 - e
     h[at2] = z1[14]
 
@@ -172,7 +175,7 @@
 def second_packs(x1, z1, sums, diagonal):
     return pl.pallas_call(
         second_kernel,
-        out_shape=[jax.ShapeDtypeStruct((n, BS, BS), x1.dtype) for n in (42, 14, 15)],
+        out_shape=[jax.ShapeDtypeStruct((n, BS, BS), x1.dtype) for n in (46 - MOVED[1], 14, 15)],
         in_specs=[VM] * 4,
         out_specs=[VM] * 3,
         compiler_params=params(),
@@ -366,12 +369,15 @@
         if t >= LOW:
             start = 14 + sum(13 - n for n in range(t - LOW))
             return jnp.where(facing, z1[start + s - t], z2[near_start(t) + s - t])
-        if t == 4 and LOW <= s < LAST:
-            at = s - LOW
-            return turned(jnp.where(facing, z1[60 + at], z2[30 + at]))
-        slots = low_slots(t - 1)
-        at = sum(len(low_slots(n)) for n in range(t - 1)) + slots.index(HALF + s - t)
-        return jnp.where(facing, x1[30 + at], x2[at])
+        found = []
+        for moved, straight, start, along, more in zip(MOVED, (x1, x2), (30, 0), (z1, z2), (60, 30)):
+            if t == 4 and LOW <= s < LOW + moved:
+                found.append(turned(along[more + s - LOW]))
+            else:
+                at = sum(len(low_slots(n, moved)) for n in range(t - 1))
+                at += low_slots(t - 1, moved).index(HALF + s - t)
+                found.append(straight[start + at])
+        return jnp.where(facing, *found)
 
     fill_pairs(block, range(1, LOW), 1, pairs1)
     fill_pairs(block, range(LOW, LAST), LOW, pairs2)
@@ -542,13 +548,13 @@
     first, sums = cross_part(near_rows, far_rows, sums, x1, z1, corner, diagonal)
     sums, swapped = lax.optimization_barrier((sums[:, 0], swapped))
     steps = [1 << n for n in range(lax.axis_size(AXES).bit_length() - 1)]
-    sums = sum_over(sums, steps[4:] + steps[:1] + steps[1:2] + steps[3:4])
+    sums = sum_over(sums, steps[4:] + steps[:1] + steps[1:3])
     partial = mid_part(own, near_rows, far_rows, first, swapped)
     partial, sums = lax.optimization_barrier((partial, sums))
     away, *pairs = away_part(near_rows, partial, x1, x2, z1, z2, g, h, diagonal)
     came = to_partner(away)
     out = near_part(mask, near_rows, partial, inside, *pairs)
-    traces = sum_over(sums, steps[2:3])
+    traces = sum_over(sums, steps[3:4])
     square = join(mask, came, out)
     return square, traces
 

time: 82.2 us -> 80.7 us (0.982)
  starting transfers between devices: 43.6 us -> 42.5 us
    ppermute x16, starting transfers between devices: 43.6 us -> 42.5 us  [permute(): lax.ppermute(value, AXES, [(i, j) for i, j in pairs if 0 <= j < devices])]
where the time goes in v8:
time: 80.7 us; the launch traced here: 80.4 us
  starting transfers between devices  42.5 us (53%)
  waiting for transfers between devices  19.7 us (24%)
  Pallas kernels  14.4 us (18%)
  local copies, waits for them, and re-layouts  1.59 us (2%)
  other arithmetic  1.23 us (2%)
  between operations  1 us (1%)
    ppermute x16, starting transfers between devices, permute(): lax.ppermute(value, AXES, [(i, j) for i, j in pairs if 0 <= j < devices])  42.5 us
    ppermute x16, waiting for transfers between devices, permute(): lax.ppermute(value, AXES, [(i, j) for i, j in pairs if 0 <= j < devices])  19.7 us
    pallas_call x1, Pallas kernels, own_part(): pl.pallas_call(own_kernel_products, out_shape=(jax.ShapeDtypeStruct((4 *...  2.96 us
    pallas_call x1, Pallas kernels, near_part(): pl.pallas_call(near_kernel, out_shape=jax.ShapeDtypeStruct((2, BAND, BS,...  2.68 us
    pallas_call x1, Pallas kernels, mid_part(): pl.pallas_call(mid_kernel, out_shape=jax.ShapeDtypeStruct(near_rows.shape...  2.29 us
    pallas_call x1, Pallas kernels, away_part(): pl.pallas_call(away_kernel, out_shape=[jax.ShapeDtypeStruct(shape, x1.dty...  1.85 us
  transfers between devices with their start and end apart: 16, of which 6 were waited for; matrix products, arithmetic and copies ran while one was open for 1% of the time, Pallas kernels for 12%

profile of v8, /device:TPU:0, one launch (start us, length us, event | category | flops | bytes accessed | tf_op | source)
XLA Modules:
  0.0 80.4 jit_solution(18319762024579466603)
XLA Ops:
  0.6 0.7 pad_add_fusion.table
  1.3 1.5 %copy-done = bf16[2,27,128,128]{3,2,1,0:T(8,128)(2,1)S(1)} copy-done((bf16[2,27,128,128]{3,2,1,0:T(8,128)(2,1)S(1)}, bf16[2,27,128,128]{3,2,1,0:T(8,128)(2,1)}, u32[]{:S(2)}) %copy-start) | copy-done | bytes 1769496
  2.8 1.3 %own_rows.1 = (bf16[2,27,128,128]{3,2,1,0:T(8,128)(2,1)S(1)}, bf16[2,27,128,128]{3,2,1,0:T(8,128)(2,1)S(1)}, s32[2,27,1,128]{3,2,1,0:T(1,128)S(1)}) custom-call(s32[3,27]{1,0:T(4,128)S(1)} %pad_add_fusion.table, bf16[2,27,128,128]{3,2,1,0:T(8,128)(2,1)S(1)} %copy-done), custom_call_target="tpu_custom_call" | custom-call | tf_op jit(solution)/shard_map/own_rows/pallas_call | solution.py:105
  4.2 0.6 collective-permute-start
  4.7 3.3 %collective-permute-done.part = bf16[2,27,128,128]{3,2,1,0:T(8,128)(2,1)S(1)} collective-permute-done((bf16[2,27,128,128]{3,2,1,0:T(8,128)(2,1)S(1)}, bf16[2,27,128,128]{3,2,1,0:T(8,128)(2,1)S(1)}, u32[]{:S(2)}, u32[]{:S(2)}) %collective-permute-start) | collective-permute-done | bytes 1769504 | tf_op jit(solution)/shard_map/ppermute | solution.py:32
  8.0 0.4 first_packs.1
  8.4 0.8 %collective-permute-start.1 = (bf16[73,128,128]{2,1,0:T(8,128)(2,1)S(1)}, bf16[73,128,128]{2,1,0:T(8,128)(2,1)S(1)}, u32[]{:S(2)}, u32[]{:S(2)}) collective-permute-start(bf16[73,128,128]{2,1,0:T(8,128)(2,1)S(1)} %get-tuple-element.35), channel_id=1, source_target_pairs={{1,2},{2,1},{5,6},{6,5},{9,10},{10,9},{13,14},{14,13},{17,18},{18,... | collective-permute-start | bytes 7176200 | tf_op jit(solution)/shard_map/ppermute | solution.py:32
  9.2 0.8 collective-permute-start.2
  10.0 10.0 %collective-permute-start.3 = (bf16[1,128,128]{2,1,0:T(8,128)(2,1)S(1)}, bf16[1,128,128]{2,1,0:T(8,128)(2,1)S(1)}, u32[]{:S(2)}, u32[]{:S(2)}) collective-permute-start(bf16[1,128,128]{2,1,0:T(8,128)(2,1)S(1)} %get-tuple-element.37), channel_id=1, source_target_pairs={{0,6},{4,10},{7,1},{8,14},{11,5},{12,18},{15,9},{16,22},{19,13},{2... | collective-permute-start | bytes 98312 | tf_op jit(solution)/shard_map/ppermute | solution.py:32
  20.0 3.0 %own_part.1 = (bf16[512,512]{1,0:T(8,128)(2,1)S(1)}, f32[256,512]{1,0:T(8,128)S(1)}, bf16[512,1792]{1,0:T(8,128)(2,1)S(1)}, bf16[512,1280]{1,0:T(8,128)(2,1)S(1)}, f32[2,128]{1,0:T(2,128)S(1)}) custom-call(bf16[2,27,128,128]{3,2,1,0:T(8,128)(2,1)S(1)} %get-tuple-element.29.mine, bf16[2,27,128,128]{3,2,1,0:T(8,128)(2,1)S(1)} %collective-permute-done.part), custom_call_target="tpu_custom_call" | custom-call | flops 2000000000 | bytes 1000000 | tf_op jit(solution)/shard_map/own_part/pallas_call | solution.py:271
  23.4 1.3 %collective-permute-start.5 = (bf16[45,128,128]{2,1,0:T(8,128)(2,1)S(1)}, bf16[45,128,128]{2,1,0:T(8,128)(2,1)S(1)}, u32[]{:S(2)}, u32[]{:S(2)}) collective-permute-start(bf16[45,128,128]{2,1,0:T(8,128)(2,1)S(1)} %join_cross.1), channel_id=1, source_target_pairs={{1,0},{2,3},{5,4},{6,7},{9,8},{10,11},{13,12},{14,15},{17,16},{18,... | collective-permute-start | bytes 4423688 | tf_op jit(solution)/shard_map/ppermute | solution.py:32
  24.7 1.3 %collective-permute-start.10 = (bf16[45,128,128]{2,1,0:T(8,128)(2,1)S(1)}, bf16[45,128,128]{2,1,0:T(8,128)(2,1)S(1)}, u32[]{:S(2)}, u32[]{:S(2)}) collective-permute-start(bf16[45,128,128]{2,1,0:T(8,128)(2,1)S(1)} %get-tuple-element.45), channel_id=1, source_target_pairs={{1,3},{2,0},{5,7},{6,4},{9,11},{10,8},{13,15},{14,12},{17,19},{18,... | collective-permute-start | bytes 4423688 | tf_op jit(solution)/shard_map/ppermute | solution.py:32
  26.0 0.7 collective-permute-start.11
  26.7 4.7 %collective-permute-start.4 = (bf16[1,128,128]{2,1,0:T(8,128)(2,1)S(1)}, bf16[1,128,128]{2,1,0:T(8,128)(2,1)S(1)}, u32[]{:S(2)}, u32[]{:S(2)}) collective-permute-start(bf16[1,128,128]{2,1,0:T(8,128)(2,1)S(1)} %get-tuple-element.38), channel_id=1, source_target_pairs={{0,8},{4,12},{8,16},{11,3},{12,20},{15,7},{16,24},{19,11},{20,28},... | collective-permute-start | bytes 98312 | tf_op jit(solution)/shard_map/ppermute | solution.py:32
  31.4 0.7 collective-permute-start.13
  32.1 0.9 %collective-permute-done.4._diagonal.single = bf16[1,128,128]{2,1,0:T(8,128)(2,1)S(1)} collective-permute-done((bf16[1,128,128]{2,1,0:T(8,128)(2,1)S(1)}, bf16[1,128,128]{2,1,0:T(8,128)(2,1)S(1)}, u32[]{:S(2)}, u32[]{:S(2)}) %collective-permute-start.4) | collective-permute-done | bytes 32800 | tf_op jit(solution)/shard_map/ppermute | solution.py:32
  33.0 0.9 %collective-permute-start.12 = (bf16[14,128,128]{2,1,0:T(8,128)(2,1)S(1)}, bf16[14,128,128]{2,1,0:T(8,128)(2,1)S(1)}, u32[]{:S(2)}, u32[]{:S(2)}) collective-permute-start(bf16[14,128,128]{2,1,0:T(8,128)(2,1)S(1)} %get-tuple-element.41._), channel_id=1, source_target_pairs={{2,4},{5,3},{6,8},{9,7},{10,12},{13,11},{14,16},{17,15},{18,20},{2... | collective-permute-start | bytes 1376264 | tf_op jit(solution)/shard_map/ppermute | solution.py:32
  33.9 1.5 %cross_part.1 = (f32[512,1280]{1,0:T(8,128)S(1)}, f32[2,128]{1,0:T(2,128)S(1)}) custom-call(bf16[512,1792]{1,0:T(8,128)(2,1)S(1)} %get-tuple-element.31.near_rows, bf16[512,1280]{1,0:T(8,128)(2,1)S(1)} %get-tuple-element.33.far_rows, f32[2,128]{1,0:T(2,128)S(1)} %get-tuple-element.34.before._sums._diagonal, ...), custom_call_target="tpu_custom_call" | custom-call | flops 1000000000 | bytes 1000000 | tf_op jit(solution)/shard_map/cross_part/pallas_call | solution.py:319
  35.5 9.5 %collective-permute-done.5.swapped = bf16[45,128,128]{2,1,0:T(8,128)(2,1)S(1)} collective-permute-done((bf16[45,128,128]{2,1,0:T(8,128)(2,1)S(1)}, bf16[45,128,128]{2,1,0:T(8,128)(2,1)S(1)}, u32[]{:S(2)}, u32[]{:S(2)}) %collective-permute-start.5) | collective-permute-done | bytes 1474592 | tf_op jit(solution)/shard_map/ppermute | solution.py:32
  45.0 3.1 %collective-permute-start.6 = (f32[2]{0:T(128)S(1)}, f32[2]{0:T(128)S(1)}, u32[]{:S(2)}, u32[]{:S(2)}) collective-permute-start(f32[2]{0:T(128)S(1)} %slice_reduce_fusion), channel_id=1, source_target_pairs={{0,16},{1,17},{2,18},{3,19},{4,20},{5,21},{6,22},{7,23},{8,24},{9,... | collective-permute-start | bytes 32 | tf_op jit(solution)/shard_map/ppermute | solution.py:32
  48.1 2.3 %mid_part.1.partial = f32[512,1792]{1,0:T(8,128)S(1)} custom-call(bf16[512,512]{1,0:T(8,128)(2,1)S(1)} %get-tuple-element.32.own, bf16[512,1792]{1,0:T(8,128)(2,1)S(1)} %get-tuple-element.31.near_rows, bf16[512,1280]{1,0:T(8,128)(2,1)S(1)} %get-tuple-element.33.far_rows, f32[512,1280]{1,0:T(8,128)S(1)} %get-tuple-element.39.first, ...), custom_call_target="tpu_custom_call" | custom-call | flops 2000000000 | bytes 1000000 | tf_op jit(solution)/shard_map/mid_part/pallas_call | solution.py:347
  50.4 10.3 %collective-permute-start.7 = (f32[2]{0:T(128)S(1)}, f32[2]{0:T(128)S(1)}, u32[]{:S(2)}, u32[]{:S(2)}) collective-permute-start(f32[2]{0:T(128)S(1)} %add.23), channel_id=1, source_target_pairs={{0,1},{1,0},{2,3},{3,2},{4,5},{5,4},{6,7},{7,6},{8,9},{9,8},{10,11... | collective-permute-start | bytes 32 | tf_op jit(solution)/shard_map/ppermute | solution.py:32
  60.8 0.8 %collective-permute-done.7 = f32[2]{0:T(128)S(1)} collective-permute-done((f32[2]{0:T(128)S(1)}, f32[2]{0:T(128)S(1)}, u32[]{:S(2)}, u32[]{:S(2)}) %collective-permute-start.7) | collective-permute-done | bytes 40 | tf_op jit(solution)/shard_map/ppermute | solution.py:32
  61.6 3.5 %collective-permute-done.8 = f32[2]{0:T(128)S(1)} collective-permute-done((f32[2]{0:T(128)S(1)}, f32[2]{0:T(128)S(1)}, u32[]{:S(2)}, u32[]{:S(2)}) %collective-permute-start.8) | collective-permute-done | bytes 40 | tf_op jit(solution)/shard_map/ppermute | solution.py:32
  65.1 4.1 %collective-permute-start.9 = (f32[2]{0:T(128)S(1)}, f32[2]{0:T(128)S(1)}, u32[]{:S(2)}, u32[]{:S(2)}) collective-permute-start(f32[2]{0:T(128)S(1)} %add.25), channel_id=1, source_target_pairs={{0,4},{1,5},{2,6},{3,7},{4,0},{5,1},{6,2},{7,3},{8,12},{9,13},{10,... | collective-permute-start | bytes 32 | tf_op jit(solution)/shard_map/ppermute | solution.py:32
  69.2 1.6 %collective-permute-done.9 = f32[2]{0:T(128)S(1)} collective-permute-done((f32[2]{0:T(128)S(1)}, f32[2]{0:T(128)S(1)}, u32[]{:S(2)}, u32[]{:S(2)}) %collective-permute-start.9) | collective-permute-done | bytes 40 | tf_op jit(solution)/shard_map/ppermute | solution.py:32
  70.9 1.9 %away_part.1 = (bf16[21,128,128]{2,1,0:T(8,128)(2,1)S(1)}, bf16[512,1792]{1,0:T(8,128)(2,1)S(1)}, bf16[512,1280]{1,0:T(8,128)(2,1)S(1)}, bf16[768,768]{1,0:T(8,128)(2,1)S(1)}) custom-call(bf16[512,1792]{1,0:T(8,128)(2,1)S(1)} %get-tuple-element.31.near_rows, f32[512,1792]{1,0:T(8,128)S(1)} %mid_part.1.partial, ...), custom_call_target="tpu_custom_call" | custom-call | flops 2000000000 | bytes 1000000 | tf_op jit(solution)/shard_map/away_part/pallas_call | solution.py:419
  72.7 0.6 collective-permute-start.14
  73.3 2.6 %collective-permute-start.15 = (f32[2]{0:T(128)S(1)}, f32[2]{0:T(128)S(1)}, u32[]{:S(2)}, u32[]{:S(2)}) collective-permute-start(f32[2]{0:T(128)S(1)} %add.26), channel_id=1, source_target_pairs={{0,8},{1,9},{2,10},{3,11},{4,12},{5,13},{6,14},{7,15},{8,0},{9,1},... | collective-permute-start | bytes 32 | tf_op jit(solution)/shard_map/ppermute | solution.py:32
  75.9 2.7 %near_part.1._ = bf16[2,27,128,128]{3,2,1,0:T(8,128)(2,1)} custom-call(s32[2,27,1,128]{3,2,1,0:T(1,128)S(1)} %get-tuple-element.28.mask, bf16[512,1792]{1,0:T(8,128)(2,1)S(1)} %get-tuple-element.31.near_rows, f32[512,1792]{1,0:T(8,128)S(1)} %mid_part.1.partial, f32[256,512]{1,0:T(8,128)S(1)} %get-tuple-element.49.inner, ...), custom_call_target="tpu_custom_call" | custom-call | flops 1000000000 | bytes 1000000 | tf_op jit(solution)/shard_map/near_part/pallas_call | solution.py:461
  78.6 0.5 add.27
  79.2 1.1 %join.1 = bf16[2,27,128,128]{3,2,1,0:T(8,128)(2,1)} custom-call(s32[2,27,1,128]{3,2,1,0:T(1,128)S(1)} %get-tuple-element.28.mask, bf16[21,128,128]{2,1,0:T(8,128)(2,1)S(1)} %collective-permute-done.14.came, bf16[2,27,128,128]{3,2,1,0:T(8,128)(2,1)} %near_part.1._), custom_call_target="tpu_custom_call", output_to_operand_aliasing={{}: (2, {})} | custom-call | tf_op jit(solution)/shard_map/join/pallas_call | solution.py:502
  (19 shorter events, 0.5 us)
Async XLA Ops:
  1.3 1.5 %copy-start = (bf16[2,27,128,128]{3,2,1,0:T(8,128)(2,1)S(1)}, bf16[2,27,128,128]{3,2,1,0:T(8,128)(2,1)}, u32[]{:S(2)}) copy-start(bf16[2,27,128,128]{3,2,1,0:T(8,128)(2,1)} %blocks.1) | copy-start | bytes 5308420
  4.2 3.9 %collective-permute-start = (bf16[2,27,128,128]{3,2,1,0:T(8,128)(2,1)S(1)}, bf16[2,27,128,128]{3,2,1,0:T(8,128)(2,1)S(1)}, u32[]{:S(2)}, u32[]{:S(2)}) collective-permute-start(bf16[2,27,128,128]{3,2,1,0:T(8,128)(2,1)S(1)} %get-tuple-element.30), channel_id=1, source_target_pairs={{0,1},{1,0},{2,3},{3,2},{4,5},{5,4},{6,7},{7,6},{8,9},{9,8},{10,11... | collective-permute-start | bytes 5308424 | tf_op jit(solution)/shard_map/ppermute | solution.py:32
  8.4 14.6 %collective-permute-start.1 = (bf16[73,128,128]{2,1,0:T(8,128)(2,1)S(1)}, bf16[73,128,128]{2,1,0:T(8,128)(2,1)S(1)}, u32[]{:S(2)}, u32[]{:S(2)}) collective-permute-start(bf16[73,128,128]{2,1,0:T(8,128)(2,1)S(1)} %get-tuple-element.35), channel_id=1, source_target_pairs={{1,2},{2,1},{5,6},{6,5},{9,10},{10,9},{13,14},{14,13},{17,18},{18,... | collective-permute-start | bytes 7176200 | tf_op jit(solution)/shard_map/ppermute | solution.py:32
  9.2 13.8 %collective-permute-start.2 = (bf16[63,128,128]{2,1,0:T(8,128)(2,1)S(1)}, bf16[63,128,128]{2,1,0:T(8,128)(2,1)S(1)}, u32[]{:S(2)}, u32[]{:S(2)}) collective-permute-start(bf16[63,128,128]{2,1,0:T(8,128)(2,1)S(1)} %get-tuple-element.36), channel_id=1, source_target_pairs={{2,6},{5,1},{6,10},{9,5},{10,14},{13,9},{14,18},{17,13},{18,22},{2... | collective-permute-start | bytes 6193160 | tf_op jit(solution)/shard_map/ppermute | solution.py:32
  10.0 13.3 %collective-permute-start.3 = (bf16[1,128,128]{2,1,0:T(8,128)(2,1)S(1)}, bf16[1,128,128]{2,1,0:T(8,128)(2,1)S(1)}, u32[]{:S(2)}, u32[]{:S(2)}) collective-permute-start(bf16[1,128,128]{2,1,0:T(8,128)(2,1)S(1)} %get-tuple-element.37), channel_id=1, source_target_pairs={{0,6},{4,10},{7,1},{8,14},{11,5},{12,18},{15,9},{16,22},{19,13},{2... | collective-permute-start | bytes 98312 | tf_op jit(solution)/shard_map/ppermute | solution.py:32
  23.4 21.6 %collective-permute-start.5 = (bf16[45,128,128]{2,1,0:T(8,128)(2,1)S(1)}, bf16[45,128,128]{2,1,0:T(8,128)(2,1)S(1)}, u32[]{:S(2)}, u32[]{:S(2)}) collective-permute-start(bf16[45,128,128]{2,1,0:T(8,128)(2,1)S(1)} %join_cross.1), channel_id=1, source_target_pairs={{1,0},{2,3},{5,4},{6,7},{9,8},{10,11},{13,12},{14,15},{17,16},{18,... | collective-permute-start | bytes 4423688 | tf_op jit(solution)/shard_map/ppermute | solution.py:32
  24.7 46.2 %collective-permute-start.10 = (bf16[45,128,128]{2,1,0:T(8,128)(2,1)S(1)}, bf16[45,128,128]{2,1,0:T(8,128)(2,1)S(1)}, u32[]{:S(2)}, u32[]{:S(2)}) collective-permute-start(bf16[45,128,128]{2,1,0:T(8,128)(2,1)S(1)} %get-tuple-element.45), channel_id=1, source_target_pairs={{1,3},{2,0},{5,7},{6,4},{9,11},{10,8},{13,15},{14,12},{17,19},{18,... | collective-permute-start | bytes 4423688 | tf_op jit(solution)/shard_map/ppermute | solution.py:32
  26.0 44.8 %collective-permute-start.11 = (bf16[31,128,128]{2,1,0:T(8,128)(2,1)S(1)}, bf16[31,128,128]{2,1,0:T(8,128)(2,1)S(1)}, u32[]{:S(2)}, u32[]{:S(2)}) collective-permute-start(bf16[31,128,128]{2,1,0:T(8,128)(2,1)S(1)} %get-tuple-element.46), channel_id=1, source_target_pairs={{1,4},{5,8},{6,3},{9,12},{10,7},{13,16},{14,11},{17,20},{18,15},{2... | collective-permute-start | bytes 3047432 | tf_op jit(solution)/shard_map/ppermute | solution.py:32
  26.7 6.3 %collective-permute-start.4 = (bf16[1,128,128]{2,1,0:T(8,128)(2,1)S(1)}, bf16[1,128,128]{2,1,0:T(8,128)(2,1)S(1)}, u32[]{:S(2)}, u32[]{:S(2)}) collective-permute-start(bf16[1,128,128]{2,1,0:T(8,128)(2,1)S(1)} %get-tuple-element.38), channel_id=1, source_target_pairs={{0,8},{4,12},{8,16},{11,3},{12,20},{15,7},{16,24},{19,11},{20,28},... | collective-permute-start | bytes 98312 | tf_op jit(solution)/shard_map/ppermute | solution.py:32
  31.4 39.4 %collective-permute-start.13 = (bf16[15,128,128]{2,1,0:T(8,128)(2,1)S(1)}, bf16[15,128,128]{2,1,0:T(8,128)(2,1)S(1)}, u32[]{:S(2)}, u32[]{:S(2)}) collective-permute-start(bf16[15,128,128]{2,1,0:T(8,128)(2,1)S(1)} %get-tuple-element.47), channel_id=1, source_target_pairs={{2,6},{5,1},{6,10},{9,5},{10,14},{13,9},{14,18},{17,13},{18,22},{2... | collective-permute-start | bytes 1474568 | tf_op jit(solution)/shard_map/ppermute | solution.py:32
  33.0 37.8 %collective-permute-start.12 = (bf16[14,128,128]{2,1,0:T(8,128)(2,1)S(1)}, bf16[14,128,128]{2,1,0:T(8,128)(2,1)S(1)}, u32[]{:S(2)}, u32[]{:S(2)}) collective-permute-start(bf16[14,128,128]{2,1,0:T(8,128)(2,1)S(1)} %get-tuple-element.41._), channel_id=1, source_target_pairs={{2,4},{5,3},{6,8},{9,7},{10,12},{13,11},{14,16},{17,15},{18,20},{2... | collective-permute-start | bytes 1376264 | tf_op jit(solution)/shard_map/ppermute | solution.py:32
  45.0 5.5 %collective-permute-start.6 = (f32[2]{0:T(128)S(1)}, f32[2]{0:T(128)S(1)}, u32[]{:S(2)}, u32[]{:S(2)}) collective-permute-start(f32[2]{0:T(128)S(1)} %slice_reduce_fusion), channel_id=1, source_target_pairs={{0,16},{1,17},{2,18},{3,19},{4,20},{5,21},{6,22},{7,23},{8,24},{9,... | collective-permute-start | bytes 32 | tf_op jit(solution)/shard_map/ppermute | solution.py:32
  50.4 11.1 %collective-permute-start.7 = (f32[2]{0:T(128)S(1)}, f32[2]{0:T(128)S(1)}, u32[]{:S(2)}, u32[]{:S(2)}) collective-permute-start(f32[2]{0:T(128)S(1)} %add.23), channel_id=1, source_target_pairs={{0,1},{1,0},{2,3},{3,2},{4,5},{5,4},{6,7},{7,6},{8,9},{9,8},{10,11... | collective-permute-start | bytes 32 | tf_op jit(solution)/shard_map/ppermute | solution.py:32
  61.6 3.5 %collective-permute-start.8 = (f32[2]{0:T(128)S(1)}, f32[2]{0:T(128)S(1)}, u32[]{:S(2)}, u32[]{:S(2)}) collective-permute-start(f32[2]{0:T(128)S(1)} %add.24), channel_id=1, source_target_pairs={{0,2},{1,3},{2,0},{3,1},{4,6},{5,7},{6,4},{7,5},{8,10},{9,11},{10,... | collective-permute-start | bytes 32 | tf_op jit(solution)/shard_map/ppermute | solution.py:32
  65.1 5.7 %collective-permute-start.9 = (f32[2]{0:T(128)S(1)}, f32[2]{0:T(128)S(1)}, u32[]{:S(2)}, u32[]{:S(2)}) collective-permute-start(f32[2]{0:T(128)S(1)} %add.25), channel_id=1, source_target_pairs={{0,4},{1,5},{2,6},{3,7},{4,0},{5,1},{6,2},{7,3},{8,12},{9,13},{10,... | collective-permute-start | bytes 32 | tf_op jit(solution)/shard_map/ppermute | solution.py:32
  72.7 6.4 %collective-permute-start.14 = (bf16[21,128,128]{2,1,0:T(8,128)(2,1)S(1)}, bf16[21,128,128]{2,1,0:T(8,128)(2,1)S(1)}, u32[]{:S(2)}, u32[]{:S(2)}) collective-permute-start(bf16[21,128,128]{2,1,0:T(8,128)(2,1)S(1)} %get-tuple-element.48), channel_id=1, source_target_pairs={{0,1},{1,0},{2,3},{3,2},{4,5},{5,4},{6,7},{7,6},{8,9},{9,8},{10,11... | collective-permute-start | bytes 2064392 | tf_op jit(solution)/shard_map/ppermute | solution.py:32
  73.3 5.3 %collective-permute-start.15 = (f32[2]{0:T(128)S(1)}, f32[2]{0:T(128)S(1)}, u32[]{:S(2)}, u32[]{:S(2)}) collective-permute-start(f32[2]{0:T(128)S(1)} %add.26), channel_id=1, source_target_pairs={{0,8},{1,9},{2,10},{3,11},{4,12},{5,13},{6,14},{7,15},{8,0},{9,1},... | collective-permute-start | bytes 32 | tf_op jit(solution)/shard_map/ppermute | solution.py:32
